TPU v7x, 512 devices: a whole 4x8x8 slice. The times are simulated.
512 devices in a mesh: group: 2 (over core), dp: 32 (over y, x), mp: 8 (over z).
Axes of the slice: x: 4, y: 8, z: 8, core: 2. Of those that a mesh axis runs over, the one named last changes fastest.
Arguments:
- teacher_hidden: bfloat16 [65536, 4096], P(('group', 'dp'), 'mp'), may hold values from -60 to 60
- teacher_gain: float32 [4096], replicated, may hold values from 0.5 to 1.5
- projector: bfloat16 [4096, 3584], P('dp', 'mp'), may hold values from -0.09375 to 0.09375
- live: int32 [65536], P(('group', 'dp')), may hold values from 0 to 1, as said below
- placement: int32 [65536], P(('group', 'dp')), may hold values from 0 to 31
- student_hidden: bfloat16 [65536, 3584], P(('group', 'dp', 'mp')), may hold values from -60 to 60
- student_gain: float32 [3584], P('mp'), may hold values from 0.5 to 1.5
Outputs:
- grad_hidden: bfloat16 [65536, 3584], P(('group', 'dp', 'mp'))
- grad_gain: float32 [3584], P('mp')
- mean_loss: float32 [], replicated
Inputs may be any that keep to these rules, and one draw needn't show every extreme that they name: For each g and m, in every block of 128 teacher rows starting at ((g * 32 + d) * 8 + m) * 128, at most 4 live rows name the same placement, and for each g and m one placement value is named by exactly 4 live rows of every block of that g and m.
All inputs are finite; a program needn't handle non-finite values.
Results may differ from a plain program's by a relative error of at most 0.0057.
Values may be sent and summed in bfloat16 or wider, within the bound.
No kernel may reach another device: no remote copies, remote signals or barrier semaphores. Data moves between devices by JAX's collectives and lax.ppermute only.
A program may use at most 64 MiB of HBM per device.

v0:
```python
import jax
import jax.numpy as jnp
from jax import lax
from jax.sharding import PartitionSpec as P

EPSILON = 1e-06


def pack_rows(block_rows, shard_ids, live_rows, dp_count, capacity):
    row_total = block_rows.shape[0]
    matches = (
        (shard_ids[:, None] == jnp.arange(dp_count, dtype=jnp.int32)[None, :])
        & (live_rows[:, None] == 1)
    ).astype(jnp.int32)
    earlier = jnp.cumsum(matches, axis=0) - matches
    picked = matches[:, :, None] * (
        earlier[:, :, None] == jnp.arange(capacity, dtype=jnp.int32)[None, None, :]
    ).astype(jnp.int32)
    sources = jnp.sum(picked * jnp.arange(row_total, dtype=jnp.int32)[:, None, None], axis=0)
    counts = jnp.sum(matches, axis=0)
    buffer = jnp.take(block_rows, sources.reshape(-1), axis=0).reshape(
        dp_count, capacity, block_rows.shape[1]
    )
    return (buffer, counts)


def place_rows(received, arrived, slot_count):
    dp_count, capacity, columns = received.shape
    offsets = jnp.cumsum(arrived) - arrived
    within = jnp.arange(capacity, dtype=jnp.int32)
    slots = (offsets[:, None] + within[None, :]).reshape(-1)
    usable = (within[None, :] < arrived[:, None]).reshape(-1)
    chooser = (
        (jnp.arange(slot_count, dtype=jnp.int32)[:, None] == slots[None, :]) & usable[None, :]
    ).astype(jnp.bfloat16)
    target = jnp.dot(
        chooser, received.reshape(dp_count * capacity, columns), preferred_element_type=jnp.float32
    ).astype(jnp.bfloat16)
    filled = (jnp.arange(slot_count, dtype=jnp.int32) < jnp.sum(arrived)).astype(jnp.float32)
    return (target, filled)


def local(teacher_hidden, teacher_gain, projector, live, placement, student_hidden, student_gain):
    dp_count = lax.axis_size("dp")
    mp_count = lax.axis_size("mp")
    column = lax.axis_index("mp")
    gathered = lax.all_gather(teacher_hidden, "mp", axis=1, tiled=True)
    values = gathered.astype(jnp.float32)
    inverse_rms = lax.rsqrt(jnp.mean(values * values, axis=-1, keepdims=True) + EPSILON)
    normed = (values * inverse_rms * teacher_gain).astype(jnp.bfloat16)
    out_columns = projector.shape[1]
    projected = jnp.dot(
        normed,
        lax.all_gather(projector, "dp", axis=0, tiled=True),
        preferred_element_type=jnp.float32,
    ).astype(jnp.bfloat16)
    slot_count = student_hidden.shape[0]
    capacity = slot_count // dp_count
    blocks = projected.reshape(mp_count, slot_count, out_columns)
    live_blocks = live.reshape(mp_count, slot_count)
    shard_blocks = placement.reshape(mp_count, slot_count)
    regrouped = lax.all_to_all(blocks, "mp", split_axis=0, concat_axis=2, tiled=True).reshape(
        slot_count, out_columns * mp_count
    )
    own_live = lax.dynamic_index_in_dim(live_blocks, column, 0, keepdims=False)
    own_shards = lax.dynamic_index_in_dim(shard_blocks, column, 0, keepdims=False)
    buffer, counts = pack_rows(regrouped, own_shards, own_live, dp_count, capacity)
    received, arrived = (
        lax.all_to_all(buffer, "dp", split_axis=0, concat_axis=0, tiled=True),
        lax.all_to_all(counts.astype(jnp.bfloat16), "dp", split_axis=0, concat_axis=0, tiled=True),
    )
    arrived = arrived.astype(jnp.int32)
    target, filled = place_rows(received, arrived, slot_count)
    gains = lax.all_gather(student_gain, "mp", axis=0, tiled=True)
    hidden_values = student_hidden.astype(jnp.float32)
    student_rms = lax.rsqrt(
        jnp.mean(hidden_values * hidden_values, axis=-1, keepdims=True) + EPSILON
    )
    normal = hidden_values * student_rms
    mismatch = (normal * gains - target.astype(jnp.float32)) * filled[:, None]
    weighted = mismatch * gains
    gradient = (
        student_rms * (weighted - normal * jnp.mean(weighted * normal, axis=-1, keepdims=True))
    ).astype(jnp.bfloat16)
    gain_terms = jnp.sum(mismatch * normal, axis=0)
    squares = jnp.sum(mismatch * mismatch)
    tally = jnp.sum(filled)
    share_width = student_gain.shape[0]
    totals, square_sum, tally_sum = lax.psum((gain_terms, squares, tally), ("group", "dp", "mp"))
    own_terms = lax.dynamic_slice_in_dim(totals, column * share_width, share_width)
    grad_gain = own_terms / tally_sum
    mean_loss = square_sum / (2.0 * tally_sum * gains.shape[0])
    return (gradient, grad_gain, mean_loss)


def solution(mesh):
    placed = (
        P(("group", "dp"), "mp"),
        P(),
        P("dp", "mp"),
        P(("group", "dp")),
        P(("group", "dp")),
        P(("group", "dp", "mp"), None),
        P("mp"),
    )
    return jax.shard_map(
        local,
        mesh=mesh,
        in_specs=placed,
        out_specs=(P(("group", "dp", "mp"), None), P("mp"), P()),
        check_vma=False,
    )
```

profile of v0, /device:TPU:1, one launch (start us, length us, event | category | flops | bytes accessed | tf_op | source)
XLA Modules:
  0.0 407.4 jit_solution(9121656083510307299)
XLA Ops:
  8.0 0.7 all-gather.5.cloned.1.call-update
  8.7 104.5 %all-gather.3.cloned.1.call-done = bf16[1024,4096]{1,0:T(8,128)(2,1)} async-done(((bf16[1024,512]{1,0:T(8,128)(2,1)}), bf16[1024,4096]{1,0:T(8,128)(2,1)}) %all-gather.3.cloned.1.call-update) | async-done | bytes 8388624 | tf_op jit(solution)/shard_map/all_gather | solution.py:47
  113.2 5.1 %fusion = f32[1024]{0:T(1024)S(1)} fusion(bf16[1024,4096]{1,0:T(8,128)(2,1)} %all-gather.3.cloned.1.call-done), kind=kLoop, calls=%fused_computation.3 | loop fusion | flops 12581888 | bytes 8392704 | tf_op jit(solution)/shard_map/reduce_sum | solution.py:49
  118.2 79.3 %all-gather.5.cloned.1.call-done = bf16[4096,448]{0,1:T(8,128)(2,1)} async-done(((bf16[128,448]{0,1:T(8,128)(2,1)}), bf16[4096,448]{0,1:T(8,128)(2,1)}) %all-gather.5.cloned.1.call-update) | async-done | bytes 3670032 | tf_op jit(solution)/shard_map/all_gather | solution.py:54
  197.5 8.5 %fusion.23 = bf16[56,8,8,128]{3,2,1,0:T(8,128)(2,1)S(1)} fusion(bf16[4096,448]{0,1:T(8,128)(2,1)} %all-gather.5.cloned.1.call-done, bf16[1024,4096]{1,0:T(8,128)(2,1)} %all-gather.3.cloned.1.call-done, f32[4096]{0:T(1024)S(1)} %copy-done.3, f32[1024]{0:T(1024)S(1)} %add_rsqrt_fusion), kind=kOutput, calls=%fused_computation.27 | convolution fusion | flops 3775332352 | bytes 12996608 | tf_op jit(solution)/shard_map/dot_general | solution.py:52
  206.0 1.1 copy.33
  207.1 7.1 %all-to-all-start.1 = ((bf16[8,128,448]{1,2,0:T(8,128)(2,1)}), bf16[8,128,448]{1,2,0:T(8,128)(2,1)S(1)}, u32[]{:S(2)}, u32[]{:S(2)}) async-start(bf16[8,128,448]{1,2,0:T(8,128)(2,1)} %bitcast.23), calls=%async_computation.1 | async-start | bytes 1835008 | tf_op jit(solution)/shard_map/all_to_all | solution.py:62
  214.2 0.7 compare_bitcast_fusion
  215.4 0.7 copy.23
  216.7 20.4 %all-to-all-done.1 = bf16[8,128,448]{1,2,0:T(8,128)(2,1)S(1)} async-done(((bf16[8,128,448]{1,2,0:T(8,128)(2,1)}), bf16[8,128,448]{1,2,0:T(8,128)(2,1)S(1)}, u32[]{:S(2)}, u32[]{:S(2)}) %all-to-all-start.1) | async-done | bytes 917536 | tf_op jit(solution)/shard_map/all_to_all | solution.py:62
  237.1 6.5 %all-to-all-start = ((bf16[32,1,1]{2,1,0:T(2,128)(2,1)}), bf16[32,1,1]{2,1,0:T(2,128)(2,1)S(1)}, u32[]{:S(2)}, u32[]{:S(2)}) async-start(bf16[32,1,1]{2,1,0:T(2,128)(2,1)} %copy.23), calls=%async_computation | async-start | bytes 32768 | tf_op jit(solution)/shard_map/all_to_all | solution.py:70
  244.1 1.1 gather_fusion
  245.5 1.4 broadcast_select_fusion
  246.9 5.3 %all-to-all-done = bf16[32,1,1]{2,1,0:T(2,128)(2,1)S(1)} async-done(((bf16[32,1,1]{2,1,0:T(2,128)(2,1)}), bf16[32,1,1]{2,1,0:T(2,128)(2,1)S(1)}, u32[]{:S(2)}, u32[]{:S(2)}) %all-to-all-start) | async-done | bytes 96 | tf_op jit(solution)/shard_map/all_to_all | solution.py:70
  252.2 3.9 all-to-all-start.2
  256.1 1.3 dynamic-slice
  258.4 21.5 %all-reduce = f32[3584]{0:T(1024)S(1)} all-reduce(f32[3584]{0:T(1024)S(1)} %dynamic-update-slice), channel_id=1, replica_groups=mesh['group'=2,'dp'=32,'mp'=8] {'mp'}, use_global_device_ids=true, to_apply=%add | all-reduce | flops 3584 | bytes 28672
  280.2 1.2 convert_reduce_fusion.1
  281.4 1.2 fusion.35
  283.9 1.1 reshape.301
  285.0 2.8 fusion.18
  287.8 107.6 %all-reduce.1 = (f32[3584]{0:T(1024)S(1)}, f32[]{:T(128)}, f32[]{:T(128)}) all-reduce(f32[3584]{0:T(1024)S(1)} %get-tuple-element.3, f32[]{:T(128)} %fusion.35, f32[]{:T(128)} %get-tuple-element.5), channel_id=1, replica_groups=mesh['group'=2,'dp'=32,'mp'=8] {'group','dp','mp'}, use_global_device_ids=true, to_apply=%region_9.10 | all-reduce | flops 3586 | bytes 28688 | tf_op jit(solution)/shard_map/psum | solution.py:89
  396.8 1.3 dynamic-slice_divide_fusion
  398.1 1.4 fusion.17
  (43 shorter events, 4.3 us)
Async XLA Ops:
  7.2 207.8 %copy-start = (s32[1024]{0:T(1024)S(1)}, s32[1024]{0:T(1024)}, u32[]{:S(2)}) copy-start(s32[1024]{0:T(1024)} %param.11) | copy-start | bytes 12292
  7.2 106.0 %all-gather.3.cloned.1.call-start = ((), (), s32[]{:S(2)}) async-start(), calls=%async_computation.3 | async-start | bytes 9437184 | tf_op jit(solution)/shard_map/all_gather | solution.py:47
  7.9 189.6 %all-gather.5.cloned.1.call-start = ((), (), s32[]{:S(2)}) async-start(), calls=%async_computation.4 | async-start | bytes 3784704 | tf_op jit(solution)/shard_map/all_gather | solution.py:54
  8.7 188.9 %copy-start.3 = (f32[4096]{0:T(1024)S(1)}, f32[4096]{0:T(1024)}, u32[]{:S(2)}) copy-start(f32[4096]{0:T(1024)} %param.8) | copy-start | bytes 49156
  207.1 30.0 %all-to-all-start.1 = ((bf16[8,128,448]{1,2,0:T(8,128)(2,1)}), bf16[8,128,448]{1,2,0:T(8,128)(2,1)S(1)}, u32[]{:S(2)}, u32[]{:S(2)}) async-start(bf16[8,128,448]{1,2,0:T(8,128)(2,1)} %bitcast.23), calls=%async_computation.1 | async-start | bytes 1835008 | tf_op jit(solution)/shard_map/all_to_all | solution.py:62
  237.1 15.1 %all-to-all-start = ((bf16[32,1,1]{2,1,0:T(2,128)(2,1)}), bf16[32,1,1]{2,1,0:T(2,128)(2,1)S(1)}, u32[]{:S(2)}, u32[]{:S(2)}) async-start(bf16[32,1,1]{2,1,0:T(2,128)(2,1)} %copy.23), calls=%async_computation | async-start | bytes 32768 | tf_op jit(solution)/shard_map/all_to_all | solution.py:70
  245.4 12.6 %copy-start.2 = (f32[448]{0:T(512)S(1)}, f32[448]{0:T(512)}, u32[]{:S(2)}) copy-start(f32[448]{0:T(512)} %param.13) | copy-start | bytes 5380
  245.5 34.4 %copy-start.1 = (bf16[128,3584]{1,0:T(8,128)(2,1)S(1)}, bf16[128,3584]{1,0:T(8,128)(2,1)}, u32[]{:S(2)}) copy-start(bf16[128,3584]{1,0:T(8,128)(2,1)} %param.12) | copy-start | bytes 2752516
  252.2 31.7 %all-to-all-start.2 = ((bf16[32,4,3584]{2,1,0:T(4,128)(2,1)}), bf16[32,4,3584]{2,1,0:T(4,128)(2,1)S(1)}, u32[]{:S(2)}, u32[]{:S(2)}) async-start(bf16[32,4,3584]{2,1,0:T(4,128)(2,1)} %broadcast_select_fusion), calls=%async_computation.2 | async-start | bytes 1835008 | tf_op jit(solution)/shard_map/all_to_all | solution.py:69
Sparse Core Ops, SparseCore 0:
  10.1 103.0 all-gather.2
  116.2 81.2 all-gather.4
where the time goes:
time: 408 us; the launch traced here: 407 us
  waiting for transfers between devices  211 us (52%)
  blocking collectives  129 us (32%)
  starting transfers between devices  17.6 us (4%)
  between operations  17.3 us (4%)
  other arithmetic  14.2 us (3%)
  matrix products  11.3 us (3%)
  local copies, waits for them, and re-layouts  7 us (2%)
    psum x1, blocking collectives, local(): lax.psum((gain_terms, squares, tally), ('group', 'dp', 'mp'))  108 us
    all_gather x1, waiting for transfers between devices, local(): gathered = lax.all_gather(teacher_hidden, 'mp', axis=1, tiled=True)  104 us
    all_gather x1, waiting for transfers between devices, local(): lax.all_gather(projector, 'dp', axis=0, tiled=True)  79.3 us
    unnamed x1, blocking collectives  21.5 us
    all_to_all x1, waiting for transfers between devices, local(): lax.all_to_all(blocks, 'mp', split_axis=0, concat_axis=2, tiled=True)  20.4 us
    dot_general x1, matrix products, local(): jnp.dot(normed, lax.all_gather(projector, 'dp', axis=0, tiled=True), pref...  8.49 us
  transfers between devices with their start and end apart: 5, of which 4 were waited for; matrix products, arithmetic and copies ran while one was open for 4% of the time, Pallas kernels for 0%

commit v1 on v0

v1 whole, which is shorter than its diff:
```python
import functools

import jax
import jax.numpy as jnp
from jax import lax
from jax.experimental import pallas as pl
from jax.experimental.pallas import tpu as pltpu
from jax.sharding import PartitionSpec as P

EPSILON = 1e-06
RING = 4
MIB = 1024 * 1024
EMPTY = 1e30
EMPTY_FROM = 1e20


def norm_kernel(moved_ref, slot_ref, gain_ref, top_ref, low_ref, packed):
    parts, rows, features = moved_ref.shape
    order = lax.broadcasted_iota(jnp.int32, (rows, rows), 0)
    packer = (order == slot_ref[...]).astype(jnp.bfloat16)
    total = jnp.zeros((rows, 1), jnp.float32)
    for part in range(parts):
        values = jnp.dot(packer, moved_ref[part], preferred_element_type=jnp.float32)
        packed[part] = values
        total += jnp.sum(values * values, axis=1, keepdims=True)
    inverse_rms = lax.rsqrt(total * (1.0 / (parts * features)) + EPSILON)
    half = rows // 2
    taken = jnp.sum(packer.astype(jnp.float32), axis=1, keepdims=True)
    first_column = lax.broadcasted_iota(jnp.int32, (rows, features), 1) == 0
    for part in range(parts):
        columns = slice(part * features, (part + 1) * features)
        normed = packed[part] * inverse_rms * gain_ref[:, columns]
        if part == 0:
            normed = jnp.where(first_column & (taken == 0.0), EMPTY, normed)
        normed = normed.astype(jnp.bfloat16)
        top_ref[:, columns] = normed[:half]
        low_ref[:, columns] = normed[half:]


def norm_rows(moved, slot, teacher_gain):
    parts, rows, features = moved.shape
    half = jax.ShapeDtypeStruct((rows // 2, parts * features), jnp.bfloat16)
    return pl.pallas_call(
        norm_kernel,
        out_shape=(half, half),
        scratch_shapes=[pltpu.VMEM((parts, rows, features), jnp.float32)],
        compiler_params=pltpu.CompilerParams(vmem_limit_bytes=16 * MIB),
        cost_estimate=pl.CostEstimate(
            flops=2 * rows * rows * parts * features,
            bytes_accessed=4 * rows * parts * features,
            transcendentals=rows,
        ),
    )(moved, slot[None, :], teacher_gain[None, :])


def product_kernel(shards, count, place_ref, *refs):
    sources, weight_sources = refs[:count], refs[count : count + 2]
    out_ref, rows_buffer, weights, sums, row_sems, weight_sems = refs[count + 2 :]
    y_count, shares = weights.shape[1:3]
    steps = weight_sems.shape[1]
    spans = y_count // steps
    part = rows_buffer.shape[1] // steps
    height = sources[0].shape[0]
    row_copies = [
        pltpu.make_async_copy(source, rows_buffer.at[pl.ds(i * height, height)], row_sems.at[i])
        for i, source in enumerate(sources)
    ]
    weight_copies = [
        [
            pltpu.make_async_copy(
                source.at[pl.ds(step * spans, spans)],
                weights.at[side, pl.ds(step * spans, spans)],
                weight_sems.at[side, step],
            )
            for step in range(steps)
        ]
        for side, source in enumerate(weight_sources)
    ]
    for copy in row_copies:
        copy.start()
    for step in range(steps):
        for side in range(2):
            weight_copies[side][step].start()
    for copy in row_copies:
        copy.wait()

    core = place_ref[0]
    for step in range(steps):
        rows = rows_buffer[:, step * part : (step + 1) * part]
        for side in range(2):
            weight_copies[side][step].wait()
            tiles = []
            for span in range(step * spans, (step + 1) * spans):
                for pair in range(shares // 2):
                    halves = weights[side, span, 2 * pair : 2 * pair + 2]
                    tiles.append(halves.reshape(-1, halves.shape[-1]))
            partial = lax.dot_general(
                rows,
                jnp.concatenate(tiles, axis=1),
                (((1,), (1,)), ((), ())),
                preferred_element_type=jnp.float32,
            )
            if step == 0:
                sums[side] = partial
            else:
                sums[side] += partial

    total_rows, width = sums.shape[1:]
    depth = total_rows // shards
    to = lax.broadcasted_iota(jnp.int32, (total_rows, total_rows), 0)
    source = lax.broadcasted_iota(jnp.int32, (total_rows, total_rows), 1)
    turn = (source == (to % depth) * shards + to // depth).astype(jnp.bfloat16)
    empty = rows_buffer[:, :128].astype(jnp.float32)[:, 0:1] > EMPTY_FROM

    def turned(side):
        kept = jnp.where(empty, EMPTY, sums[side]).astype(jnp.bfloat16)
        return jnp.dot(turn, kept, preferred_element_type=jnp.float32).astype(jnp.bfloat16)

    mine = turned(0)
    other = turned(1)

    @pl.when(core == 0)
    def _():
        out_ref[:, :width] = mine
        out_ref[:, width:] = other

    @pl.when(core != 0)
    def _():
        out_ref[:, :width] = other
        out_ref[:, width:] = mine


def product(place, pieces, mine, other, shards):
    y_count, shares, half, tile = mine.shape
    width = 2 * half
    depth = y_count * (shares // 2) * tile
    count = len(pieces)
    total_rows = pieces[0].shape[0] * count
    steps = 4
    return pl.pallas_call(
        functools.partial(product_kernel, shards, count),
        out_shape=jax.ShapeDtypeStruct((total_rows, 2 * width), jnp.bfloat16),
        in_specs=[pl.BlockSpec(memory_space=pltpu.SMEM)]
        + [pl.BlockSpec(memory_space=pl.ANY)] * (count + 2),
        out_specs=pl.BlockSpec(memory_space=pltpu.VMEM),
        scratch_shapes=[
            pltpu.VMEM((total_rows, depth), jnp.bfloat16),
            pltpu.VMEM((2,) + mine.shape, jnp.bfloat16),
            pltpu.VMEM((2, total_rows, width), jnp.float32),
            pltpu.SemaphoreType.DMA((count,)),
            pltpu.SemaphoreType.DMA((2, steps)),
        ],
        compiler_params=pltpu.CompilerParams(vmem_limit_bytes=32 * MIB),
        cost_estimate=pl.CostEstimate(
            flops=4 * total_rows * depth * width,
            bytes_accessed=2 * depth * (total_rows + 2 * width),
            transcendentals=0,
        ),
    )(place, *pieces, mine, other)


def finish_kernel(
    mp_count, received_ref, hidden_ref, gain_ref, gradient_ref, message_ref, weighted_sum, gain_sum
):
    y_count, x_count, deep, quarter = received_ref.shape
    rows, width = hidden_ref.shape
    capacity = deep // x_count
    spans = [slice(x * quarter, (x + 1) * quarter) for x in range(x_count)]
    total = jnp.zeros((rows, 1), jnp.float32)
    for span in spans:
        values = hidden_ref[:, span].astype(jnp.float32)
        total += jnp.sum(values * values, axis=1, keepdims=True)
    inverse_rms = lax.rsqrt(total * (1.0 / width) + EPSILON)
    to = lax.broadcasted_iota(jnp.int32, (rows, rows), 0)
    source = lax.broadcasted_iota(jnp.int32, (rows, rows), 1)

    def rank_of(row, x):
        y, j, rank = row // deep, (row // capacity) % x_count, row % capacity
        return (y * x_count + (x - j + x_count) % x_count) * capacity + rank

    row_terms = jnp.zeros((rows, 1), jnp.float32)
    squares = jnp.zeros((rows, 1), jnp.float32)
    tally = None
    for x, span in enumerate(spans):
        block = received_ref[:, x].reshape(y_count * deep, quarter)
        live = jnp.where(block[:, 0:1].astype(jnp.float32) < EMPTY_FROM, 1.0, 0.0)
        live = jnp.broadcast_to(live, (rows, rows))
        if tally is None:
            tally = jnp.sum(live, axis=0, keepdims=True)[:, 0:1]
            filled = (
                lax.broadcasted_iota(jnp.int32, (rows, 1), 0).astype(jnp.float32) < tally
            ).astype(jnp.float32)
        before = (rank_of(source, x) < rank_of(to, x)).astype(jnp.bfloat16)
        slot = jnp.dot(before, live.astype(jnp.bfloat16), preferred_element_type=jnp.float32)
        chooser = jnp.where(slot == source.astype(jnp.float32), live, 0.0).astype(jnp.bfloat16)
        target = lax.dot_general(
            chooser, block, (((0,), (0,)), ((), ())), preferred_element_type=jnp.float32
        )
        gain = gain_ref[:, span]
        normal = hidden_ref[:, span].astype(jnp.float32) * inverse_rms
        mismatch = (normal * gain - target) * filled
        weighted = mismatch * gain
        weighted_sum[:, span] = weighted
        row_terms += jnp.sum(weighted * normal, axis=1, keepdims=True)
        squares += jnp.sum(mismatch * mismatch, axis=1, keepdims=True)
        gain_sum[:, span] = jnp.sum(mismatch * normal, axis=0, keepdims=True)
    row_mean = row_terms * (1.0 / width)
    for span in spans:
        normal = hidden_ref[:, span].astype(jnp.float32) * inverse_rms
        gradient_ref[:, span] = (
            inverse_rms * (weighted_sum[:, span] - normal * row_mean)
        ).astype(jnp.bfloat16)
    share = width // mp_count
    square_sum = jnp.sum(squares, axis=0, keepdims=True)
    lane = lax.broadcasted_iota(jnp.int32, (1, message_ref.shape[2] - share), 1)
    tail = jnp.where(lane == 0, square_sum, jnp.where(lane == 1, tally, 0.0))
    for m in range(mp_count):
        message_ref[m, :, :share] = gain_sum[:, m * share : (m + 1) * share]
        message_ref[m, :, share:] = tail


def finish(received, hidden, gains, mp_count):
    rows, width = hidden.shape
    share = width // mp_count
    in_vmem = pl.BlockSpec(memory_space=pltpu.VMEM)
    return pl.pallas_call(
        functools.partial(finish_kernel, mp_count),
        out_shape=(
            jax.ShapeDtypeStruct((rows, width), jnp.bfloat16),
            jax.ShapeDtypeStruct((mp_count, 1, share + 64), jnp.float32),
        ),
        in_specs=[in_vmem] * 3,
        out_specs=(in_vmem, in_vmem),
        scratch_shapes=[
            pltpu.VMEM((rows, width), jnp.float32),
            pltpu.VMEM((1, width), jnp.float32),
        ],
        compiler_params=pltpu.CompilerParams(vmem_limit_bytes=16 * MIB),
        cost_estimate=pl.CostEstimate(
            flops=2 * rows * rows * width, bytes_accessed=6 * rows * width, transcendentals=rows
        ),
    )(received, hidden, gains[None, :])


def ring_gather(top, low, x_count, dp_count):
    forward = [(d, d - d % x_count + (d + 1) % x_count) for d in range(dp_count)]
    backward = [(d, d - d % x_count + (d - 1) % x_count) for d in range(dp_count)]
    left_top = lax.ppermute(top, "dp", forward)
    right_low = lax.ppermute(low, "dp", backward)
    left_low = lax.ppermute(low, "dp", forward)
    right_top = lax.ppermute(top, "dp", backward)
    far_top = lax.ppermute(left_top, "dp", forward)
    far_low = lax.ppermute(right_low, "dp", backward)
    return [top, low, left_top, left_low, far_top, far_low, right_top, right_low]


def projector_columns(projector, student_gain, mp_count, x_count, y_count):
    core = lax.axis_index("group")
    dp_count = x_count * y_count
    columns = projector.T
    half, tile = columns.shape[0] // 2, columns.shape[1]
    share = lax.dynamic_slice_in_dim(columns, core * half, half, 0)
    moves = []
    for c in range(2):
        for d in range(dp_count):
            for z in range(mp_count):
                source = (c * dp_count + d) * mp_count + z
                y, x = divmod(d, x_count)
                to_d = y * x_count + z // 2
                moves.append((source, ((z % 2) * dp_count + to_d) * mp_count + 2 * x + c))
    piece = lax.ppermute(share, ("group", "dp", "mp"), moves)
    high = lax.reduce_precision(student_gain, 8, 7)
    middle = lax.reduce_precision(student_gain - high, 8, 7)
    low = student_gain - high - middle
    width = student_gain.shape[0]
    extra = 16
    parts = jnp.concatenate(
        [high, middle, low, jnp.zeros((extra * tile - 3 * width,), jnp.float32)]
    ).astype(jnp.bfloat16)
    message = jnp.concatenate([piece, parts.reshape(extra, tile)], axis=0)
    spread = lax.all_to_all(
        jnp.broadcast_to(message[None], (mp_count,) + message.shape), "mp", 0, 0, tiled=True
    )
    parts = spread[:, half:].reshape(mp_count, extra * tile).astype(jnp.float32)
    gains = parts[:, :width] + parts[:, width : 2 * width] + parts[:, 2 * width : 3 * width]
    tiles = spread[:, :half].reshape(mp_count * half, tile)
    y_groups = [[y * x_count + x for y in range(y_count)] for x in range(x_count)]
    mine = lax.all_gather(tiles, "dp", axis=0, axis_index_groups=y_groups, tiled=True)
    return mine.reshape(y_count, mp_count, half, tile), gains.reshape(mp_count * width)


def local(teacher_hidden, teacher_gain, projector, live, placement, student_hidden, student_gain):
    dp_count = lax.axis_size("dp")
    mp_count = lax.axis_size("mp")
    group_count = lax.axis_size("group")
    x_count = RING
    y_count = dp_count // x_count
    column = lax.axis_index("mp")
    core = lax.axis_index("group")
    slot_count = student_hidden.shape[0]
    capacity = slot_count // dp_count
    share_width = student_gain.shape[0]
    width = share_width * mp_count

    features = teacher_hidden.shape[1]
    blocks = teacher_hidden.reshape(mp_count, slot_count, features)
    moved = lax.all_to_all(blocks, "mp", 0, 0, tiled=True)
    mine, gains = projector_columns(projector, student_gain, mp_count, x_count, y_count)

    own_live = lax.dynamic_index_in_dim(live.reshape(mp_count, slot_count), column, 0, keepdims=False)
    own_shards = lax.dynamic_index_in_dim(placement.reshape(mp_count, slot_count), column, 0, keepdims=False)
    order = jnp.arange(slot_count, dtype=jnp.int32)
    same = (
        (own_shards[:, None] == own_shards[None, :])
        & (own_live[:, None] == 1)
        & (order[:, None] < order[None, :])
    )
    rank = jnp.sum(same.astype(jnp.int32), axis=0)
    slot = jnp.where(own_live == 1, rank * dp_count + own_shards, -1)

    top, low = norm_rows(moved, slot, teacher_gain)
    pieces = ring_gather(top, low, x_count, dp_count)
    mine, pieces[2], pieces[3], pieces[6], pieces[7] = lax.optimization_barrier(
        (mine, pieces[2], pieces[3], pieces[6], pieces[7])
    )
    other = lax.ppermute(mine, "group", [(0, 1), (1, 0)])

    buffer = product(core.astype(jnp.int32).reshape(1), pieces, mine, other, dp_count)
    quarter = buffer.shape[1]
    deep = x_count * capacity
    received = lax.all_to_all(
        buffer.reshape(dp_count, deep, quarter), "dp", 0, 0, tiled=True
    ).reshape(y_count, x_count, deep, quarter)
    gradient, message = finish(received, student_hidden, gains, mp_count)

    over_mp = jnp.sum(lax.all_to_all(message, "mp", 0, 0, tiled=True), axis=(0, 1))
    peers = group_count * dp_count
    totals = jnp.sum(
        lax.all_to_all(
            jnp.broadcast_to(over_mp[None, :], (peers, over_mp.shape[0])), ("group", "dp"), 0, 0, tiled=True
        ),
        axis=0,
    )
    square_sum = totals[share_width]
    tally_sum = totals[share_width + 1]
    grad_gain = totals[:share_width] / tally_sum
    mean_loss = square_sum / (2.0 * tally_sum * width)
    return (gradient, grad_gain, mean_loss)


def solution(mesh):
    placed = (
        P(("group", "dp"), "mp"),
        P(),
        P("dp", "mp"),
        P(("group", "dp")),
        P(("group", "dp")),
        P(("group", "dp", "mp"), None),
        P("mp"),
    )
    return jax.shard_map(
        local,
        mesh=mesh,
        in_specs=placed,
        out_specs=(P(("group", "dp", "mp"), None), P("mp"), P()),
        check_vma=False,
    )
```

time: 408 us -> 220 us (0.54)
  waiting for transfers between devices: 211 us -> 72.8 us
  blocking collectives: 129 us -> 58.2 us
  starting transfers between devices: 17.6 us -> 42.9 us
  Pallas kernels: 0 us -> 14.2 us
  matrix products: 11.3 us -> 0 us
  other arithmetic: 14.2 us -> 4.49 us
    all_gather x2 -> x1, waiting for transfers between devices: 184 us -> 0.01 us  [projector_columns(): lax.all_gather(tiles, 'dp', axis=0, axis_index_groups=y_groups, tiled=True)]
    psum x1 -> x0, blocking collectives: 108 us -> none  [local(): lax.psum((gain_terms, squares, tally), ('group', 'dp', 'mp'))]
    all_to_all x0 -> x3, blocking collectives: none -> 58.2 us  [the longest x1 28.9 us: projector_columns(): lax.all_to_all(jnp.broadcast_to(message[None], (mp_count,) + message.shap...]
    ppermute x0 -> x8, starting transfers between devices: none -> 28.9 us  [the longest x1 6.46 us: local(): other = lax.ppermute(mine, 'group', [(0, 1), (1, 0)])]
    ppermute x0 -> x8, waiting for transfers between devices: none -> 26.7 us  [the longest x1 9.34 us: ring_gather(): far_top = lax.ppermute(left_top, 'dp', forward)]
    unnamed x1 -> x0, blocking collectives: 21.5 us -> none
    all_to_all x3 -> x2, waiting for transfers between devices: 25.7 us -> 46 us  [the longest x1 23.8 us: local(): moved = lax.all_to_all(blocks, 'mp', 0, 0, tiled=True)]
    pallas_call x0 -> x3, Pallas kernels: none -> 14.2 us  [the longest x1 10.2 us: product(): pl.pallas_call(functools.partial(product_kernel, shards, count), out_shap...]
  transfers between devices with their start and end apart: 5 -> 11, of which waited for: 4 -> 9; matrix products, arithmetic and copies ran while one was open for 4% -> 2% of each run, Pallas kernels for 0% -> 0%
where the time goes in v1:
time: 220 us; the launch traced here: 219 us
  waiting for transfers between devices  72.8 us (33%)
  blocking collectives  58.2 us (26%)
  starting transfers between devices  42.9 us (20%)
  between operations  16.7 us (8%)
  Pallas kernels  14.2 us (6%)
  local copies, waits for them, and re-layouts  9.84 us (4%)
  other arithmetic  4.49 us (2%)
    all_to_all x1, blocking collectives, projector_columns(): lax.all_to_all(jnp.broadcast_to(message[None], (mp_count,) + message.shap...  28.9 us
    all_to_all x1, waiting for transfers between devices, local(): moved = lax.all_to_all(blocks, 'mp', 0, 0, tiled=True)  23.8 us
    all_to_all x1, waiting for transfers between devices, local(): lax.all_to_all(buffer.reshape(dp_count, deep, quarter), 'dp', 0, 0, tiled...  22.3 us
    all_to_all x1, blocking collectives, local(): lax.all_to_all(jnp.broadcast_to(over_mp[None, :], (peers, over_mp.shape[0...  20.3 us
    all_to_all x1, starting transfers between devices, local(): lax.all_to_all(buffer.reshape(dp_count, deep, quarter), 'dp', 0, 0, tiled...  10.4 us
    pallas_call x1, Pallas kernels, product(): pl.pallas_call(functools.partial(product_kernel, shards, count), out_shap...  10.2 us
    ppermute x1, waiting for transfers between devices, ring_gather(): far_top = lax.ppermute(left_top, 'dp', forward)  9.34 us
    all_to_all x1, blocking collectives, local(): lax.all_to_all(message, 'mp', 0, 0, tiled=True)  8.97 us
  transfers between devices with their start and end apart: 11, of which 9 were waited for; matrix products, arithmetic and copies ran while one was open for 2% of the time, Pallas kernels for 0%

profile of v1, /device:TPU:1, one launch (start us, length us, event | category | flops | bytes accessed | tf_op | source)
XLA Modules:
  0.0 218.9 jit_solution(4571855937075695008)
XLA Ops:
  8.1 5.4 %collective-permute-start = (bf16[224,128]{1,0:T(8,128)(2,1)S(1)}, bf16[224,128]{1,0:T(8,128)(2,1)S(1)}, u32[]{:S(2)}, u32[]{:S(2)}) collective-permute-start(bf16[224,128]{1,0:T(8,128)(2,1)S(1)} %dynamic-slice_bitcast_fusion), channel_id=1, source_target_pairs={{0,0},{1,256},{2,8},{3,264},{4,16},{5,272},{6,24},{7,280},{8,2},{9... | collective-permute-start | bytes 172040 | tf_op jit(solution)/shard_map/ppermute | solution.py:271
  15.4 28.9 %all_to_all.26 = bf16[8,240,128]{2,1,0:T(8,128)(2,1)S(1)} all-to-all(bf16[8,240,128]{2,1,0:T(8,128)(2,1)S(1)} %broadcast_in_dim.15), channel_id=1, replica_groups=mesh['group'=2,'dp'=32,'mp'=8] {'mp'}, dimensions={0} | all-to-all | bytes 983040 | tf_op jit(solution)/shard_map/all_to_all | solution.py:281
  45.9 3.6 %all-to-all-start = ((bf16[8,128,512]{2,1,0:T(8,128)(2,1)}), bf16[8,128,512]{2,1,0:T(8,128)(2,1)S(1)}, u32[]{:S(2)}, u32[]{:S(2)}) async-start(bf16[8,128,512]{2,1,0:T(8,128)(2,1)} %bitcast.32), calls=%async_computation | async-start | bytes 2097152 | tf_op jit(solution)/shard_map/all_to_all | solution.py:307
  51.8 23.8 %all-to-all-done.moved_ref = bf16[8,128,512]{2,1,0:T(8,128)(2,1)S(1)} async-done(((bf16[8,128,512]{2,1,0:T(8,128)(2,1)}), bf16[8,128,512]{2,1,0:T(8,128)(2,1)S(1)}, u32[]{:S(2)}, u32[]{:S(2)}) %all-to-all-start) | async-done | bytes 1048608 | tf_op jit(solution)/shard_map/all_to_all | solution.py:307
  76.2 1.9 collective-permute-start.3
  78.1 3.4 %collective-permute-start.1 = (bf16[64,4096]{1,0:T(8,128)(2,1)S(1)}, bf16[64,4096]{1,0:T(8,128)(2,1)S(1)}, u32[]{:S(2)}, u32[]{:S(2)}) collective-permute-start(bf16[64,4096]{1,0:T(8,128)(2,1)S(1)} %get-tuple-element.12.refs_0_), channel_id=1, source_target_pairs={{0,8},{8,16},{16,24},{24,0},{32,40},{40,48},{48,56},{56,32},{64,72... | collective-permute-start | bytes 1572872 | tf_op jit(solution)/shard_map/ppermute | solution.py:248
  81.5 3.1 %collective-permute-start.4 = (bf16[64,4096]{1,0:T(8,128)(2,1)S(1)}, bf16[64,4096]{1,0:T(8,128)(2,1)S(1)}, u32[]{:S(2)}, u32[]{:S(2)}) collective-permute-start(bf16[64,4096]{1,0:T(8,128)(2,1)S(1)} %get-tuple-element.13.refs_1_), channel_id=1, source_target_pairs={{0,24},{8,0},{16,8},{24,16},{32,56},{40,32},{48,40},{56,48},{64,88... | collective-permute-start | bytes 1572872 | tf_op jit(solution)/shard_map/ppermute | solution.py:249
  84.6 2.2 collective-permute-start.2
  86.8 1.2 collective-permute-done.3.refs_6_
  88.0 3.1 %collective-permute-done.1.refs_2_ = bf16[64,4096]{1,0:T(8,128)(2,1)S(1)} collective-permute-done((bf16[64,4096]{1,0:T(8,128)(2,1)S(1)}, bf16[64,4096]{1,0:T(8,128)(2,1)S(1)}, u32[]{:S(2)}, u32[]{:S(2)}) %collective-permute-start.1) | collective-permute-done | bytes 524320 | tf_op jit(solution)/shard_map/ppermute | solution.py:248
  91.1 8.0 %collective-permute-done.4.refs_7_ = bf16[64,4096]{1,0:T(8,128)(2,1)S(1)} collective-permute-done((bf16[64,4096]{1,0:T(8,128)(2,1)S(1)}, bf16[64,4096]{1,0:T(8,128)(2,1)S(1)}, u32[]{:S(2)}, u32[]{:S(2)}) %collective-permute-start.4) | collective-permute-done | bytes 524320 | tf_op jit(solution)/shard_map/ppermute | solution.py:249
  99.1 3.1 %collective-permute-done.2.refs_3_ = bf16[64,4096]{1,0:T(8,128)(2,1)S(1)} collective-permute-done((bf16[64,4096]{1,0:T(8,128)(2,1)S(1)}, bf16[64,4096]{1,0:T(8,128)(2,1)S(1)}, u32[]{:S(2)}, u32[]{:S(2)}) %collective-permute-start.2) | collective-permute-done | bytes 524320 | tf_op jit(solution)/shard_map/ppermute | solution.py:250
  103.0 6.5 %collective-permute-start.7 = (bf16[8,8,224,128]{3,2,1,0:T(8,128)(2,1)}, bf16[8,8,224,128]{3,2,1,0:T(8,128)(2,1)S(1)}, u32[]{:S(2)}, u32[]{:S(2)}) collective-permute-start(bf16[8,8,224,128]{3,2,1,0:T(8,128)(2,1)} %bitcast.29), channel_id=1, source_target_pairs={{0,256},{256,0},{1,257},{257,1},{2,258},{258,2},{3,259},{259,3},{4... | collective-permute-start | bytes 11010056 | tf_op jit(solution)/shard_map/ppermute | solution.py:326
  109.5 2.2 collective-permute-start.5
  111.7 4.3 %collective-permute-start.6 = (bf16[64,4096]{1,0:T(8,128)(2,1)S(1)}, bf16[64,4096]{1,0:T(8,128)(2,1)S(1)}, u32[]{:S(2)}, u32[]{:S(2)}) collective-permute-start(bf16[64,4096]{1,0:T(8,128)(2,1)S(1)} %collective-permute-done.4.refs_7_), channel_id=1, source_target_pairs={{0,24},{8,0},{16,8},{24,16},{32,56},{40,32},{48,40},{56,48},{64,88... | collective-permute-start | bytes 1572872 | tf_op jit(solution)/shard_map/ppermute | solution.py:253
  116.8 9.3 %collective-permute-done.5.refs_4_ = bf16[64,4096]{1,0:T(8,128)(2,1)S(1)} collective-permute-done((bf16[64,4096]{1,0:T(8,128)(2,1)S(1)}, bf16[64,4096]{1,0:T(8,128)(2,1)S(1)}, u32[]{:S(2)}, u32[]{:S(2)}) %collective-permute-start.5) | collective-permute-done | bytes 524320 | tf_op jit(solution)/shard_map/ppermute | solution.py:252
  127.0 2.0 copy-done.3
  131.2 10.2 %shard_map.95 = bf16[512,896]{1,0:T(8,128)(2,1)} custom-call(s32[1]{0:T(128)} %bitcast.place_ref, bf16[64,4096]{1,0:T(8,128)(2,1)S(1)} %get-tuple-element.12.refs_0_, bf16[64,4096]{1,0:T(8,128)(2,1)S(1)} %get-tuple-element.13.refs_1_, bf16[64,4096]{1,0:T(8,128)(2,1)S(1)} %collective-permute-done.1.refs_2_, bf16[64,4096]{1,0:T(8,128)(2,1)S(1)} %copy-done.7, ...), custom_call_target="tpu_custom_call" | custom-call | flops 3758096384 | bytes 11534336 | tf_op jit(solution)/shard_map/pallas_call | solution.py:140
  141.3 10.4 %all-to-all-start.2 = ((bf16[32,16,896]{2,1,0:T(8,128)(2,1)}), bf16[32,16,896]{2,1,0:T(8,128)(2,1)S(1)}, u32[]{:S(2)}, u32[]{:S(2)}) async-start(bf16[32,16,896]{2,1,0:T(8,128)(2,1)} %bitcast.12), calls=%async_computation.2 | async-start | bytes 1835008 | tf_op jit(solution)/shard_map/all_to_all | solution.py:331
  152.6 22.3 %all-to-all-done.2 = bf16[32,16,896]{2,1,0:T(8,128)(2,1)S(1)} async-done(((bf16[32,16,896]{2,1,0:T(8,128)(2,1)}), bf16[32,16,896]{2,1,0:T(8,128)(2,1)S(1)}, u32[]{:S(2)}, u32[]{:S(2)}) %all-to-all-start.2) | async-done | bytes 917536 | tf_op jit(solution)/shard_map/all_to_all | solution.py:331
  174.9 3.3 %shard_map.96 = (bf16[128,3584]{1,0:T(8,128)(2,1)}, f32[8,1,512]{2,1,0:T(1,128)S(1)}) custom-call(bf16[8,4,16,896]{3,2,1,0:T(8,128)(2,1)S(1)} %bitcast.27, bf16[128,3584]{1,0:T(8,128)(2,1)S(1)} %copy-done.1, f32[1,3584]{1,0:T(1,128)S(1)} %broadcast_in_dim_reshape.3.gain_ref), custom_call_target="tpu_custom_call" | custom-call | flops 117440512 | bytes 2752512 | tf_op jit(solution)/shard_map/pallas_call | solution.py:226
  178.2 9.0 %all_to_all.27 = f32[8,1,512]{2,1,0:T(1,128)S(1)} all-to-all(f32[8,1,512]{2,1,0:T(1,128)S(1)} %get-tuple-element.20), channel_id=1, replica_groups=mesh['group'=2,'dp'=32,'mp'=8] {'mp'}, dimensions={0} | all-to-all | bytes 32768 | tf_op jit(solution)/shard_map/all_to_all | solution.py:336
  187.3 20.3 %all_to_all.28 = f32[64,1,512]{2,1,0:T(1,128)S(1)} all-to-all(f32[64,1,512]{2,1,0:T(1,128)S(1)} %broadcast_in_dim.16), channel_id=1, replica_groups=mesh['group'=2,'dp'=32,'mp'=8] {'group','dp'}, dimensions={0} | all-to-all | bytes 262144 | tf_op jit(solution)/shard_map/all_to_all | solution.py:339
  208.3 1.3 slice_divide_fusion
  (43 shorter events, 13.7 us)
Async XLA Ops:
  7.2 0.9 copy-start
  7.2 68.3 %copy-start.2 = (f32[4096]{0:T(1024)S(1)}, f32[4096]{0:T(1024)}, u32[]{:S(2)}) copy-start(f32[4096]{0:T(1024)} %param.8) | copy-start | bytes 49156
  7.2 95.9 %all-gather.2.cloned.1.call-start = ((), (), s32[]{:S(2)}) async-start(), calls=%async_computation.5 | async-start | bytes 4128768 | tf_op jit(solution)/shard_map/all_gather | solution.py:288
  8.1 7.2 %collective-permute-start = (bf16[224,128]{1,0:T(8,128)(2,1)S(1)}, bf16[224,128]{1,0:T(8,128)(2,1)S(1)}, u32[]{:S(2)}, u32[]{:S(2)}) collective-permute-start(bf16[224,128]{1,0:T(8,128)(2,1)S(1)} %dynamic-slice_bitcast_fusion), channel_id=1, source_target_pairs={{0,0},{1,256},{2,8},{3,264},{4,16},{5,272},{6,24},{7,280},{8,2},{9... | collective-permute-start | bytes 172040 | tf_op jit(solution)/shard_map/ppermute | solution.py:271
  44.3 0.8 copy-start.8
  45.9 29.6 %all-to-all-start = ((bf16[8,128,512]{2,1,0:T(8,128)(2,1)}), bf16[8,128,512]{2,1,0:T(8,128)(2,1)S(1)}, u32[]{:S(2)}, u32[]{:S(2)}) async-start(bf16[8,128,512]{2,1,0:T(8,128)(2,1)} %bitcast.32), calls=%async_computation | async-start | bytes 2097152 | tf_op jit(solution)/shard_map/all_to_all | solution.py:307
  76.2 11.8 %collective-permute-start.3 = (bf16[64,4096]{1,0:T(8,128)(2,1)S(1)}, bf16[64,4096]{1,0:T(8,128)(2,1)S(1)}, u32[]{:S(2)}, u32[]{:S(2)}) collective-permute-start(bf16[64,4096]{1,0:T(8,128)(2,1)S(1)} %get-tuple-element.12.refs_0_), channel_id=1, source_target_pairs={{0,24},{8,0},{16,8},{24,16},{32,56},{40,32},{48,40},{56,48},{64,88... | collective-permute-start | bytes 1572872 | tf_op jit(solution)/shard_map/ppermute | solution.py:251
  78.1 13.0 %collective-permute-start.1 = (bf16[64,4096]{1,0:T(8,128)(2,1)S(1)}, bf16[64,4096]{1,0:T(8,128)(2,1)S(1)}, u32[]{:S(2)}, u32[]{:S(2)}) collective-permute-start(bf16[64,4096]{1,0:T(8,128)(2,1)S(1)} %get-tuple-element.12.refs_0_), channel_id=1, source_target_pairs={{0,8},{8,16},{16,24},{24,0},{32,40},{40,48},{48,56},{56,32},{64,72... | collective-permute-start | bytes 1572872 | tf_op jit(solution)/shard_map/ppermute | solution.py:248
  81.5 17.6 %collective-permute-start.4 = (bf16[64,4096]{1,0:T(8,128)(2,1)S(1)}, bf16[64,4096]{1,0:T(8,128)(2,1)S(1)}, u32[]{:S(2)}, u32[]{:S(2)}) collective-permute-start(bf16[64,4096]{1,0:T(8,128)(2,1)S(1)} %get-tuple-element.13.refs_1_), channel_id=1, source_target_pairs={{0,24},{8,0},{16,8},{24,16},{32,56},{40,32},{48,40},{56,48},{64,88... | collective-permute-start | bytes 1572872 | tf_op jit(solution)/shard_map/ppermute | solution.py:249
  84.6 17.6 %collective-permute-start.2 = (bf16[64,4096]{1,0:T(8,128)(2,1)S(1)}, bf16[64,4096]{1,0:T(8,128)(2,1)S(1)}, u32[]{:S(2)}, u32[]{:S(2)}) collective-permute-start(bf16[64,4096]{1,0:T(8,128)(2,1)S(1)} %get-tuple-element.13.refs_1_), channel_id=1, source_target_pairs={{0,8},{8,16},{16,24},{24,0},{32,40},{40,48},{48,56},{56,32},{64,72... | collective-permute-start | bytes 1572872 | tf_op jit(solution)/shard_map/ppermute | solution.py:250
  102.3 0.8 copy-start.6
  103.0 24.0 %collective-permute-start.7 = (bf16[8,8,224,128]{3,2,1,0:T(8,128)(2,1)}, bf16[8,8,224,128]{3,2,1,0:T(8,128)(2,1)S(1)}, u32[]{:S(2)}, u32[]{:S(2)}) collective-permute-start(bf16[8,8,224,128]{3,2,1,0:T(8,128)(2,1)} %bitcast.29), channel_id=1, source_target_pairs={{0,256},{256,0},{1,257},{257,1},{2,258},{258,2},{3,259},{259,3},{4... | collective-permute-start | bytes 11010056 | tf_op jit(solution)/shard_map/ppermute | solution.py:326
  109.5 16.6 %collective-permute-start.5 = (bf16[64,4096]{1,0:T(8,128)(2,1)S(1)}, bf16[64,4096]{1,0:T(8,128)(2,1)S(1)}, u32[]{:S(2)}, u32[]{:S(2)}) collective-permute-start(bf16[64,4096]{1,0:T(8,128)(2,1)S(1)} %collective-permute-done.1.refs_2_), channel_id=1, source_target_pairs={{0,8},{8,16},{16,24},{24,0},{32,40},{40,48},{48,56},{56,32},{64,72... | collective-permute-start | bytes 1572872 | tf_op jit(solution)/shard_map/ppermute | solution.py:252
  111.7 15.4 %collective-permute-start.6 = (bf16[64,4096]{1,0:T(8,128)(2,1)S(1)}, bf16[64,4096]{1,0:T(8,128)(2,1)S(1)}, u32[]{:S(2)}, u32[]{:S(2)}) collective-permute-start(bf16[64,4096]{1,0:T(8,128)(2,1)S(1)} %collective-permute-done.4.refs_7_), channel_id=1, source_target_pairs={{0,24},{8,0},{16,8},{24,16},{32,56},{40,32},{48,40},{56,48},{64,88... | collective-permute-start | bytes 1572872 | tf_op jit(solution)/shard_map/ppermute | solution.py:253
  116.0 0.8 copy-start.4
  127.0 2.0 copy-start.3
  129.1 1.0 copy-start.5
  130.1 1.0 copy-start.7
  131.2 43.7 %copy-start.1 = (bf16[128,3584]{1,0:T(8,128)(2,1)S(1)}, bf16[128,3584]{1,0:T(8,128)(2,1)}, u32[]{:S(2)}) copy-start(bf16[128,3584]{1,0:T(8,128)(2,1)} %hidden_ref.1) | copy-start | bytes 2752516
  141.3 33.6 %all-to-all-start.2 = ((bf16[32,16,896]{2,1,0:T(8,128)(2,1)}), bf16[32,16,896]{2,1,0:T(8,128)(2,1)S(1)}, u32[]{:S(2)}, u32[]{:S(2)}) async-start(bf16[32,16,896]{2,1,0:T(8,128)(2,1)} %bitcast.12), calls=%async_computation.2 | async-start | bytes 1835008 | tf_op jit(solution)/shard_map/all_to_all | solution.py:331
Sparse Core Ops, SparseCore 0:
  46.1 49.7 all-gather.1

commit v2 on v1

--- a/solution.py
+++ b/solution.py
@@ -53,110 +53,118 @@
     )(moved, slot[None, :], teacher_gain[None, :])
 
 
-def product_kernel(shards, count, place_ref, *refs):
-    sources, weight_sources = refs[:count], refs[count : count + 2]
-    out_ref, rows_buffer, weights, sums, row_sems, weight_sems = refs[count + 2 :]
-    y_count, shares = weights.shape[1:3]
-    steps = weight_sems.shape[1]
+def block_product(sources, weight_source, rows_buffer, weights, total, row_sems, weight_sems):
+    steps = weight_sems.shape[0]
+    y_count, shares, half, tile = weights.shape
     spans = y_count // steps
     part = rows_buffer.shape[1] // steps
     height = sources[0].shape[0]
-    row_copies = [
-        pltpu.make_async_copy(source, rows_buffer.at[pl.ds(i * height, height)], row_sems.at[i])
-        for i, source in enumerate(sources)
-    ]
-    weight_copies = [
-        [
+    copies = []
+    for step in range(steps):
+        features = pl.ds(step * part, part)
+        chunk = [
             pltpu.make_async_copy(
-                source.at[pl.ds(step * spans, spans)],
-                weights.at[side, pl.ds(step * spans, spans)],
-                weight_sems.at[side, step],
+                source.at[:, features],
+                rows_buffer.at[pl.ds(i * height, height), features],
+                row_sems.at[i, step],
             )
-            for step in range(steps)
+            for i, source in enumerate(sources)
         ]
-        for side, source in enumerate(weight_sources)
-    ]
-    for copy in row_copies:
-        copy.start()
+        blocks = pl.ds(step * spans, spans)
+        chunk.append(
+            pltpu.make_async_copy(weight_source.at[blocks], weights.at[blocks], weight_sems.at[step])
+        )
+        copies.append(chunk)
+    for chunk in copies:
+        for copy in chunk:
+            copy.start()
     for step in range(steps):
-        for side in range(2):
-            weight_copies[side][step].start()
-    for copy in row_copies:
-        copy.wait()
-
-    core = place_ref[0]
-    for step in range(steps):
-        rows = rows_buffer[:, step * part : (step + 1) * part]
-        for side in range(2):
-            weight_copies[side][step].wait()
-            tiles = []
-            for span in range(step * spans, (step + 1) * spans):
-                for pair in range(shares // 2):
-                    halves = weights[side, span, 2 * pair : 2 * pair + 2]
-                    tiles.append(halves.reshape(-1, halves.shape[-1]))
-            partial = lax.dot_general(
-                rows,
-                jnp.concatenate(tiles, axis=1),
-                (((1,), (1,)), ((), ())),
-                preferred_element_type=jnp.float32,
-            )
-            if step == 0:
-                sums[side] = partial
-            else:
-                sums[side] += partial
-
-    total_rows, width = sums.shape[1:]
-    depth = total_rows // shards
-    to = lax.broadcasted_iota(jnp.int32, (total_rows, total_rows), 0)
-    source = lax.broadcasted_iota(jnp.int32, (total_rows, total_rows), 1)
+        for copy in copies[step]:
+            copy.wait()
+        tiles = [
+            weights[span, 2 * pair : 2 * pair + 2].reshape(2 * half, tile)
+            for span in range(step * spans, (step + 1) * spans)
+            for pair in range(shares // 2)
+        ]
+        partial = lax.dot_general(
+            rows_buffer[:, step * part : (step + 1) * part],
+            jnp.concatenate(tiles, axis=1),
+            (((1,), (1,)), ((), ())),
+            preferred_element_type=jnp.float32,
+        )
+        if step == 0:
+            total[...] = partial
+        else:
+            total[...] += partial
+
+
+def turned(shards, total, rows_buffer):
+    rows = total.shape[0]
+    depth = rows // shards
+    to = lax.broadcasted_iota(jnp.int32, (rows, rows), 0)
+    source = lax.broadcasted_iota(jnp.int32, (rows, rows), 1)
     turn = (source == (to % depth) * shards + to // depth).astype(jnp.bfloat16)
     empty = rows_buffer[:, :128].astype(jnp.float32)[:, 0:1] > EMPTY_FROM
-
-    def turned(side):
-        kept = jnp.where(empty, EMPTY, sums[side]).astype(jnp.bfloat16)
-        return jnp.dot(turn, kept, preferred_element_type=jnp.float32).astype(jnp.bfloat16)
-
-    mine = turned(0)
-    other = turned(1)
-
-    @pl.when(core == 0)
+    kept = jnp.where(empty, EMPTY, total[...]).astype(jnp.bfloat16)
+    return jnp.dot(turn, kept, preferred_element_type=jnp.float32).astype(jnp.bfloat16)
+
+
+def first_kernel(shards, count, *refs):
+    out_ref, rows_buffer, weights, total, row_sems, weight_sems = refs[count + 1 :]
+    block_product(refs[:count], refs[count], rows_buffer, weights, total, row_sems, weight_sems)
+    out_ref[...] = turned(shards, total, rows_buffer)
+
+
+def second_kernel(shards, count, core_ref, first_ref, *refs):
+    out_ref, rows_buffer, weights, total, row_sems, weight_sems = refs[count + 1 :]
+    block_product(refs[:count], refs[count], rows_buffer, weights, total, row_sems, weight_sems)
+    width = total.shape[1]
+    mine = first_ref[...]
+    other = turned(shards, total, rows_buffer)
+
+    @pl.when(core_ref[0] == 0)
     def _():
         out_ref[:, :width] = mine
         out_ref[:, width:] = other
 
-    @pl.when(core != 0)
+    @pl.when(core_ref[0] != 0)
     def _():
         out_ref[:, :width] = other
         out_ref[:, width:] = mine
 
 
-def product(place, pieces, mine, other, shards):
-    y_count, shares, half, tile = mine.shape
+def product(pieces, weights, shards, core=None, first=None):
+    y_count, shares, half, tile = weights.shape
     width = 2 * half
     depth = y_count * (shares // 2) * tile
     count = len(pieces)
     total_rows = pieces[0].shape[0] * count
     steps = 4
+    joined = first is not None
+    in_vmem = pl.BlockSpec(memory_space=pltpu.VMEM)
+    head = [pl.BlockSpec(memory_space=pltpu.SMEM), in_vmem] if joined else []
+    kernel = second_kernel if joined else first_kernel
     return pl.pallas_call(
-        functools.partial(product_kernel, shards, count),
-        out_shape=jax.ShapeDtypeStruct((total_rows, 2 * width), jnp.bfloat16),
-        in_specs=[pl.BlockSpec(memory_space=pltpu.SMEM)]
-        + [pl.BlockSpec(memory_space=pl.ANY)] * (count + 2),
-        out_specs=pl.BlockSpec(memory_space=pltpu.VMEM),
+        functools.partial(kernel, shards, count),
+        out_shape=jax.ShapeDtypeStruct(
+            (total_rows, 2 * width if joined else width), jnp.bfloat16
+        ),
+        in_specs=head + [pl.BlockSpec(memory_space=pl.ANY)] * (count + 1),
+        out_specs=in_vmem,
         scratch_shapes=[
             pltpu.VMEM((total_rows, depth), jnp.bfloat16),
-            pltpu.VMEM((2,) + mine.shape, jnp.bfloat16),
-            pltpu.VMEM((2, total_rows, width), jnp.float32),
-            pltpu.SemaphoreType.DMA((count,)),
-            pltpu.SemaphoreType.DMA((2, steps)),
+            pltpu.VMEM(weights.shape, jnp.bfloat16),
+            pltpu.VMEM((total_rows, width), jnp.float32),
+            pltpu.SemaphoreType.DMA((count, steps)),
+            pltpu.SemaphoreType.DMA((steps,)),
         ],
-        compiler_params=pltpu.CompilerParams(vmem_limit_bytes=32 * MIB),
+        compiler_params=pltpu.CompilerParams(vmem_limit_bytes=56 * MIB),
         cost_estimate=pl.CostEstimate(
-            flops=4 * total_rows * depth * width,
-            bytes_accessed=2 * depth * (total_rows + 2 * width),
+            flops=2 * total_rows * depth * width,
+            bytes_accessed=2 * depth * (total_rows + width),
             transcendentals=0,
         ),
-    )(place, *pieces, mine, other)
+    )(*((core, first) if joined else ()), *pieces, weights)
 
 
 def finish_kernel(
@@ -320,12 +328,10 @@
 
     top, low = norm_rows(moved, slot, teacher_gain)
     pieces = ring_gather(top, low, x_count, dp_count)
-    mine, pieces[2], pieces[3], pieces[6], pieces[7] = lax.optimization_barrier(
-        (mine, pieces[2], pieces[3], pieces[6], pieces[7])
-    )
+    mine, pieces = lax.optimization_barrier((mine, pieces))
     other = lax.ppermute(mine, "group", [(0, 1), (1, 0)])
-
-    buffer = product(core.astype(jnp.int32).reshape(1), pieces, mine, other, dp_count)
+    first = product(pieces, mine, dp_count)
+    buffer = product(pieces, other, dp_count, core.astype(jnp.int32).reshape(1), first)
     quarter = buffer.shape[1]
     deep = x_count * capacity
     received = lax.all_to_all(

time: 220 us -> 215 us (0.977)
  waiting for transfers between devices: 72.8 us -> 67 us
  Pallas kernels: 14.2 us -> 19.3 us
  local copies, waits for them, and re-layouts: 9.84 us -> 6.75 us
    ppermute x1, waiting for transfers between devices: 7.99 us -> 0.01 us  [ring_gather(): right_low = lax.ppermute(low, 'dp', backward)]
    pallas_call x1 -> x2, Pallas kernels: 10.2 us -> 15.3 us  [product(): pl.pallas_call(functools.partial(kernel, shards, count), out_shape=jax.Sh...]
    ppermute x1, waiting for transfers between devices: 1.18 us -> 5.9 us  [ring_gather(): right_top = lax.ppermute(top, 'dp', backward)]
    unnamed x19 -> x25, local copies, waits for them, and re-layouts: 7.36 us -> 4.32 us
    ppermute x1, waiting for transfers between devices: 3.14 us -> 0.14 us  [ring_gather(): left_low = lax.ppermute(low, 'dp', forward)]
  transfers between devices with their start and end apart: 11 -> 11, of which waited for: 9 -> 7; matrix products, arithmetic and copies ran while one was open for 2% -> 2% of each run, Pallas kernels for 0% -> 4%
where the time goes in v2:
time: 215 us; the launch traced here: 214 us
  waiting for transfers between devices  67 us (31%)
  blocking collectives  56.8 us (26%)
  starting transfers between devices  43.1 us (20%)
  Pallas kernels  19.3 us (9%)
  between operations  16.7 us (8%)
  local copies, waits for them, and re-layouts  6.75 us (3%)
  other arithmetic  4.43 us (2%)
    all_to_all x1, blocking collectives, projector_columns(): lax.all_to_all(jnp.broadcast_to(message[None], (mp_count,) + message.shap...  28.9 us
    all_to_all x1, waiting for transfers between devices, local(): moved = lax.all_to_all(blocks, 'mp', 0, 0, tiled=True)  23.8 us
    all_to_all x1, waiting for transfers between devices, local(): lax.all_to_all(buffer.reshape(dp_count, deep, quarter), 'dp', 0, 0, tiled...  23.6 us
    all_to_all x1, blocking collectives, local(): lax.all_to_all(jnp.broadcast_to(over_mp[None, :], (peers, over_mp.shape[0...  18.9 us
    pallas_call x2, Pallas kernels, product(): pl.pallas_call(functools.partial(kernel, shards, count), out_shape=jax.Sh...  15.3 us
    ppermute x1, waiting for transfers between devices, ring_gather(): far_top = lax.ppermute(left_top, 'dp', forward)  11.2 us
    all_to_all x1, starting transfers between devices, local(): lax.all_to_all(buffer.reshape(dp_count, deep, quarter), 'dp', 0, 0, tiled...  9.87 us
    all_to_all x1, blocking collectives, local(): lax.all_to_all(message, 'mp', 0, 0, tiled=True)  8.97 us
  transfers between devices with their start and end apart: 11, of which 7 were waited for; matrix products, arithmetic and copies ran while one was open for 2% of the time, Pallas kernels for 4%

profile of v2, /device:TPU:1, one launch (start us, length us, event | category | flops | bytes accessed | tf_op | source)
XLA Modules:
  0.0 214.0 jit_solution(11031287976842658994)
XLA Ops:
  8.1 5.4 %collective-permute-start = (bf16[224,128]{1,0:T(8,128)(2,1)S(1)}, bf16[224,128]{1,0:T(8,128)(2,1)S(1)}, u32[]{:S(2)}, u32[]{:S(2)}) collective-permute-start(bf16[224,128]{1,0:T(8,128)(2,1)S(1)} %dynamic-slice_bitcast_fusion), channel_id=1, source_target_pairs={{0,0},{1,256},{2,8},{3,264},{4,16},{5,272},{6,24},{7,280},{8,2},{9... | collective-permute-start | bytes 172040 | tf_op jit(solution)/shard_map/ppermute | solution.py:279
  14.2 1.1 collective-permute-done
  15.4 28.9 %all_to_all.26 = bf16[8,240,128]{2,1,0:T(8,128)(2,1)S(1)} all-to-all(bf16[8,240,128]{2,1,0:T(8,128)(2,1)S(1)} %broadcast_in_dim.13), channel_id=1, replica_groups=mesh['group'=2,'dp'=32,'mp'=8] {'mp'}, dimensions={0} | all-to-all | bytes 983040 | tf_op jit(solution)/shard_map/all_to_all | solution.py:289
  46.0 3.6 %all-to-all-start.1 = ((bf16[8,128,512]{2,1,0:T(8,128)(2,1)}), bf16[8,128,512]{2,1,0:T(8,128)(2,1)S(1)}, u32[]{:S(2)}, u32[]{:S(2)}) async-start(bf16[8,128,512]{2,1,0:T(8,128)(2,1)} %bitcast.33), calls=%async_computation.1 | async-start | bytes 2097152 | tf_op jit(solution)/shard_map/all_to_all | solution.py:315
  51.8 23.8 %all-to-all-done.1.moved_ref = bf16[8,128,512]{2,1,0:T(8,128)(2,1)S(1)} async-done(((bf16[8,128,512]{2,1,0:T(8,128)(2,1)}), bf16[8,128,512]{2,1,0:T(8,128)(2,1)S(1)}, u32[]{:S(2)}, u32[]{:S(2)}) %all-to-all-start.1) | async-done | bytes 1048608 | tf_op jit(solution)/shard_map/all_to_all | solution.py:315
  76.3 2.9 %collective-permute-start.1 = (bf16[64,4096]{1,0:T(8,128)(2,1)S(1)}, bf16[64,4096]{1,0:T(8,128)(2,1)S(1)}, u32[]{:S(2)}, u32[]{:S(2)}) collective-permute-start(bf16[64,4096]{1,0:T(8,128)(2,1)S(1)} %get-tuple-element.18.refs_0_), channel_id=1, source_target_pairs={{0,8},{8,16},{16,24},{24,0},{32,40},{40,48},{48,56},{56,32},{64,72... | collective-permute-start | bytes 1572872 | tf_op jit(solution)/shard_map/ppermute | solution.py:256
  79.1 3.6 %collective-permute-start.4 = (bf16[64,4096]{1,0:T(8,128)(2,1)S(1)}, bf16[64,4096]{1,0:T(8,128)(2,1)S(1)}, u32[]{:S(2)}, u32[]{:S(2)}) collective-permute-start(bf16[64,4096]{1,0:T(8,128)(2,1)S(1)} %get-tuple-element.19.refs_1_), channel_id=1, source_target_pairs={{0,24},{8,0},{16,8},{24,16},{32,56},{40,32},{48,40},{56,48},{64,88... | collective-permute-start | bytes 1572872 | tf_op jit(solution)/shard_map/ppermute | solution.py:257
  82.8 1.9 collective-permute-start.6
  84.7 3.4 %collective-permute-start.2 = (bf16[64,4096]{1,0:T(8,128)(2,1)S(1)}, bf16[64,4096]{1,0:T(8,128)(2,1)S(1)}, u32[]{:S(2)}, u32[]{:S(2)}) collective-permute-start(bf16[64,4096]{1,0:T(8,128)(2,1)S(1)} %get-tuple-element.19.refs_1_), channel_id=1, source_target_pairs={{0,8},{8,16},{16,24},{24,0},{32,40},{40,48},{48,56},{56,32},{64,72... | collective-permute-start | bytes 1572872 | tf_op jit(solution)/shard_map/ppermute | solution.py:258
  88.1 1.2 collective-permute-done.1.refs_2_
  89.3 1.9 collective-permute-start.3
  91.2 4.6 %collective-permute-start.5 = (bf16[64,4096]{1,0:T(8,128)(2,1)S(1)}, bf16[64,4096]{1,0:T(8,128)(2,1)}, u32[]{:S(2)}, u32[]{:S(2)}) collective-permute-start(bf16[64,4096]{1,0:T(8,128)(2,1)S(1)} %collective-permute-done.4.refs_7_), channel_id=1, source_target_pairs={{0,24},{8,0},{16,8},{24,16},{32,56},{40,32},{48,40},{56,48},{64,88... | collective-permute-start | bytes 1572872 | tf_op jit(solution)/shard_map/ppermute | solution.py:261
  95.8 5.9 %collective-permute-done.6.refs_6_ = bf16[64,4096]{1,0:T(8,128)(2,1)S(1)} collective-permute-done((bf16[64,4096]{1,0:T(8,128)(2,1)S(1)}, bf16[64,4096]{1,0:T(8,128)(2,1)S(1)}, u32[]{:S(2)}, u32[]{:S(2)}) %collective-permute-start.6) | collective-permute-done | bytes 524320 | tf_op jit(solution)/shard_map/ppermute | solution.py:259
  101.8 11.2 %collective-permute-done.3.refs_4_ = bf16[64,4096]{1,0:T(8,128)(2,1)S(1)} collective-permute-done((bf16[64,4096]{1,0:T(8,128)(2,1)S(1)}, bf16[64,4096]{1,0:T(8,128)(2,1)S(1)}, u32[]{:S(2)}, u32[]{:S(2)}) %collective-permute-start.3) | collective-permute-done | bytes 524320 | tf_op jit(solution)/shard_map/ppermute | solution.py:260
  113.9 6.0 %collective-permute-start.7 = (bf16[8,8,224,128]{3,2,1,0:T(8,128)(2,1)}, bf16[8,8,224,128]{3,2,1,0:T(8,128)(2,1)S(1)}, u32[]{:S(2)}, u32[]{:S(2)}) collective-permute-start(bf16[8,8,224,128]{3,2,1,0:T(8,128)(2,1)} %bitcast.30), channel_id=1, source_target_pairs={{0,256},{256,0},{1,257},{257,1},{2,258},{258,2},{3,259},{259,3},{4... | collective-permute-start | bytes 11010056 | tf_op jit(solution)/shard_map/ppermute | solution.py:332
  119.9 6.9 %shard_map.95.first_ref = bf16[512,448]{1,0:T(8,128)(2,1)} custom-call(bf16[64,4096]{1,0:T(8,128)(2,1)} %copy-done.1, bf16[64,4096]{1,0:T(8,128)(2,1)} %copy-done.2, bf16[64,4096]{1,0:T(8,128)(2,1)} %copy-done.6, bf16[64,4096]{1,0:T(8,128)(2,1)} %copy-done.9, bf16[64,4096]{1,0:T(8,128)(2,1)} %copy-done.10, bf16[64,4096]{1,0:T(8,128)(2,1)} %collective-permute-done.5.refs_5_, ...), custom_call_target="tpu_custom_call" | custom-call | flops 1879048192 | bytes 7864320 | tf_op jit(solution)/shard_map/pallas_call | solution.py:147
  126.9 1.8 copy-done.5
  128.7 8.4 %shard_map.96 = bf16[512,896]{1,0:T(8,128)(2,1)} custom-call(s32[1]{0:T(128)} %bitcast.core_ref, bf16[512,448]{1,0:T(8,128)(2,1)} %shard_map.95.first_ref, bf16[64,4096]{1,0:T(8,128)(2,1)} %copy-done.1, bf16[64,4096]{1,0:T(8,128)(2,1)} %copy-done.2, bf16[64,4096]{1,0:T(8,128)(2,1)} %copy-done.6, bf16[64,4096]{1,0:T(8,128)(2,1)} %copy-done.9, ...), custom_call_target="tpu_custom_call" | custom-call | flops 1879048192 | bytes 7864320 | tf_op jit(solution)/shard_map/pallas_call | solution.py:147
  137.0 9.9 %all-to-all-start.2 = ((bf16[32,16,896]{2,1,0:T(8,128)(2,1)}), bf16[32,16,896]{2,1,0:T(8,128)(2,1)S(1)}, u32[]{:S(2)}, u32[]{:S(2)}) async-start(bf16[32,16,896]{2,1,0:T(8,128)(2,1)} %bitcast.29), calls=%async_computation.2 | async-start | bytes 1835008 | tf_op jit(solution)/shard_map/all_to_all | solution.py:337
  147.9 23.6 %all-to-all-done.2 = bf16[32,16,896]{2,1,0:T(8,128)(2,1)S(1)} async-done(((bf16[32,16,896]{2,1,0:T(8,128)(2,1)}), bf16[32,16,896]{2,1,0:T(8,128)(2,1)S(1)}, u32[]{:S(2)}, u32[]{:S(2)}) %all-to-all-start.2) | async-done | bytes 917536 | tf_op jit(solution)/shard_map/all_to_all | solution.py:337
  171.5 3.3 %shard_map.97 = (bf16[128,3584]{1,0:T(8,128)(2,1)}, f32[8,1,512]{2,1,0:T(1,128)S(1)}) custom-call(bf16[8,4,16,896]{3,2,1,0:T(8,128)(2,1)S(1)} %bitcast.27, bf16[128,3584]{1,0:T(8,128)(2,1)S(1)} %copy-done.3, f32[1,3584]{1,0:T(1,128)S(1)} %broadcast_in_dim_reshape.3.gain_ref), custom_call_target="tpu_custom_call" | custom-call | flops 117440512 | bytes 2752512 | tf_op jit(solution)/shard_map/pallas_call | solution.py:234
  174.8 9.0 %all_to_all.27 = f32[8,1,512]{2,1,0:T(1,128)S(1)} all-to-all(f32[8,1,512]{2,1,0:T(1,128)S(1)} %get-tuple-element.28), channel_id=1, replica_groups=mesh['group'=2,'dp'=32,'mp'=8] {'mp'}, dimensions={0} | all-to-all | bytes 32768 | tf_op jit(solution)/shard_map/all_to_all | solution.py:342
  183.9 18.9 %all_to_all.28 = f32[64,1,512]{2,1,0:T(1,128)S(1)} all-to-all(f32[64,1,512]{2,1,0:T(1,128)S(1)} %broadcast_in_dim.16), channel_id=1, replica_groups=mesh['group'=2,'dp'=32,'mp'=8] {'group','dp'}, dimensions={0} | all-to-all | bytes 262144 | tf_op jit(solution)/shard_map/all_to_all | solution.py:345
  203.5 1.2 slice_divide_fusion
  (50 shorter events, 9.1 us)
Async XLA Ops:
  7.2 0.9 copy-start
  7.2 68.4 %copy-start.4 = (f32[4096]{0:T(1024)S(1)}, f32[4096]{0:T(1024)}, u32[]{:S(2)}) copy-start(f32[4096]{0:T(1024)} %param.8) | copy-start | bytes 49156
  7.2 106.7 %all-gather.2.cloned.1.call-start = ((), (), s32[]{:S(2)}) async-start(), calls=%async_computation.5 | async-start | bytes 4128768 | tf_op jit(solution)/shard_map/all_gather | solution.py:296
  8.1 7.2 %collective-permute-start = (bf16[224,128]{1,0:T(8,128)(2,1)S(1)}, bf16[224,128]{1,0:T(8,128)(2,1)S(1)}, u32[]{:S(2)}, u32[]{:S(2)}) collective-permute-start(bf16[224,128]{1,0:T(8,128)(2,1)S(1)} %dynamic-slice_bitcast_fusion), channel_id=1, source_target_pairs={{0,0},{1,256},{2,8},{3,264},{4,16},{5,272},{6,24},{7,280},{8,2},{9... | collective-permute-start | bytes 172040 | tf_op jit(solution)/shard_map/ppermute | solution.py:279
  44.3 0.8 copy-start.11
  46.0 29.6 %all-to-all-start.1 = ((bf16[8,128,512]{2,1,0:T(8,128)(2,1)}), bf16[8,128,512]{2,1,0:T(8,128)(2,1)S(1)}, u32[]{:S(2)}, u32[]{:S(2)}) async-start(bf16[8,128,512]{2,1,0:T(8,128)(2,1)} %bitcast.33), calls=%async_computation.1 | async-start | bytes 2097152 | tf_op jit(solution)/shard_map/all_to_all | solution.py:315
  76.3 43.6 %copy-start.1 = (bf16[64,4096]{1,0:T(8,128)(2,1)}, bf16[64,4096]{1,0:T(8,128)(2,1)S(1)}, u32[]{:S(2)}) copy-start(bf16[64,4096]{1,0:T(8,128)(2,1)S(1)} %get-tuple-element.18.refs_0_) | copy-start | bytes 1572868
  76.3 43.6 %copy-start.2 = (bf16[64,4096]{1,0:T(8,128)(2,1)}, bf16[64,4096]{1,0:T(8,128)(2,1)S(1)}, u32[]{:S(2)}) copy-start(bf16[64,4096]{1,0:T(8,128)(2,1)S(1)} %get-tuple-element.19.refs_1_) | copy-start | bytes 1572868
  76.3 13.0 %collective-permute-start.1 = (bf16[64,4096]{1,0:T(8,128)(2,1)S(1)}, bf16[64,4096]{1,0:T(8,128)(2,1)S(1)}, u32[]{:S(2)}, u32[]{:S(2)}) collective-permute-start(bf16[64,4096]{1,0:T(8,128)(2,1)S(1)} %get-tuple-element.18.refs_0_), channel_id=1, source_target_pairs={{0,8},{8,16},{16,24},{24,0},{32,40},{40,48},{48,56},{56,32},{64,72... | collective-permute-start | bytes 1572872 | tf_op jit(solution)/shard_map/ppermute | solution.py:256
  79.1 12.0 %collective-permute-start.4 = (bf16[64,4096]{1,0:T(8,128)(2,1)S(1)}, bf16[64,4096]{1,0:T(8,128)(2,1)S(1)}, u32[]{:S(2)}, u32[]{:S(2)}) collective-permute-start(bf16[64,4096]{1,0:T(8,128)(2,1)S(1)} %get-tuple-element.19.refs_1_), channel_id=1, source_target_pairs={{0,24},{8,0},{16,8},{24,16},{32,56},{40,32},{48,40},{56,48},{64,88... | collective-permute-start | bytes 1572872 | tf_op jit(solution)/shard_map/ppermute | solution.py:257
  82.8 18.9 %collective-permute-start.6 = (bf16[64,4096]{1,0:T(8,128)(2,1)S(1)}, bf16[64,4096]{1,0:T(8,128)(2,1)S(1)}, u32[]{:S(2)}, u32[]{:S(2)}) collective-permute-start(bf16[64,4096]{1,0:T(8,128)(2,1)S(1)} %get-tuple-element.18.refs_0_), channel_id=1, source_target_pairs={{0,24},{8,0},{16,8},{24,16},{32,56},{40,32},{48,40},{56,48},{64,88... | collective-permute-start | bytes 1572872 | tf_op jit(solution)/shard_map/ppermute | solution.py:259
  84.7 17.1 %collective-permute-start.2 = (bf16[64,4096]{1,0:T(8,128)(2,1)S(1)}, bf16[64,4096]{1,0:T(8,128)(2,1)S(1)}, u32[]{:S(2)}, u32[]{:S(2)}) collective-permute-start(bf16[64,4096]{1,0:T(8,128)(2,1)S(1)} %get-tuple-element.19.refs_1_), channel_id=1, source_target_pairs={{0,8},{8,16},{16,24},{24,0},{32,40},{40,48},{48,56},{56,32},{64,72... | collective-permute-start | bytes 1572872 | tf_op jit(solution)/shard_map/ppermute | solution.py:258
  89.3 30.6 %copy-start.6 = (bf16[64,4096]{1,0:T(8,128)(2,1)}, bf16[64,4096]{1,0:T(8,128)(2,1)S(1)}, u32[]{:S(2)}) copy-start(bf16[64,4096]{1,0:T(8,128)(2,1)S(1)} %collective-permute-done.1.refs_2_) | copy-start | bytes 1572868
  89.3 23.8 %collective-permute-start.3 = (bf16[64,4096]{1,0:T(8,128)(2,1)S(1)}, bf16[64,4096]{1,0:T(8,128)(2,1)S(1)}, u32[]{:S(2)}, u32[]{:S(2)}) collective-permute-start(bf16[64,4096]{1,0:T(8,128)(2,1)S(1)} %collective-permute-done.1.refs_2_), channel_id=1, source_target_pairs={{0,8},{8,16},{16,24},{24,0},{32,40},{40,48},{48,56},{56,32},{64,72... | collective-permute-start | bytes 1572872 | tf_op jit(solution)/shard_map/ppermute | solution.py:260
  91.2 28.7 %copy-start.7 = (bf16[64,4096]{1,0:T(8,128)(2,1)}, bf16[64,4096]{1,0:T(8,128)(2,1)S(1)}, u32[]{:S(2)}) copy-start(bf16[64,4096]{1,0:T(8,128)(2,1)S(1)} %collective-permute-done.4.refs_7_) | copy-start | bytes 1572868
  91.2 22.7 %collective-permute-start.5 = (bf16[64,4096]{1,0:T(8,128)(2,1)S(1)}, bf16[64,4096]{1,0:T(8,128)(2,1)}, u32[]{:S(2)}, u32[]{:S(2)}) collective-permute-start(bf16[64,4096]{1,0:T(8,128)(2,1)S(1)} %collective-permute-done.4.refs_7_), channel_id=1, source_target_pairs={{0,24},{8,0},{16,8},{24,16},{32,56},{40,32},{48,40},{56,48},{64,88... | collective-permute-start | bytes 1572872 | tf_op jit(solution)/shard_map/ppermute | solution.py:261
  101.7 18.2 %copy-start.8 = (bf16[64,4096]{1,0:T(8,128)(2,1)}, bf16[64,4096]{1,0:T(8,128)(2,1)S(1)}, u32[]{:S(2)}) copy-start(bf16[64,4096]{1,0:T(8,128)(2,1)S(1)} %collective-permute-done.6.refs_6_) | copy-start | bytes 1572868
  101.8 18.1 %copy-start.9 = (bf16[64,4096]{1,0:T(8,128)(2,1)}, bf16[64,4096]{1,0:T(8,128)(2,1)S(1)}, u32[]{:S(2)}) copy-start(bf16[64,4096]{1,0:T(8,128)(2,1)S(1)} %collective-permute-done.2.refs_3_) | copy-start | bytes 1572868
  113.1 0.8 copy-start.10
  113.9 13.0 %collective-permute-start.7 = (bf16[8,8,224,128]{3,2,1,0:T(8,128)(2,1)}, bf16[8,8,224,128]{3,2,1,0:T(8,128)(2,1)S(1)}, u32[]{:S(2)}, u32[]{:S(2)}) collective-permute-start(bf16[8,8,224,128]{3,2,1,0:T(8,128)(2,1)} %bitcast.30), channel_id=1, source_target_pairs={{0,256},{256,0},{1,257},{257,1},{2,258},{258,2},{3,259},{259,3},{4... | collective-permute-start | bytes 11010056 | tf_op jit(solution)/shard_map/ppermute | solution.py:332
  126.9 1.8 copy-start.5
  128.7 42.9 %copy-start.3 = (bf16[128,3584]{1,0:T(8,128)(2,1)S(1)}, bf16[128,3584]{1,0:T(8,128)(2,1)}, u32[]{:S(2)}) copy-start(bf16[128,3584]{1,0:T(8,128)(2,1)} %hidden_ref.1) | copy-start | bytes 2752516
  137.0 34.5 %all-to-all-start.2 = ((bf16[32,16,896]{2,1,0:T(8,128)(2,1)}), bf16[32,16,896]{2,1,0:T(8,128)(2,1)S(1)}, u32[]{:S(2)}, u32[]{:S(2)}) async-start(bf16[32,16,896]{2,1,0:T(8,128)(2,1)} %bitcast.29), calls=%async_computation.2 | async-start | bytes 1835008 | tf_op jit(solution)/shard_map/all_to_all | solution.py:337
Sparse Core Ops, SparseCore 0:
  46.1 49.7 all-gather.1

commit v3 on v2

--- a/solution.py
+++ b/solution.py
@@ -10,50 +10,43 @@
 EPSILON = 1e-06
 RING = 4
 MIB = 1024 * 1024
+SLOT_LANES = 128
 EMPTY = 1e30
 EMPTY_FROM = 1e20
 
 
-def norm_kernel(moved_ref, slot_ref, gain_ref, top_ref, low_ref, packed):
+def norm_kernel(moved_ref, slot_ref, gain_ref, out_ref):
     parts, rows, features = moved_ref.shape
-    order = lax.broadcasted_iota(jnp.int32, (rows, rows), 0)
-    packer = (order == slot_ref[...]).astype(jnp.bfloat16)
     total = jnp.zeros((rows, 1), jnp.float32)
     for part in range(parts):
-        values = jnp.dot(packer, moved_ref[part], preferred_element_type=jnp.float32)
-        packed[part] = values
+        values = moved_ref[part].astype(jnp.float32)
         total += jnp.sum(values * values, axis=1, keepdims=True)
     inverse_rms = lax.rsqrt(total * (1.0 / (parts * features)) + EPSILON)
-    half = rows // 2
-    taken = jnp.sum(packer.astype(jnp.float32), axis=1, keepdims=True)
-    first_column = lax.broadcasted_iota(jnp.int32, (rows, features), 1) == 0
     for part in range(parts):
         columns = slice(part * features, (part + 1) * features)
-        normed = packed[part] * inverse_rms * gain_ref[:, columns]
-        if part == 0:
-            normed = jnp.where(first_column & (taken == 0.0), EMPTY, normed)
-        normed = normed.astype(jnp.bfloat16)
-        top_ref[:, columns] = normed[:half]
-        low_ref[:, columns] = normed[half:]
+        values = moved_ref[part].astype(jnp.float32)
+        out_ref[:, columns] = (values * inverse_rms * gain_ref[:, columns]).astype(jnp.bfloat16)
+    slot = slot_ref[...].astype(jnp.float32)
+    out_ref[:, parts * features :] = jnp.broadcast_to(slot, (rows, SLOT_LANES)).astype(jnp.bfloat16)
 
 
 def norm_rows(moved, slot, teacher_gain):
     parts, rows, features = moved.shape
-    half = jax.ShapeDtypeStruct((rows // 2, parts * features), jnp.bfloat16)
     return pl.pallas_call(
         norm_kernel,
-        out_shape=(half, half),
-        scratch_shapes=[pltpu.VMEM((parts, rows, features), jnp.float32)],
+        out_shape=jax.ShapeDtypeStruct((rows, parts * features + SLOT_LANES), jnp.bfloat16),
         compiler_params=pltpu.CompilerParams(vmem_limit_bytes=16 * MIB),
         cost_estimate=pl.CostEstimate(
-            flops=2 * rows * rows * parts * features,
+            flops=4 * rows * parts * features,
             bytes_accessed=4 * rows * parts * features,
             transcendentals=rows,
         ),
-    )(moved, slot[None, :], teacher_gain[None, :])
-
-
-def block_product(sources, weight_source, rows_buffer, weights, total, row_sems, weight_sems):
+    )(moved, slot[:, None], teacher_gain[None, :])
+
+
+def block_product(
+    sources, weight_source, rows_buffer, slots, weights, total, row_sems, slot_sems, weight_sems
+):
     steps = weight_sems.shape[0]
     y_count, shares, half, tile = weights.shape
     spans = y_count // steps
@@ -75,6 +68,15 @@
             pltpu.make_async_copy(weight_source.at[blocks], weights.at[blocks], weight_sems.at[step])
         )
         copies.append(chunk)
+    depth = rows_buffer.shape[1]
+    copies[-1] += [
+        pltpu.make_async_copy(
+            source.at[:, pl.ds(depth, SLOT_LANES)],
+            slots.at[pl.ds(i * height, height)],
+            slot_sems.at[i],
+        )
+        for i, source in enumerate(sources)
+    ]
     for chunk in copies:
         for copy in chunk:
             copy.start()
@@ -98,29 +100,40 @@
             total[...] += partial
 
 
-def turned(shards, total, rows_buffer):
+def turned(shards, total, slots):
     rows = total.shape[0]
+    capacity = SLOT_LANES // shards
+    block = SLOT_LANES
+    source = lax.broadcasted_iota(jnp.int32, (rows, rows), 0)
+    to = lax.broadcasted_iota(jnp.int32, (rows, rows), 1)
     depth = rows // shards
-    to = lax.broadcasted_iota(jnp.int32, (rows, rows), 0)
-    source = lax.broadcasted_iota(jnp.int32, (rows, rows), 1)
-    turn = (source == (to % depth) * shards + to // depth).astype(jnp.bfloat16)
-    empty = rows_buffer[:, :128].astype(jnp.float32)[:, 0:1] > EMPTY_FROM
-    kept = jnp.where(empty, EMPTY, total[...]).astype(jnp.bfloat16)
-    return jnp.dot(turn, kept, preferred_element_type=jnp.float32).astype(jnp.bfloat16)
+    wanted = (to % capacity) * shards + to // depth
+    here = (to // capacity) % (depth // capacity) == source // block
+    slot = slots[...].astype(jnp.float32)[:, 0:1]
+    chosen = (here & (slot == wanted.astype(jnp.float32))).astype(jnp.bfloat16)
+
+    def gathered(values):
+        return lax.dot_general(
+            chosen, values, (((0,), (0,)), ((), ())), preferred_element_type=jnp.float32
+        )
+
+    held = gathered(jnp.ones((rows, SLOT_LANES), jnp.bfloat16))[:, 0:1]
+    placed = gathered(total[...].astype(jnp.bfloat16))
+    return jnp.where(held > 0.5, placed, EMPTY).astype(jnp.bfloat16)
 
 
 def first_kernel(shards, count, *refs):
-    out_ref, rows_buffer, weights, total, row_sems, weight_sems = refs[count + 1 :]
-    block_product(refs[:count], refs[count], rows_buffer, weights, total, row_sems, weight_sems)
-    out_ref[...] = turned(shards, total, rows_buffer)
+    out_ref, rows_buffer, slots, weights, total, *sems = refs[count + 1 :]
+    block_product(refs[:count], refs[count], rows_buffer, slots, weights, total, *sems)
+    out_ref[...] = turned(shards, total, slots)
 
 
 def second_kernel(shards, count, core_ref, first_ref, *refs):
-    out_ref, rows_buffer, weights, total, row_sems, weight_sems = refs[count + 1 :]
-    block_product(refs[:count], refs[count], rows_buffer, weights, total, row_sems, weight_sems)
+    out_ref, rows_buffer, slots, weights, total, *sems = refs[count + 1 :]
+    block_product(refs[:count], refs[count], rows_buffer, slots, weights, total, *sems)
     width = total.shape[1]
     mine = first_ref[...]
-    other = turned(shards, total, rows_buffer)
+    other = turned(shards, total, slots)
 
     @pl.when(core_ref[0] == 0)
     def _():
@@ -153,9 +166,11 @@
         out_specs=in_vmem,
         scratch_shapes=[
             pltpu.VMEM((total_rows, depth), jnp.bfloat16),
+            pltpu.VMEM((total_rows, SLOT_LANES), jnp.bfloat16),
             pltpu.VMEM(weights.shape, jnp.bfloat16),
             pltpu.VMEM((total_rows, width), jnp.float32),
             pltpu.SemaphoreType.DMA((count, steps)),
+            pltpu.SemaphoreType.DMA((count,)),
             pltpu.SemaphoreType.DMA((steps,)),
         ],
         compiler_params=pltpu.CompilerParams(vmem_limit_bytes=56 * MIB),
@@ -250,19 +265,13 @@
     )(received, hidden, gains[None, :])
 
 
-def ring_gather(top, low, x_count, dp_count):
+def ring_moves(x_count, dp_count):
     forward = [(d, d - d % x_count + (d + 1) % x_count) for d in range(dp_count)]
     backward = [(d, d - d % x_count + (d - 1) % x_count) for d in range(dp_count)]
-    left_top = lax.ppermute(top, "dp", forward)
-    right_low = lax.ppermute(low, "dp", backward)
-    left_low = lax.ppermute(low, "dp", forward)
-    right_top = lax.ppermute(top, "dp", backward)
-    far_top = lax.ppermute(left_top, "dp", forward)
-    far_low = lax.ppermute(right_low, "dp", backward)
-    return [top, low, left_top, left_low, far_top, far_low, right_top, right_low]
-
-
-def projector_columns(projector, student_gain, mp_count, x_count, y_count):
+    return forward, backward
+
+
+def projector_columns(projector, student_gain, after, mp_count, x_count, y_count):
     core = lax.axis_index("group")
     dp_count = x_count * y_count
     columns = projector.T
@@ -286,6 +295,7 @@
         [high, middle, low, jnp.zeros((extra * tile - 3 * width,), jnp.float32)]
     ).astype(jnp.bfloat16)
     message = jnp.concatenate([piece, parts.reshape(extra, tile)], axis=0)
+    message, _ = lax.optimization_barrier((message, after))
     spread = lax.all_to_all(
         jnp.broadcast_to(message[None], (mp_count,) + message.shape), "mp", 0, 0, tiled=True
     )
@@ -294,7 +304,7 @@
     tiles = spread[:, :half].reshape(mp_count * half, tile)
     y_groups = [[y * x_count + x for y in range(y_count)] for x in range(x_count)]
     mine = lax.all_gather(tiles, "dp", axis=0, axis_index_groups=y_groups, tiled=True)
-    return mine.reshape(y_count, mp_count, half, tile), gains.reshape(mp_count * width)
+    return mine.reshape(y_count, mp_count, half, tile), gains.reshape(mp_count * width), spread
 
 
 def local(teacher_hidden, teacher_gain, projector, live, placement, student_hidden, student_gain):
@@ -312,8 +322,14 @@
 
     features = teacher_hidden.shape[1]
     blocks = teacher_hidden.reshape(mp_count, slot_count, features)
-    moved = lax.all_to_all(blocks, "mp", 0, 0, tiled=True)
-    mine, gains = projector_columns(projector, student_gain, mp_count, x_count, y_count)
+    half = slot_count // 2
+    top_rows, low_rows = blocks[:, :half], blocks[:, half:]
+    moved_top = lax.all_to_all(top_rows, "mp", 0, 0, tiled=True)
+    mine, gains, spread = projector_columns(
+        projector, student_gain, moved_top, mp_count, x_count, y_count
+    )
+    moved_top, low_rows, _ = lax.optimization_barrier((moved_top, low_rows, spread))
+    moved_low = lax.all_to_all(low_rows, "mp", 0, 0, tiled=True)
 
     own_live = lax.dynamic_index_in_dim(live.reshape(mp_count, slot_count), column, 0, keepdims=False)
     own_shards = lax.dynamic_index_in_dim(placement.reshape(mp_count, slot_count), column, 0, keepdims=False)
@@ -326,8 +342,17 @@
     rank = jnp.sum(same.astype(jnp.int32), axis=0)
     slot = jnp.where(own_live == 1, rank * dp_count + own_shards, -1)
 
-    top, low = norm_rows(moved, slot, teacher_gain)
-    pieces = ring_gather(top, low, x_count, dp_count)
+    top = norm_rows(moved_top, slot[:half], teacher_gain)
+    forward, backward = ring_moves(x_count, dp_count)
+    left_top = lax.ppermute(top, "dp", forward)
+    right_top = lax.ppermute(top, "dp", backward)
+    far_top = lax.ppermute(left_top, "dp", forward)
+    moved_low, left_top, right_top = lax.optimization_barrier((moved_low, left_top, right_top))
+    low = norm_rows(moved_low, slot[half:], teacher_gain)
+    left_low = lax.ppermute(low, "dp", forward)
+    right_low = lax.ppermute(low, "dp", backward)
+    far_low = lax.ppermute(right_low, "dp", backward)
+    pieces = [top, low, left_top, left_low, far_top, far_low, right_top, right_low]
     mine, pieces = lax.optimization_barrier((mine, pieces))
     other = lax.ppermute(mine, "group", [(0, 1), (1, 0)])
     first = product(pieces, mine, dp_count)

time: 215 us -> 220 us (1.023)
  starting transfers between devices: 43.1 us -> 53.3 us
  blocking collectives: 56.8 us -> 51.5 us
    all_to_all x1 -> x2, waiting for transfers between devices: 23.8 us -> 4.27 us  [the longest x1 4.26 us: local(): moved_top = lax.all_to_all(top_rows, 'mp', 0, 0, tiled=True)]
    all_to_all x1 -> x2, starting transfers between devices: 3.57 us -> 14.4 us  [the longest x1 10.9 us: local(): moved_top = lax.all_to_all(top_rows, 'mp', 0, 0, tiled=True)]
    ppermute x6, waiting for transfers between devices: 18.5 us -> 28.6 us  [the longest x1 11.2 us: local(): left_low = lax.ppermute(low, 'dp', forward)]
    all_to_all x1, blocking collectives: 28.9 us -> 20 us  [projector_columns(): lax.all_to_all(jnp.broadcast_to(message[None], (mp_count,) + message.shap...]
    ppermute x1, waiting for transfers between devices: 1.06 us -> 8.37 us  [projector_columns(): piece = lax.ppermute(share, ('group', 'dp', 'mp'), moves)]
    ppermute x6, starting transfers between devices: 18.3 us -> 21.6 us  [the longest x1 5.99 us: local(): left_top = lax.ppermute(top, 'dp', forward)]
    all_to_all x1, blocking collectives: 8.97 us -> 12.3 us  [local(): lax.all_to_all(message, 'mp', 0, 0, tiled=True)]
    slice x0 -> x1, local copies, waits for them, and re-layouts: none -> 2.32 us  [local(): top_rows, low_rows = (blocks[:, :half], blocks[:, half:])]
  transfers between devices with their start and end apart: 11 -> 12, of which waited for: 7 -> 7; matrix products, arithmetic and copies ran while one was open for 2% -> 2% of each run, Pallas kernels for 4% -> 4%
where the time goes in v3:
time: 220 us; the launch traced here: 219 us
  waiting for transfers between devices  64.9 us (30%)
  starting transfers between devices  53.3 us (24%)
  blocking collectives  51.5 us (23%)
  Pallas kernels  19.6 us (9%)
  between operations  16.8 us (8%)
  local copies, waits for them, and re-layouts  8.63 us (4%)
  other arithmetic  4.49 us (2%)
    all_to_all x1, waiting for transfers between devices, local(): lax.all_to_all(buffer.reshape(dp_count, deep, quarter), 'dp', 0, 0, tiled...  23.6 us
    all_to_all x1, blocking collectives, projector_columns(): lax.all_to_all(jnp.broadcast_to(message[None], (mp_count,) + message.shap...  20 us
    all_to_all x1, blocking collectives, local(): lax.all_to_all(jnp.broadcast_to(over_mp[None, :], (peers, over_mp.shape[0...  19.1 us
    pallas_call x2, Pallas kernels, product(): pl.pallas_call(functools.partial(kernel, shards, count), out_shape=jax.Sh...  15.6 us
    all_to_all x1, blocking collectives, local(): lax.all_to_all(message, 'mp', 0, 0, tiled=True)  12.3 us
    ppermute x1, waiting for transfers between devices, local(): left_low = lax.ppermute(low, 'dp', forward)  11.2 us
    all_to_all x1, starting transfers between devices, local(): moved_top = lax.all_to_all(top_rows, 'mp', 0, 0, tiled=True)  10.9 us
    ppermute x1, waiting for transfers between devices, local(): right_top = lax.ppermute(top, 'dp', backward)  10.4 us
  transfers between devices with their start and end apart: 12, of which 7 were waited for; matrix products, arithmetic and copies ran while one was open for 2% of the time, Pallas kernels for 4%

profile of v3, /device:TPU:1, one launch (start us, length us, event | category | flops | bytes accessed | tf_op | source)
XLA Modules:
  0.0 219.1 jit_solution(14327417142938197907)
XLA Ops:
  7.2 2.3 %fusion.3 = (bf16[8,64,512]{2,1,0:T(8,128)(2,1)}, bf16[8,64,512]{2,1,0:T(8,128)(2,1)}) fusion(bf16[8,128,512]{2,1,0:T(8,128)(2,1)} %bitcast.38), kind=kLoop, calls=%fused_computation.22 | loop fusion | bytes 2097152 | tf_op jit(solution)/shard_map/slice | solution.py:326
  9.5 10.9 %all-to-all-start = ((bf16[8,64,512]{2,1,0:T(8,128)(2,1)}), bf16[8,64,512]{2,1,0:T(8,128)(2,1)S(1)}, u32[]{:S(2)}, u32[]{:S(2)}) async-start(bf16[8,64,512]{2,1,0:T(8,128)(2,1)} %get-tuple-element.38), calls=%async_computation | async-start | bytes 1048576 | tf_op jit(solution)/shard_map/all_to_all | solution.py:327
  20.5 4.4 %collective-permute-start = (bf16[224,128]{1,0:T(8,128)(2,1)S(1)}, bf16[224,128]{1,0:T(8,128)(2,1)S(1)}, u32[]{:S(2)}, u32[]{:S(2)}) collective-permute-start(bf16[224,128]{1,0:T(8,128)(2,1)S(1)} %dynamic-slice_bitcast_fusion), channel_id=1, source_target_pairs={{0,0},{1,256},{2,8},{3,264},{4,16},{5,272},{6,24},{7,280},{8,2},{9... | collective-permute-start | bytes 172040 | tf_op jit(solution)/shard_map/ppermute | solution.py:288
  25.7 8.4 %collective-permute-done = bf16[224,128]{1,0:T(8,128)(2,1)S(1)} collective-permute-done((bf16[224,128]{1,0:T(8,128)(2,1)S(1)}, bf16[224,128]{1,0:T(8,128)(2,1)S(1)}, u32[]{:S(2)}, u32[]{:S(2)}) %collective-permute-start) | collective-permute-done | bytes 57376 | tf_op jit(solution)/shard_map/ppermute | solution.py:288
  34.1 4.3 %all-to-all-done.moved_ref = bf16[8,64,512]{2,1,0:T(8,128)(2,1)S(1)} async-done(((bf16[8,64,512]{2,1,0:T(8,128)(2,1)}), bf16[8,64,512]{2,1,0:T(8,128)(2,1)S(1)}, u32[]{:S(2)}, u32[]{:S(2)}) %all-to-all-start) | async-done | bytes 524320 | tf_op jit(solution)/shard_map/all_to_all | solution.py:327
  38.4 20.0 %all_to_all.31 = bf16[8,240,128]{2,1,0:T(8,128)(2,1)S(1)} all-to-all(bf16[8,240,128]{2,1,0:T(8,128)(2,1)S(1)} %broadcast_in_dim.17), channel_id=1, replica_groups=mesh['group'=2,'dp'=32,'mp'=8] {'mp'}, dimensions={0} | all-to-all | bytes 983040 | tf_op jit(solution)/shard_map/all_to_all | solution.py:299
  61.6 3.5 %all-to-all-start.2 = ((bf16[8,64,512]{2,1,0:T(8,128)(2,1)}), bf16[8,64,512]{2,1,0:T(8,128)(2,1)S(1)}, u32[]{:S(2)}, u32[]{:S(2)}) async-start(bf16[8,64,512]{2,1,0:T(8,128)(2,1)} %get-tuple-element.22), calls=%async_computation.2 | async-start | bytes 1048576 | tf_op jit(solution)/shard_map/all_to_all | solution.py:332
  66.4 2.1 collective-permute-start.2
  68.5 6.0 %collective-permute-start.1 = (bf16[64,4224]{1,0:T(8,128)(2,1)S(1)}, bf16[64,4224]{1,0:T(8,128)(2,1)S(1)}, u32[]{:S(2)}, u32[]{:S(2)}) collective-permute-start(bf16[64,4224]{1,0:T(8,128)(2,1)S(1)} %shard_map.94.refs_0_), channel_id=1, source_target_pairs={{0,8},{8,16},{16,24},{24,0},{32,40},{40,48},{48,56},{56,32},{64,72... | collective-permute-start | bytes 1622024 | tf_op jit(solution)/shard_map/ppermute | solution.py:347
  74.6 10.4 %collective-permute-done.2.refs_6_ = bf16[64,4224]{1,0:T(8,128)(2,1)S(1)} collective-permute-done((bf16[64,4224]{1,0:T(8,128)(2,1)S(1)}, bf16[64,4224]{1,0:T(8,128)(2,1)S(1)}, u32[]{:S(2)}, u32[]{:S(2)}) %collective-permute-start.2) | collective-permute-done | bytes 540704 | tf_op jit(solution)/shard_map/ppermute | solution.py:348
  86.1 4.4 %collective-permute-start.5 = (bf16[64,4224]{1,0:T(8,128)(2,1)S(1)}, bf16[64,4224]{1,0:T(8,128)(2,1)S(1)}, u32[]{:S(2)}, u32[]{:S(2)}) collective-permute-start(bf16[64,4224]{1,0:T(8,128)(2,1)S(1)} %shard_map.95.refs_1_), channel_id=1, source_target_pairs={{0,24},{8,0},{16,8},{24,16},{32,56},{40,32},{48,40},{56,48},{64,88... | collective-permute-start | bytes 1622024 | tf_op jit(solution)/shard_map/ppermute | solution.py:353
  90.5 1.9 collective-permute-start.4
  92.4 3.2 %collective-permute-start.3 = (bf16[64,4224]{1,0:T(8,128)(2,1)S(1)}, bf16[64,4224]{1,0:T(8,128)(2,1)S(1)}, u32[]{:S(2)}, u32[]{:S(2)}) collective-permute-start(bf16[64,4224]{1,0:T(8,128)(2,1)S(1)} %shard_map.95.refs_1_), channel_id=1, source_target_pairs={{0,8},{8,16},{16,24},{24,0},{32,40},{40,48},{48,56},{56,32},{64,72... | collective-permute-start | bytes 1622024 | tf_op jit(solution)/shard_map/ppermute | solution.py:352
  95.6 6.3 %collective-permute-done.5.refs_7_ = bf16[64,4224]{1,0:T(8,128)(2,1)S(1)} collective-permute-done((bf16[64,4224]{1,0:T(8,128)(2,1)S(1)}, bf16[64,4224]{1,0:T(8,128)(2,1)S(1)}, u32[]{:S(2)}, u32[]{:S(2)}) %collective-permute-start.5) | collective-permute-done | bytes 540704 | tf_op jit(solution)/shard_map/ppermute | solution.py:353
  101.9 4.0 %collective-permute-start.6 = (bf16[64,4224]{1,0:T(8,128)(2,1)S(1)}, bf16[64,4224]{1,0:T(8,128)(2,1)}, u32[]{:S(2)}, u32[]{:S(2)}) collective-permute-start(bf16[64,4224]{1,0:T(8,128)(2,1)S(1)} %collective-permute-done.5.refs_7_), channel_id=1, source_target_pairs={{0,24},{8,0},{16,8},{24,16},{32,56},{40,32},{48,40},{56,48},{64,88... | collective-permute-start | bytes 1622024 | tf_op jit(solution)/shard_map/ppermute | solution.py:354
  105.9 11.2 %collective-permute-done.3.refs_3_ = bf16[64,4224]{1,0:T(8,128)(2,1)S(1)} collective-permute-done((bf16[64,4224]{1,0:T(8,128)(2,1)S(1)}, bf16[64,4224]{1,0:T(8,128)(2,1)S(1)}, u32[]{:S(2)}, u32[]{:S(2)}) %collective-permute-start.3) | collective-permute-done | bytes 540704 | tf_op jit(solution)/shard_map/ppermute | solution.py:352
  118.0 4.6 %collective-permute-start.7 = (bf16[8,8,224,128]{3,2,1,0:T(8,128)(2,1)}, bf16[8,8,224,128]{3,2,1,0:T(8,128)(2,1)S(1)}, u32[]{:S(2)}, u32[]{:S(2)}) collective-permute-start(bf16[8,8,224,128]{3,2,1,0:T(8,128)(2,1)} %bitcast.35), channel_id=1, source_target_pairs={{0,256},{256,0},{1,257},{257,1},{2,258},{258,2},{3,259},{259,3},{4... | collective-permute-start | bytes 11010056 | tf_op jit(solution)/shard_map/ppermute | solution.py:357
  122.7 7.1 %shard_map.96.first_ref = bf16[512,448]{1,0:T(8,128)(2,1)} custom-call(bf16[64,4224]{1,0:T(8,128)(2,1)} %copy-done.1, bf16[64,4224]{1,0:T(8,128)(2,1)} %copy-done.2, bf16[64,4224]{1,0:T(8,128)(2,1)} %copy-done.7, bf16[64,4224]{1,0:T(8,128)(2,1)} %copy-done.10, bf16[64,4224]{1,0:T(8,128)(2,1)} %copy-done.9, bf16[64,4224]{1,0:T(8,128)(2,1)} %collective-permute-done.6.refs_5_, ...), custom_call_target="tpu_custom_call" | custom-call | flops 1879048192 | bytes 7864320 | tf_op jit(solution)/shard_map/pallas_call | solution.py:160
  131.6 8.5 %shard_map.97 = bf16[512,896]{1,0:T(8,128)(2,1)} custom-call(s32[1]{0:T(128)} %bitcast.core_ref, bf16[512,448]{1,0:T(8,128)(2,1)} %shard_map.96.first_ref, bf16[64,4224]{1,0:T(8,128)(2,1)} %copy-done.1, bf16[64,4224]{1,0:T(8,128)(2,1)} %copy-done.2, bf16[64,4224]{1,0:T(8,128)(2,1)} %copy-done.7, bf16[64,4224]{1,0:T(8,128)(2,1)} %copy-done.10, ...), custom_call_target="tpu_custom_call" | custom-call | flops 1879048192 | bytes 7864320 | tf_op jit(solution)/shard_map/pallas_call | solution.py:160
  140.1 8.1 %all-to-all-start.3 = ((bf16[32,16,896]{2,1,0:T(8,128)(2,1)}), bf16[32,16,896]{2,1,0:T(8,128)(2,1)S(1)}, u32[]{:S(2)}, u32[]{:S(2)}) async-start(bf16[32,16,896]{2,1,0:T(8,128)(2,1)} %bitcast.34), calls=%async_computation.3 | async-start | bytes 1835008 | tf_op jit(solution)/shard_map/all_to_all | solution.py:362
  149.2 23.6 %all-to-all-done.3 = bf16[32,16,896]{2,1,0:T(8,128)(2,1)S(1)} async-done(((bf16[32,16,896]{2,1,0:T(8,128)(2,1)}), bf16[32,16,896]{2,1,0:T(8,128)(2,1)S(1)}, u32[]{:S(2)}, u32[]{:S(2)}) %all-to-all-start.3) | async-done | bytes 917536 | tf_op jit(solution)/shard_map/all_to_all | solution.py:362
  172.8 3.3 %shard_map.98 = (bf16[128,3584]{1,0:T(8,128)(2,1)}, f32[8,1,512]{2,1,0:T(1,128)S(1)}) custom-call(bf16[8,4,16,896]{3,2,1,0:T(8,128)(2,1)S(1)} %bitcast.31, bf16[128,3584]{1,0:T(8,128)(2,1)S(1)} %copy-done.3, f32[1,3584]{1,0:T(1,128)S(1)} %broadcast_in_dim_reshape.3.gain_ref), custom_call_target="tpu_custom_call" | custom-call | flops 117440512 | bytes 2752512 | tf_op jit(solution)/shard_map/pallas_call | solution.py:249
  176.2 12.3 %all_to_all.32 = f32[8,1,512]{2,1,0:T(1,128)S(1)} all-to-all(f32[8,1,512]{2,1,0:T(1,128)S(1)} %get-tuple-element.36), channel_id=1, replica_groups=mesh['group'=2,'dp'=32,'mp'=8] {'mp'}, dimensions={0} | all-to-all | bytes 32768 | tf_op jit(solution)/shard_map/all_to_all | solution.py:367
  188.6 19.1 %all_to_all.33 = f32[64,1,512]{2,1,0:T(1,128)S(1)} all-to-all(f32[64,1,512]{2,1,0:T(1,128)S(1)} %broadcast_in_dim.40), channel_id=1, replica_groups=mesh['group'=2,'dp'=32,'mp'=8] {'group','dp'}, dimensions={0} | all-to-all | bytes 262144 | tf_op jit(solution)/shard_map/all_to_all | solution.py:370
  (57 shorter events, 12.3 us)
Async XLA Ops:
  7.2 13.3 %copy-start = (bf16[128,448]{0,1:T(8,128)(2,1)S(1)}, bf16[128,448]{0,1:T(8,128)(2,1)}, u32[]{:S(2)}) copy-start(bf16[128,448]{0,1:T(8,128)(2,1)} %param.9) | copy-start | bytes 344068
  7.2 58.9 %copy-start.4 = (f32[4096]{0:T(1024)S(1)}, f32[4096]{0:T(1024)}, u32[]{:S(2)}) copy-start(f32[4096]{0:T(1024)} %param.8) | copy-start | bytes 49156
  9.5 28.8 %all-to-all-start = ((bf16[8,64,512]{2,1,0:T(8,128)(2,1)}), bf16[8,64,512]{2,1,0:T(8,128)(2,1)S(1)}, u32[]{:S(2)}, u32[]{:S(2)}) async-start(bf16[8,64,512]{2,1,0:T(8,128)(2,1)} %get-tuple-element.38), calls=%async_computation | async-start | bytes 1048576 | tf_op jit(solution)/shard_map/all_to_all | solution.py:327
  20.4 97.6 %all-gather.2.cloned.1.call-start = ((), (), s32[]{:S(2)}) async-start(), calls=%async_computation.6 | async-start | bytes 4128768 | tf_op jit(solution)/shard_map/all_gather | solution.py:306
  20.5 13.6 %collective-permute-start = (bf16[224,128]{1,0:T(8,128)(2,1)S(1)}, bf16[224,128]{1,0:T(8,128)(2,1)S(1)}, u32[]{:S(2)}, u32[]{:S(2)}) collective-permute-start(bf16[224,128]{1,0:T(8,128)(2,1)S(1)} %dynamic-slice_bitcast_fusion), channel_id=1, source_target_pairs={{0,0},{1,256},{2,8},{3,264},{4,16},{5,272},{6,24},{7,280},{8,2},{9... | collective-permute-start | bytes 172040 | tf_op jit(solution)/shard_map/ppermute | solution.py:288
  58.4 0.8 copy-start.11
  61.6 24.1 %all-to-all-start.2 = ((bf16[8,64,512]{2,1,0:T(8,128)(2,1)}), bf16[8,64,512]{2,1,0:T(8,128)(2,1)S(1)}, u32[]{:S(2)}, u32[]{:S(2)}) async-start(bf16[8,64,512]{2,1,0:T(8,128)(2,1)} %get-tuple-element.22), calls=%async_computation.2 | async-start | bytes 1048576 | tf_op jit(solution)/shard_map/all_to_all | solution.py:332
  66.4 56.3 %copy-start.1 = (bf16[64,4224]{1,0:T(8,128)(2,1)}, bf16[64,4224]{1,0:T(8,128)(2,1)S(1)}, u32[]{:S(2)}) copy-start(bf16[64,4224]{1,0:T(8,128)(2,1)S(1)} %shard_map.94.refs_0_) | copy-start | bytes 1622020
  66.4 18.6 %collective-permute-start.2 = (bf16[64,4224]{1,0:T(8,128)(2,1)S(1)}, bf16[64,4224]{1,0:T(8,128)(2,1)S(1)}, u32[]{:S(2)}, u32[]{:S(2)}) collective-permute-start(bf16[64,4224]{1,0:T(8,128)(2,1)S(1)} %shard_map.94.refs_0_), channel_id=1, source_target_pairs={{0,24},{8,0},{16,8},{24,16},{32,56},{40,32},{48,40},{56,48},{64,88... | collective-permute-start | bytes 1622024 | tf_op jit(solution)/shard_map/ppermute | solution.py:348
  68.5 17.2 %collective-permute-start.1 = (bf16[64,4224]{1,0:T(8,128)(2,1)S(1)}, bf16[64,4224]{1,0:T(8,128)(2,1)S(1)}, u32[]{:S(2)}, u32[]{:S(2)}) collective-permute-start(bf16[64,4224]{1,0:T(8,128)(2,1)S(1)} %shard_map.94.refs_0_), channel_id=1, source_target_pairs={{0,8},{8,16},{16,24},{24,0},{32,40},{40,48},{48,56},{56,32},{64,72... | collective-permute-start | bytes 1622024 | tf_op jit(solution)/shard_map/ppermute | solution.py:347
  85.0 37.6 %copy-start.6 = (bf16[64,4224]{1,0:T(8,128)(2,1)}, bf16[64,4224]{1,0:T(8,128)(2,1)S(1)}, u32[]{:S(2)}) copy-start(bf16[64,4224]{1,0:T(8,128)(2,1)S(1)} %collective-permute-done.2.refs_6_) | copy-start | bytes 1622020
  85.7 36.9 %copy-start.7 = (bf16[64,4224]{1,0:T(8,128)(2,1)}, bf16[64,4224]{1,0:T(8,128)(2,1)S(1)}, u32[]{:S(2)}) copy-start(bf16[64,4224]{1,0:T(8,128)(2,1)S(1)} %collective-permute-done.1.refs_2_) | copy-start | bytes 1622020
  86.1 36.6 %copy-start.2 = (bf16[64,4224]{1,0:T(8,128)(2,1)}, bf16[64,4224]{1,0:T(8,128)(2,1)S(1)}, u32[]{:S(2)}) copy-start(bf16[64,4224]{1,0:T(8,128)(2,1)S(1)} %shard_map.95.refs_1_) | copy-start | bytes 1622020
  86.1 15.8 %collective-permute-start.5 = (bf16[64,4224]{1,0:T(8,128)(2,1)S(1)}, bf16[64,4224]{1,0:T(8,128)(2,1)S(1)}, u32[]{:S(2)}, u32[]{:S(2)}) collective-permute-start(bf16[64,4224]{1,0:T(8,128)(2,1)S(1)} %shard_map.95.refs_1_), channel_id=1, source_target_pairs={{0,24},{8,0},{16,8},{24,16},{32,56},{40,32},{48,40},{56,48},{64,88... | collective-permute-start | bytes 1622024 | tf_op jit(solution)/shard_map/ppermute | solution.py:353
  90.5 15.4 %collective-permute-start.4 = (bf16[64,4224]{1,0:T(8,128)(2,1)S(1)}, bf16[64,4224]{1,0:T(8,128)(2,1)S(1)}, u32[]{:S(2)}, u32[]{:S(2)}) collective-permute-start(bf16[64,4224]{1,0:T(8,128)(2,1)S(1)} %collective-permute-done.1.refs_2_), channel_id=1, source_target_pairs={{0,8},{8,16},{16,24},{24,0},{32,40},{40,48},{48,56},{56,32},{64,72... | collective-permute-start | bytes 1622024 | tf_op jit(solution)/shard_map/ppermute | solution.py:349
  92.4 24.7 %collective-permute-start.3 = (bf16[64,4224]{1,0:T(8,128)(2,1)S(1)}, bf16[64,4224]{1,0:T(8,128)(2,1)S(1)}, u32[]{:S(2)}, u32[]{:S(2)}) collective-permute-start(bf16[64,4224]{1,0:T(8,128)(2,1)S(1)} %shard_map.95.refs_1_), channel_id=1, source_target_pairs={{0,8},{8,16},{16,24},{24,0},{32,40},{40,48},{48,56},{56,32},{64,72... | collective-permute-start | bytes 1622024 | tf_op jit(solution)/shard_map/ppermute | solution.py:352
  101.9 20.8 %copy-start.8 = (bf16[64,4224]{1,0:T(8,128)(2,1)}, bf16[64,4224]{1,0:T(8,128)(2,1)S(1)}, u32[]{:S(2)}) copy-start(bf16[64,4224]{1,0:T(8,128)(2,1)S(1)} %collective-permute-done.5.refs_7_) | copy-start | bytes 1622020
  101.9 16.1 %collective-permute-start.6 = (bf16[64,4224]{1,0:T(8,128)(2,1)S(1)}, bf16[64,4224]{1,0:T(8,128)(2,1)}, u32[]{:S(2)}, u32[]{:S(2)}) collective-permute-start(bf16[64,4224]{1,0:T(8,128)(2,1)S(1)} %collective-permute-done.5.refs_7_), channel_id=1, source_target_pairs={{0,24},{8,0},{16,8},{24,16},{32,56},{40,32},{48,40},{56,48},{64,88... | collective-permute-start | bytes 1622024 | tf_op jit(solution)/shard_map/ppermute | solution.py:354
  105.9 11.2 %copy-start.9 = (bf16[64,4224]{1,0:T(8,128)(2,1)}, bf16[64,4224]{1,0:T(8,128)(2,1)S(1)}, u32[]{:S(2)}) copy-start(bf16[64,4224]{1,0:T(8,128)(2,1)S(1)} %collective-permute-done.4.refs_4_) | copy-start | bytes 1622020
  117.1 0.8 copy-start.10
  118.0 11.8 %collective-permute-start.7 = (bf16[8,8,224,128]{3,2,1,0:T(8,128)(2,1)}, bf16[8,8,224,128]{3,2,1,0:T(8,128)(2,1)S(1)}, u32[]{:S(2)}, u32[]{:S(2)}) collective-permute-start(bf16[8,8,224,128]{3,2,1,0:T(8,128)(2,1)} %bitcast.35), channel_id=1, source_target_pairs={{0,256},{256,0},{1,257},{257,1},{2,258},{258,2},{3,259},{259,3},{4... | collective-permute-start | bytes 11010056 | tf_op jit(solution)/shard_map/ppermute | solution.py:357
  129.8 1.8 copy-start.5
  131.6 41.3 %copy-start.3 = (bf16[128,3584]{1,0:T(8,128)(2,1)S(1)}, bf16[128,3584]{1,0:T(8,128)(2,1)}, u32[]{:S(2)}) copy-start(bf16[128,3584]{1,0:T(8,128)(2,1)} %hidden_ref.1) | copy-start | bytes 2752516
  140.1 32.8 %all-to-all-start.3 = ((bf16[32,16,896]{2,1,0:T(8,128)(2,1)}), bf16[32,16,896]{2,1,0:T(8,128)(2,1)S(1)}, u32[]{:S(2)}, u32[]{:S(2)}) async-start(bf16[32,16,896]{2,1,0:T(8,128)(2,1)} %bitcast.34), calls=%async_computation.3 | async-start | bytes 1835008 | tf_op jit(solution)/shard_map/all_to_all | solution.py:362
Sparse Core Ops, SparseCore 0:
  60.2 50.0 all-gather.1

commit v4 on v2

--- a/solution.py
+++ b/solution.py
@@ -53,7 +53,7 @@
     )(moved, slot[None, :], teacher_gain[None, :])
 
 
-def block_product(sources, weight_source, rows_buffer, weights, total, row_sems, weight_sems):
+def block_product(start, sources, weight_source, rows_buffer, weights, total, row_sems, weight_sems):
     steps = weight_sems.shape[0]
     y_count, shares, half, tile = weights.shape
     spans = y_count // steps
@@ -82,7 +82,10 @@
         for copy in copies[step]:
             copy.wait()
         tiles = [
-            weights[span, 2 * pair : 2 * pair + 2].reshape(2 * half, tile)
+            jnp.concatenate(
+                [weights[span, lax.rem(2 * pair + c + shares - start, shares)] for c in range(2)],
+                axis=0,
+            )
             for span in range(step * spans, (step + 1) * spans)
             for pair in range(shares // 2)
         ]
@@ -109,31 +112,31 @@
     return jnp.dot(turn, kept, preferred_element_type=jnp.float32).astype(jnp.bfloat16)
 
 
-def first_kernel(shards, count, *refs):
+def first_kernel(shards, count, place_ref, *refs):
     out_ref, rows_buffer, weights, total, row_sems, weight_sems = refs[count + 1 :]
-    block_product(refs[:count], refs[count], rows_buffer, weights, total, row_sems, weight_sems)
+    block_product(place_ref[1], refs[:count], refs[count], rows_buffer, weights, total, row_sems, weight_sems)
     out_ref[...] = turned(shards, total, rows_buffer)
 
 
-def second_kernel(shards, count, core_ref, first_ref, *refs):
+def second_kernel(shards, count, place_ref, first_ref, *refs):
     out_ref, rows_buffer, weights, total, row_sems, weight_sems = refs[count + 1 :]
-    block_product(refs[:count], refs[count], rows_buffer, weights, total, row_sems, weight_sems)
+    block_product(place_ref[1], refs[:count], refs[count], rows_buffer, weights, total, row_sems, weight_sems)
     width = total.shape[1]
     mine = first_ref[...]
     other = turned(shards, total, rows_buffer)
 
-    @pl.when(core_ref[0] == 0)
+    @pl.when(place_ref[0] == 0)
     def _():
         out_ref[:, :width] = mine
         out_ref[:, width:] = other
 
-    @pl.when(core_ref[0] != 0)
+    @pl.when(place_ref[0] != 0)
     def _():
         out_ref[:, :width] = other
         out_ref[:, width:] = mine
 
 
-def product(pieces, weights, shards, core=None, first=None):
+def product(place, pieces, weights, shards, first=None):
     y_count, shares, half, tile = weights.shape
     width = 2 * half
     depth = y_count * (shares // 2) * tile
@@ -142,7 +145,7 @@
     steps = 4
     joined = first is not None
     in_vmem = pl.BlockSpec(memory_space=pltpu.VMEM)
-    head = [pl.BlockSpec(memory_space=pltpu.SMEM), in_vmem] if joined else []
+    head = [pl.BlockSpec(memory_space=pltpu.SMEM)] + ([in_vmem] if joined else [])
     kernel = second_kernel if joined else first_kernel
     return pl.pallas_call(
         functools.partial(kernel, shards, count),
@@ -164,7 +167,7 @@
             bytes_accessed=2 * depth * (total_rows + width),
             transcendentals=0,
         ),
-    )(*((core, first) if joined else ()), *pieces, weights)
+    )(place, *((first,) if joined else ()), *pieces, weights)
 
 
 def finish_kernel(
@@ -262,7 +265,7 @@
     return [top, low, left_top, left_low, far_top, far_low, right_top, right_low]
 
 
-def projector_columns(projector, student_gain, mp_count, x_count, y_count):
+def projector_columns(projector, student_gain, after, mp_count, x_count, y_count):
     core = lax.axis_index("group")
     dp_count = x_count * y_count
     columns = projector.T
@@ -285,13 +288,18 @@
     parts = jnp.concatenate(
         [high, middle, low, jnp.zeros((extra * tile - 3 * width,), jnp.float32)]
     ).astype(jnp.bfloat16)
-    message = jnp.concatenate([piece, parts.reshape(extra, tile)], axis=0)
-    spread = lax.all_to_all(
-        jnp.broadcast_to(message[None], (mp_count,) + message.shape), "mp", 0, 0, tiled=True
-    )
-    parts = spread[:, half:].reshape(mp_count, extra * tile).astype(jnp.float32)
+    held = jnp.concatenate([piece, parts.reshape(extra, tile)], axis=0)[None]
+    while held.shape[0] < mp_count:
+        step = held.shape[0]
+        passed = lax.ppermute(held, "mp", [(z, (z - step) % mp_count) for z in range(mp_count)])
+        held = jnp.concatenate([held, passed], axis=0)
+    parts = held[:, half:].reshape(mp_count, extra * tile).astype(jnp.float32)
     gains = parts[:, :width] + parts[:, width : 2 * width] + parts[:, 2 * width : 3 * width]
-    tiles = spread[:, :half].reshape(mp_count * half, tile)
+    gains = lax.dynamic_slice_in_dim(
+        jnp.concatenate([gains, gains], axis=0), mp_count - lax.axis_index("mp"), mp_count, 0
+    )
+    tiles = held[:, :half].reshape(mp_count * half, tile)
+    tiles, _ = lax.optimization_barrier((tiles, after))
     y_groups = [[y * x_count + x for y in range(y_count)] for x in range(x_count)]
     mine = lax.all_gather(tiles, "dp", axis=0, axis_index_groups=y_groups, tiled=True)
     return mine.reshape(y_count, mp_count, half, tile), gains.reshape(mp_count * width)
@@ -313,7 +321,7 @@
     features = teacher_hidden.shape[1]
     blocks = teacher_hidden.reshape(mp_count, slot_count, features)
     moved = lax.all_to_all(blocks, "mp", 0, 0, tiled=True)
-    mine, gains = projector_columns(projector, student_gain, mp_count, x_count, y_count)
+    mine, gains = projector_columns(projector, student_gain, moved, mp_count, x_count, y_count)
 
     own_live = lax.dynamic_index_in_dim(live.reshape(mp_count, slot_count), column, 0, keepdims=False)
     own_shards = lax.dynamic_index_in_dim(placement.reshape(mp_count, slot_count), column, 0, keepdims=False)
@@ -330,8 +338,9 @@
     pieces = ring_gather(top, low, x_count, dp_count)
     mine, pieces = lax.optimization_barrier((mine, pieces))
     other = lax.ppermute(mine, "group", [(0, 1), (1, 0)])
-    first = product(pieces, mine, dp_count)
-    buffer = product(pieces, other, dp_count, core.astype(jnp.int32).reshape(1), first)
+    place = jnp.stack([core, column]).astype(jnp.int32)
+    first = product(place, pieces, mine, dp_count)
+    buffer = product(place, pieces, other, dp_count, first)
     quarter = buffer.shape[1]
     deep = x_count * capacity
     received = lax.all_to_all(

time: 215 us -> 235 us (1.093)
  starting transfers between devices: 43.1 us -> 67.4 us
  blocking collectives: 56.8 us -> 32.7 us
  waiting for transfers between devices: 67 us -> 87.5 us
    all_to_all x1 -> x0, blocking collectives: 28.9 us -> none  [projector_columns(): lax.all_to_all(jnp.broadcast_to(message[None], (mp_count,) + message.shap...]
    all_to_all x1, waiting for transfers between devices: 23.8 us -> 0.01 us  [local(): moved = lax.all_to_all(blocks, 'mp', 0, 0, tiled=True)]
    ppermute x1, waiting for transfers between devices: 1.06 us -> 20.7 us  [projector_columns(): piece = lax.ppermute(share, ('group', 'dp', 'mp'), moves)]
    ppermute x0 -> x3, starting transfers between devices: none -> 17.6 us  [projector_columns(): lax.ppermute(held, 'mp', [(z, (z - step) % mp_count) for z in range(mp_co...]
    all_gather x1, waiting for transfers between devices: 0.01 us -> 12.6 us  [projector_columns(): lax.all_gather(tiles, 'dp', axis=0, axis_index_groups=y_groups, tiled=True)]
    ppermute x0 -> x3, waiting for transfers between devices: none -> 10.8 us  [projector_columns(): lax.ppermute(held, 'mp', [(z, (z - step) % mp_count) for z in range(mp_co...]
    all_to_all x1, starting transfers between devices: 3.57 us -> 11 us  [local(): moved = lax.all_to_all(blocks, 'mp', 0, 0, tiled=True)]
    all_to_all x1, blocking collectives: 8.97 us -> 13.5 us  [local(): lax.all_to_all(message, 'mp', 0, 0, tiled=True)]
  transfers between devices with their start and end apart: 11 -> 14, of which waited for: 7 -> 9; matrix products, arithmetic and copies ran while one was open for 2% -> 2% of each run, Pallas kernels for 4% -> 4%
where the time goes in v4:
time: 235 us; the launch traced here: 234 us
  waiting for transfers between devices  87.5 us (37%)
  starting transfers between devices  67.4 us (29%)
  blocking collectives  32.7 us (14%)
  Pallas kernels  20 us (9%)
  between operations  16.7 us (7%)
  local copies, waits for them, and re-layouts  5.65 us (2%)
  other arithmetic  4.27 us (2%)
    all_to_all x1, waiting for transfers between devices, local(): lax.all_to_all(buffer.reshape(dp_count, deep, quarter), 'dp', 0, 0, tiled...  24.4 us
    ppermute x1, waiting for transfers between devices, projector_columns(): piece = lax.ppermute(share, ('group', 'dp', 'mp'), moves)  20.7 us
    all_to_all x1, blocking collectives, local(): lax.all_to_all(jnp.broadcast_to(over_mp[None, :], (peers, over_mp.shape[0...  19.1 us
    ppermute x3, starting transfers between devices, projector_columns(): lax.ppermute(held, 'mp', [(z, (z - step) % mp_count) for z in range(mp_co...  17.6 us
    pallas_call x2, Pallas kernels, product(): pl.pallas_call(functools.partial(kernel, shards, count), out_shape=jax.Sh...  16 us
    all_to_all x1, blocking collectives, local(): lax.all_to_all(message, 'mp', 0, 0, tiled=True)  13.5 us
    all_gather x1, waiting for transfers between devices, projector_columns(): lax.all_gather(tiles, 'dp', axis=0, axis_index_groups=y_groups, tiled=True)  12.6 us
    all_to_all x1, starting transfers between devices, local(): moved = lax.all_to_all(blocks, 'mp', 0, 0, tiled=True)  11 us
  transfers between devices with their start and end apart: 14, of which 9 were waited for; matrix products, arithmetic and copies ran while one was open for 2% of the time, Pallas kernels for 4%

profile of v4, /device:TPU:1, one launch (start us, length us, event | category | flops | bytes accessed | tf_op | source)
XLA Modules:
  0.0 234.2 jit_solution(4804454552045897955)
XLA Ops:
  7.2 11.0 %all-to-all-start = ((bf16[8,128,512]{2,1,0:T(8,128)(2,1)}), bf16[8,128,512]{2,1,0:T(8,128)(2,1)S(1)}, u32[]{:S(2)}, u32[]{:S(2)}) async-start(bf16[8,128,512]{2,1,0:T(8,128)(2,1)} %bitcast.36), calls=%async_computation | async-start | bytes 2097152 | tf_op jit(solution)/shard_map/all_to_all | solution.py:323
  18.3 4.4 %collective-permute-start = (bf16[224,128]{1,0:T(8,128)(2,1)S(1)}, bf16[224,128]{1,0:T(8,128)(2,1)S(1)}, u32[]{:S(2)}, u32[]{:S(2)}) collective-permute-start(bf16[224,128]{1,0:T(8,128)(2,1)S(1)} %dynamic-slice_bitcast_fusion), channel_id=1, source_target_pairs={{0,0},{1,256},{2,8},{3,264},{4,16},{5,272},{6,24},{7,280},{8,2},{9... | collective-permute-start | bytes 172040 | tf_op jit(solution)/shard_map/ppermute | solution.py:282
  23.5 20.7 %collective-permute-done = bf16[224,128]{1,0:T(8,128)(2,1)S(1)} collective-permute-done((bf16[224,128]{1,0:T(8,128)(2,1)S(1)}, bf16[224,128]{1,0:T(8,128)(2,1)S(1)}, u32[]{:S(2)}, u32[]{:S(2)}) %collective-permute-start) | collective-permute-done | bytes 57376 | tf_op jit(solution)/shard_map/ppermute | solution.py:282
  44.2 6.6 %collective-permute-start.1 = (bf16[1,240,128]{2,1,0:T(8,128)(2,1)S(1)}, bf16[1,240,128]{2,1,0:T(8,128)(2,1)S(1)}, u32[]{:S(2)}, u32[]{:S(2)}) collective-permute-start(bf16[1,240,128]{2,1,0:T(8,128)(2,1)S(1)} %maximum_bitcast_fusion), channel_id=1, source_target_pairs={{0,7},{1,0},{2,1},{3,2},{4,3},{5,4},{6,5},{7,6},{8,15},{9,8},{10,9... | collective-permute-start | bytes 184328 | tf_op jit(solution)/shard_map/ppermute | solution.py:294
  52.4 5.8 %collective-permute-start.2 = (bf16[2,240,128]{2,1,0:T(8,128)(2,1)S(1)}, bf16[2,240,128]{2,1,0:T(8,128)(2,1)S(1)}, u32[]{:S(2)}, u32[]{:S(2)}) collective-permute-start(bf16[2,240,128]{2,1,0:T(8,128)(2,1)S(1)} %pad_maximum_fusion.2), channel_id=1, source_target_pairs={{0,6},{1,7},{2,0},{3,1},{4,2},{5,3},{6,4},{7,5},{8,14},{9,15},{10,... | collective-permute-start | bytes 368648 | tf_op jit(solution)/shard_map/ppermute | solution.py:294
  58.1 3.5 %collective-permute-done.2 = bf16[2,240,128]{2,1,0:T(8,128)(2,1)S(1)} collective-permute-done((bf16[2,240,128]{2,1,0:T(8,128)(2,1)S(1)}, bf16[2,240,128]{2,1,0:T(8,128)(2,1)S(1)}, u32[]{:S(2)}, u32[]{:S(2)}) %collective-permute-start.2) | collective-permute-done | bytes 122912 | tf_op jit(solution)/shard_map/ppermute | solution.py:294
  61.6 5.2 %collective-permute-start.3 = (bf16[4,240,128]{2,1,0:T(8,128)(2,1)S(1)}, bf16[4,240,128]{2,1,0:T(8,128)(2,1)S(1)}, u32[]{:S(2)}, u32[]{:S(2)}) collective-permute-start(bf16[4,240,128]{2,1,0:T(8,128)(2,1)S(1)} %pad_maximum_fusion.1), channel_id=1, source_target_pairs={{0,4},{1,5},{2,6},{3,7},{4,0},{5,1},{6,2},{7,3},{8,12},{9,13},{10,... | collective-permute-start | bytes 737288 | tf_op jit(solution)/shard_map/ppermute | solution.py:294
  66.9 5.7 %collective-permute-done.3 = bf16[4,240,128]{2,1,0:T(8,128)(2,1)S(1)} collective-permute-done((bf16[4,240,128]{2,1,0:T(8,128)(2,1)S(1)}, bf16[4,240,128]{2,1,0:T(8,128)(2,1)S(1)}, u32[]{:S(2)}, u32[]{:S(2)}) %collective-permute-start.3) | collective-permute-done | bytes 245792 | tf_op jit(solution)/shard_map/ppermute | solution.py:294
  77.1 7.4 %collective-permute-start.4 = (bf16[64,4096]{1,0:T(8,128)(2,1)S(1)}, bf16[64,4096]{1,0:T(8,128)(2,1)S(1)}, u32[]{:S(2)}, u32[]{:S(2)}) collective-permute-start(bf16[64,4096]{1,0:T(8,128)(2,1)S(1)} %get-tuple-element.20.refs_0_), channel_id=1, source_target_pairs={{0,8},{8,16},{16,24},{24,0},{32,40},{40,48},{48,56},{56,32},{64,72... | collective-permute-start | bytes 1572872 | tf_op jit(solution)/shard_map/ppermute | solution.py:259
  84.5 5.6 %collective-permute-start.7 = (bf16[64,4096]{1,0:T(8,128)(2,1)S(1)}, bf16[64,4096]{1,0:T(8,128)(2,1)S(1)}, u32[]{:S(2)}, u32[]{:S(2)}) collective-permute-start(bf16[64,4096]{1,0:T(8,128)(2,1)S(1)} %get-tuple-element.21.refs_1_), channel_id=1, source_target_pairs={{0,24},{8,0},{16,8},{24,16},{32,56},{40,32},{48,40},{56,48},{64,88... | collective-permute-start | bytes 1572872 | tf_op jit(solution)/shard_map/ppermute | solution.py:260
  90.1 3.4 %collective-permute-start.9 = (bf16[64,4096]{1,0:T(8,128)(2,1)S(1)}, bf16[64,4096]{1,0:T(8,128)(2,1)S(1)}, u32[]{:S(2)}, u32[]{:S(2)}) collective-permute-start(bf16[64,4096]{1,0:T(8,128)(2,1)S(1)} %get-tuple-element.20.refs_0_), channel_id=1, source_target_pairs={{0,24},{8,0},{16,8},{24,16},{32,56},{40,32},{48,40},{56,48},{64,88... | collective-permute-start | bytes 1572872 | tf_op jit(solution)/shard_map/ppermute | solution.py:262
  95.4 2.8 %collective-permute-done.4.refs_2_ = bf16[64,4096]{1,0:T(8,128)(2,1)S(1)} collective-permute-done((bf16[64,4096]{1,0:T(8,128)(2,1)S(1)}, bf16[64,4096]{1,0:T(8,128)(2,1)S(1)}, u32[]{:S(2)}, u32[]{:S(2)}) %collective-permute-start.4) | collective-permute-done | bytes 524320 | tf_op jit(solution)/shard_map/ppermute | solution.py:259
  100.1 4.6 %collective-permute-start.8 = (bf16[64,4096]{1,0:T(8,128)(2,1)S(1)}, bf16[64,4096]{1,0:T(8,128)(2,1)}, u32[]{:S(2)}, u32[]{:S(2)}) collective-permute-start(bf16[64,4096]{1,0:T(8,128)(2,1)S(1)} %collective-permute-done.7.refs_7_), channel_id=1, source_target_pairs={{0,24},{8,0},{16,8},{24,16},{32,56},{40,32},{48,40},{56,48},{64,88... | collective-permute-start | bytes 1572872 | tf_op jit(solution)/shard_map/ppermute | solution.py:264
  104.7 5.6 %collective-permute-done.9.refs_6_ = bf16[64,4096]{1,0:T(8,128)(2,1)S(1)} collective-permute-done((bf16[64,4096]{1,0:T(8,128)(2,1)S(1)}, bf16[64,4096]{1,0:T(8,128)(2,1)S(1)}, u32[]{:S(2)}, u32[]{:S(2)}) %collective-permute-start.9) | collective-permute-done | bytes 524320 | tf_op jit(solution)/shard_map/ppermute | solution.py:262
  110.3 10.7 %collective-permute-done.6.refs_4_ = bf16[64,4096]{1,0:T(8,128)(2,1)S(1)} collective-permute-done((bf16[64,4096]{1,0:T(8,128)(2,1)S(1)}, bf16[64,4096]{1,0:T(8,128)(2,1)S(1)}, u32[]{:S(2)}, u32[]{:S(2)}) %collective-permute-start.6) | collective-permute-done | bytes 524320 | tf_op jit(solution)/shard_map/ppermute | solution.py:263
  121.8 12.6 %all-gather.2.cloned.1.call-done = bf16[14336,128]{1,0:T(8,128)(2,1)} async-done(((bf16[1792,128]{1,0:T(8,128)(2,1)}), bf16[14336,128]{1,0:T(8,128)(2,1)}) %all-gather.2.cloned.1.call-update) | async-done | bytes 3670032 | tf_op jit(solution)/shard_map/all_gather | solution.py:304
  134.4 2.6 %collective-permute-start.10 = (bf16[8,8,224,128]{3,2,1,0:T(8,128)(2,1)}, bf16[8,8,224,128]{3,2,1,0:T(8,128)(2,1)S(1)}, u32[]{:S(2)}, u32[]{:S(2)}) collective-permute-start(bf16[8,8,224,128]{3,2,1,0:T(8,128)(2,1)} %bitcast.33), channel_id=1, source_target_pairs={{0,256},{256,0},{1,257},{257,1},{2,258},{258,2},{3,259},{259,3},{4... | collective-permute-start | bytes 11010056 | tf_op jit(solution)/shard_map/ppermute | solution.py:340
  137.6 7.7 %shard_map.95.first_ref = bf16[512,448]{1,0:T(8,128)(2,1)} custom-call(s32[2]{0:T(128)} %pad_add_fusion.place_ref, bf16[64,4096]{1,0:T(8,128)(2,1)} %copy-done.1, bf16[64,4096]{1,0:T(8,128)(2,1)} %copy-done.2, bf16[64,4096]{1,0:T(8,128)(2,1)} %copy-done.6, bf16[64,4096]{1,0:T(8,128)(2,1)} %copy-done.9, bf16[64,4096]{1,0:T(8,128)(2,1)} %copy-done.10, ...), custom_call_target="tpu_custom_call" | custom-call | flops 1879048192 | bytes 7864320 | tf_op jit(solution)/shard_map/pallas_call | solution.py:150
  147.1 8.3 %shard_map.96 = bf16[512,896]{1,0:T(8,128)(2,1)} custom-call(s32[2]{0:T(128)} %pad_add_fusion.place_ref, bf16[512,448]{1,0:T(8,128)(2,1)} %shard_map.95.first_ref, bf16[64,4096]{1,0:T(8,128)(2,1)} %copy-done.1, bf16[64,4096]{1,0:T(8,128)(2,1)} %copy-done.2, bf16[64,4096]{1,0:T(8,128)(2,1)} %copy-done.6, bf16[64,4096]{1,0:T(8,128)(2,1)} %copy-done.9, ...), custom_call_target="tpu_custom_call" | custom-call | flops 1879048192 | bytes 7864320 | tf_op jit(solution)/shard_map/pallas_call | solution.py:150
  155.4 7.0 %all-to-all-start.1 = ((bf16[32,16,896]{2,1,0:T(8,128)(2,1)}), bf16[32,16,896]{2,1,0:T(8,128)(2,1)S(1)}, u32[]{:S(2)}, u32[]{:S(2)}) async-start(bf16[32,16,896]{2,1,0:T(8,128)(2,1)} %bitcast.32), calls=%async_computation.1 | async-start | bytes 1835008 | tf_op jit(solution)/shard_map/all_to_all | solution.py:346
  162.7 24.4 %all-to-all-done.1 = bf16[32,16,896]{2,1,0:T(8,128)(2,1)S(1)} async-done(((bf16[32,16,896]{2,1,0:T(8,128)(2,1)}), bf16[32,16,896]{2,1,0:T(8,128)(2,1)S(1)}, u32[]{:S(2)}, u32[]{:S(2)}) %all-to-all-start.1) | async-done | bytes 917536 | tf_op jit(solution)/shard_map/all_to_all | solution.py:346
  187.0 3.4 %shard_map.97 = (bf16[128,3584]{1,0:T(8,128)(2,1)}, f32[8,1,512]{2,1,0:T(1,128)S(1)}) custom-call(bf16[8,4,16,896]{3,2,1,0:T(8,128)(2,1)S(1)} %bitcast.30, bf16[128,3584]{1,0:T(8,128)(2,1)S(1)} %copy-done.3, f32[1,3584]{1,0:T(1,128)S(1)} %broadcast_in_dim_reshape.3.gain_ref), custom_call_target="tpu_custom_call" | custom-call | flops 117440512 | bytes 2752512 | tf_op jit(solution)/shard_map/pallas_call | solution.py:237
  190.4 13.5 %all_to_all.21 = f32[8,1,512]{2,1,0:T(1,128)S(1)} all-to-all(f32[8,1,512]{2,1,0:T(1,128)S(1)} %get-tuple-element.30), channel_id=1, replica_groups=mesh['group'=2,'dp'=32,'mp'=8] {'mp'}, dimensions={0} | all-to-all | bytes 32768 | tf_op jit(solution)/shard_map/all_to_all | solution.py:351
  204.0 19.1 %all_to_all.22 = f32[64,1,512]{2,1,0:T(1,128)S(1)} all-to-all(f32[64,1,512]{2,1,0:T(1,128)S(1)} %broadcast_in_dim.29), channel_id=1, replica_groups=mesh['group'=2,'dp'=32,'mp'=8] {'group','dp'}, dimensions={0} | all-to-all | bytes 262144 | tf_op jit(solution)/shard_map/all_to_all | solution.py:354
  (61 shorter events, 16.1 us)
Async XLA Ops:
  7.2 11.1 %copy-start = (bf16[128,448]{0,1:T(8,128)(2,1)S(1)}, bf16[128,448]{0,1:T(8,128)(2,1)}, u32[]{:S(2)}) copy-start(bf16[128,448]{0,1:T(8,128)(2,1)} %param.9) | copy-start | bytes 344068
  7.2 69.2 %copy-start.4 = (f32[4096]{0:T(1024)S(1)}, f32[4096]{0:T(1024)}, u32[]{:S(2)}) copy-start(f32[4096]{0:T(1024)} %param.8) | copy-start | bytes 49156
  7.2 66.9 %all-to-all-start = ((bf16[8,128,512]{2,1,0:T(8,128)(2,1)}), bf16[8,128,512]{2,1,0:T(8,128)(2,1)S(1)}, u32[]{:S(2)}, u32[]{:S(2)}) async-start(bf16[8,128,512]{2,1,0:T(8,128)(2,1)} %bitcast.36), calls=%async_computation | async-start | bytes 2097152 | tf_op jit(solution)/shard_map/all_to_all | solution.py:323
  18.2 116.2 %all-gather.2.cloned.1.call-start = ((), (), s32[]{:S(2)}) async-start(), calls=%async_computation.4 | async-start | bytes 4128768 | tf_op jit(solution)/shard_map/all_gather | solution.py:304
  18.3 25.9 %collective-permute-start = (bf16[224,128]{1,0:T(8,128)(2,1)S(1)}, bf16[224,128]{1,0:T(8,128)(2,1)S(1)}, u32[]{:S(2)}, u32[]{:S(2)}) collective-permute-start(bf16[224,128]{1,0:T(8,128)(2,1)S(1)} %dynamic-slice_bitcast_fusion), channel_id=1, source_target_pairs={{0,0},{1,256},{2,8},{3,264},{4,16},{5,272},{6,24},{7,280},{8,2},{9... | collective-permute-start | bytes 172040 | tf_op jit(solution)/shard_map/ppermute | solution.py:282
  44.2 8.2 %collective-permute-start.1 = (bf16[1,240,128]{2,1,0:T(8,128)(2,1)S(1)}, bf16[1,240,128]{2,1,0:T(8,128)(2,1)S(1)}, u32[]{:S(2)}, u32[]{:S(2)}) collective-permute-start(bf16[1,240,128]{2,1,0:T(8,128)(2,1)S(1)} %maximum_bitcast_fusion), channel_id=1, source_target_pairs={{0,7},{1,0},{2,1},{3,2},{4,3},{5,4},{6,5},{7,6},{8,15},{9,8},{10,9... | collective-permute-start | bytes 184328 | tf_op jit(solution)/shard_map/ppermute | solution.py:294
  52.4 9.2 %collective-permute-start.2 = (bf16[2,240,128]{2,1,0:T(8,128)(2,1)S(1)}, bf16[2,240,128]{2,1,0:T(8,128)(2,1)S(1)}, u32[]{:S(2)}, u32[]{:S(2)}) collective-permute-start(bf16[2,240,128]{2,1,0:T(8,128)(2,1)S(1)} %pad_maximum_fusion.2), channel_id=1, source_target_pairs={{0,6},{1,7},{2,0},{3,1},{4,2},{5,3},{6,4},{7,5},{8,14},{9,15},{10,... | collective-permute-start | bytes 368648 | tf_op jit(solution)/shard_map/ppermute | solution.py:294
  61.6 10.9 %collective-permute-start.3 = (bf16[4,240,128]{2,1,0:T(8,128)(2,1)S(1)}, bf16[4,240,128]{2,1,0:T(8,128)(2,1)S(1)}, u32[]{:S(2)}, u32[]{:S(2)}) collective-permute-start(bf16[4,240,128]{2,1,0:T(8,128)(2,1)S(1)} %pad_maximum_fusion.1), channel_id=1, source_target_pairs={{0,4},{1,5},{2,6},{3,7},{4,0},{5,1},{6,2},{7,3},{8,12},{9,13},{10,... | collective-permute-start | bytes 737288 | tf_op jit(solution)/shard_map/ppermute | solution.py:294
  77.0 60.5 %copy-start.1 = (bf16[64,4096]{1,0:T(8,128)(2,1)}, bf16[64,4096]{1,0:T(8,128)(2,1)S(1)}, u32[]{:S(2)}) copy-start(bf16[64,4096]{1,0:T(8,128)(2,1)S(1)} %get-tuple-element.20.refs_0_) | copy-start | bytes 1572868
  77.1 60.5 %copy-start.2 = (bf16[64,4096]{1,0:T(8,128)(2,1)}, bf16[64,4096]{1,0:T(8,128)(2,1)S(1)}, u32[]{:S(2)}) copy-start(bf16[64,4096]{1,0:T(8,128)(2,1)S(1)} %get-tuple-element.21.refs_1_) | copy-start | bytes 1572868
  77.1 21.1 %collective-permute-start.4 = (bf16[64,4096]{1,0:T(8,128)(2,1)S(1)}, bf16[64,4096]{1,0:T(8,128)(2,1)S(1)}, u32[]{:S(2)}, u32[]{:S(2)}) collective-permute-start(bf16[64,4096]{1,0:T(8,128)(2,1)S(1)} %get-tuple-element.20.refs_0_), channel_id=1, source_target_pairs={{0,8},{8,16},{16,24},{24,0},{32,40},{40,48},{48,56},{56,32},{64,72... | collective-permute-start | bytes 1572872 | tf_op jit(solution)/shard_map/ppermute | solution.py:259
  84.5 15.6 %collective-permute-start.7 = (bf16[64,4096]{1,0:T(8,128)(2,1)S(1)}, bf16[64,4096]{1,0:T(8,128)(2,1)S(1)}, u32[]{:S(2)}, u32[]{:S(2)}) collective-permute-start(bf16[64,4096]{1,0:T(8,128)(2,1)S(1)} %get-tuple-element.21.refs_1_), channel_id=1, source_target_pairs={{0,24},{8,0},{16,8},{24,16},{32,56},{40,32},{48,40},{56,48},{64,88... | collective-permute-start | bytes 1572872 | tf_op jit(solution)/shard_map/ppermute | solution.py:260
  90.1 20.2 %collective-permute-start.9 = (bf16[64,4096]{1,0:T(8,128)(2,1)S(1)}, bf16[64,4096]{1,0:T(8,128)(2,1)S(1)}, u32[]{:S(2)}, u32[]{:S(2)}) collective-permute-start(bf16[64,4096]{1,0:T(8,128)(2,1)S(1)} %get-tuple-element.20.refs_0_), channel_id=1, source_target_pairs={{0,24},{8,0},{16,8},{24,16},{32,56},{40,32},{48,40},{56,48},{64,88... | collective-permute-start | bytes 1572872 | tf_op jit(solution)/shard_map/ppermute | solution.py:262
  93.5 16.8 %collective-permute-start.5 = (bf16[64,4096]{1,0:T(8,128)(2,1)S(1)}, bf16[64,4096]{1,0:T(8,128)(2,1)S(1)}, u32[]{:S(2)}, u32[]{:S(2)}) collective-permute-start(bf16[64,4096]{1,0:T(8,128)(2,1)S(1)} %get-tuple-element.21.refs_1_), channel_id=1, source_target_pairs={{0,8},{8,16},{16,24},{24,0},{32,40},{40,48},{48,56},{56,32},{64,72... | collective-permute-start | bytes 1572872 | tf_op jit(solution)/shard_map/ppermute | solution.py:261
  98.2 39.4 %copy-start.6 = (bf16[64,4096]{1,0:T(8,128)(2,1)}, bf16[64,4096]{1,0:T(8,128)(2,1)S(1)}, u32[]{:S(2)}) copy-start(bf16[64,4096]{1,0:T(8,128)(2,1)S(1)} %collective-permute-done.4.refs_2_) | copy-start | bytes 1572868
  98.2 22.8 %collective-permute-start.6 = (bf16[64,4096]{1,0:T(8,128)(2,1)S(1)}, bf16[64,4096]{1,0:T(8,128)(2,1)S(1)}, u32[]{:S(2)}, u32[]{:S(2)}) collective-permute-start(bf16[64,4096]{1,0:T(8,128)(2,1)S(1)} %collective-permute-done.4.refs_2_), channel_id=1, source_target_pairs={{0,8},{8,16},{16,24},{24,0},{32,40},{40,48},{48,56},{56,32},{64,72... | collective-permute-start | bytes 1572872 | tf_op jit(solution)/shard_map/ppermute | solution.py:263
  100.1 37.4 %copy-start.7 = (bf16[64,4096]{1,0:T(8,128)(2,1)}, bf16[64,4096]{1,0:T(8,128)(2,1)S(1)}, u32[]{:S(2)}) copy-start(bf16[64,4096]{1,0:T(8,128)(2,1)S(1)} %collective-permute-done.7.refs_7_) | copy-start | bytes 1572868
  100.1 21.7 %collective-permute-start.8 = (bf16[64,4096]{1,0:T(8,128)(2,1)S(1)}, bf16[64,4096]{1,0:T(8,128)(2,1)}, u32[]{:S(2)}, u32[]{:S(2)}) collective-permute-start(bf16[64,4096]{1,0:T(8,128)(2,1)S(1)} %collective-permute-done.7.refs_7_), channel_id=1, source_target_pairs={{0,24},{8,0},{16,8},{24,16},{32,56},{40,32},{48,40},{56,48},{64,88... | collective-permute-start | bytes 1572872 | tf_op jit(solution)/shard_map/ppermute | solution.py:264
  110.3 27.2 %copy-start.8 = (bf16[64,4096]{1,0:T(8,128)(2,1)}, bf16[64,4096]{1,0:T(8,128)(2,1)S(1)}, u32[]{:S(2)}) copy-start(bf16[64,4096]{1,0:T(8,128)(2,1)S(1)} %collective-permute-done.9.refs_6_) | copy-start | bytes 1572868
  110.3 27.2 %copy-start.9 = (bf16[64,4096]{1,0:T(8,128)(2,1)}, bf16[64,4096]{1,0:T(8,128)(2,1)S(1)}, u32[]{:S(2)}) copy-start(bf16[64,4096]{1,0:T(8,128)(2,1)S(1)} %collective-permute-done.5.refs_3_) | copy-start | bytes 1572868
  134.4 10.9 %collective-permute-start.10 = (bf16[8,8,224,128]{3,2,1,0:T(8,128)(2,1)}, bf16[8,8,224,128]{3,2,1,0:T(8,128)(2,1)S(1)}, u32[]{:S(2)}, u32[]{:S(2)}) collective-permute-start(bf16[8,8,224,128]{3,2,1,0:T(8,128)(2,1)} %bitcast.33), channel_id=1, source_target_pairs={{0,256},{256,0},{1,257},{257,1},{2,258},{258,2},{3,259},{259,3},{4... | collective-permute-start | bytes 11010056 | tf_op jit(solution)/shard_map/ppermute | solution.py:340
  145.2 17.2 %copy-start.12 = (bf16[4,240,128]{2,1,0:T(8,128)(2,1)S(1)}, bf16[4,240,128]{2,1,0:T(8,128)(2,1)}, u32[]{:S(2)}) copy-start(bf16[4,240,128]{2,1,0:T(8,128)(2,1)} %copy-done.11) | copy-start | bytes 737284
  145.2 41.8 %copy-start.3 = (bf16[128,3584]{1,0:T(8,128)(2,1)S(1)}, bf16[128,3584]{1,0:T(8,128)(2,1)}, u32[]{:S(2)}) copy-start(bf16[128,3584]{1,0:T(8,128)(2,1)} %hidden_ref.1) | copy-start | bytes 2752516
  155.4 31.6 %all-to-all-start.1 = ((bf16[32,16,896]{2,1,0:T(8,128)(2,1)}), bf16[32,16,896]{2,1,0:T(8,128)(2,1)S(1)}, u32[]{:S(2)}, u32[]{:S(2)}) async-start(bf16[32,16,896]{2,1,0:T(8,128)(2,1)} %bitcast.32), calls=%async_computation.1 | async-start | bytes 1835008 | tf_op jit(solution)/shard_map/all_to_all | solution.py:346
  (3 other events, 3.3 us)
Sparse Core Ops, SparseCore 0:
  74.2 60.1 all-gather.1

commit v5 on v2

--- a/solution.py
+++ b/solution.py
@@ -10,6 +10,8 @@
 EPSILON = 1e-06
 RING = 4
 MIB = 1024 * 1024
+FIRST_MIB = 44
+SECOND_MIB = 16
 EMPTY = 1e30
 EMPTY_FROM = 1e20
 
@@ -53,11 +55,57 @@
     )(moved, slot[None, :], teacher_gain[None, :])
 
 
-def block_product(sources, weight_source, rows_buffer, weights, total, row_sems, weight_sems):
+def block_dot(rows, weights, half, spans, pairs):
+    tile = weights.shape[3]
+    tiles = [
+        weights[span, 2 * pair : 2 * pair + 2, :half].reshape(2 * half, tile)
+        for span in spans
+        for pair in range(pairs)
+    ]
+    return lax.dot_general(
+        rows,
+        jnp.concatenate(tiles, axis=1),
+        (((1,), (1,)), ((), ())),
+        preferred_element_type=jnp.float32,
+    )
+
+
+def block_product(rows, weights, half, total, steps, ready):
+    y_count, shares = weights.shape[:2]
+    spans = y_count // steps
+    part = rows.shape[1] // steps
+    for step in range(steps):
+        ready(step)
+        partial = block_dot(
+            rows[:, step * part : (step + 1) * part],
+            weights,
+            half,
+            range(step * spans, (step + 1) * spans),
+            shares // 2,
+        )
+        if step == 0:
+            total[...] = partial
+        else:
+            total[...] += partial
+
+
+def turned(shards, total, all_rows):
+    rows = total.shape[0]
+    depth = rows // shards
+    to = lax.broadcasted_iota(jnp.int32, (rows, rows), 0)
+    source = lax.broadcasted_iota(jnp.int32, (rows, rows), 1)
+    turn = (source == (to % depth) * shards + to // depth).astype(jnp.bfloat16)
+    empty = all_rows[:, :128].astype(jnp.float32)[:, 0:1] > EMPTY_FROM
+    kept = jnp.where(empty, EMPTY, total[...]).astype(jnp.bfloat16)
+    return jnp.dot(turn, kept, preferred_element_type=jnp.float32).astype(jnp.bfloat16)
+
+
+def first_kernel(shards, half, count, *refs):
+    sources, weight_source = refs[:count], refs[count]
+    out_ref, rows_ref, weights, total, row_sems, weight_sems = refs[count + 1 :]
     steps = weight_sems.shape[0]
-    y_count, shares, half, tile = weights.shape
-    spans = y_count // steps
-    part = rows_buffer.shape[1] // steps
+    spans = weights.shape[0] // steps
+    part = rows_ref.shape[1] // steps
     height = sources[0].shape[0]
     copies = []
     for step in range(steps):
@@ -65,7 +113,7 @@
         chunk = [
             pltpu.make_async_copy(
                 source.at[:, features],
-                rows_buffer.at[pl.ds(i * height, height), features],
+                rows_ref.at[pl.ds(i * height, height), features],
                 row_sems.at[i, step],
             )
             for i, source in enumerate(sources)
@@ -78,49 +126,50 @@
     for chunk in copies:
         for copy in chunk:
             copy.start()
-    for step in range(steps):
+
+    def ready(step):
         for copy in copies[step]:
             copy.wait()
-        tiles = [
-            weights[span, 2 * pair : 2 * pair + 2].reshape(2 * half, tile)
-            for span in range(step * spans, (step + 1) * spans)
-            for pair in range(shares // 2)
-        ]
-        partial = lax.dot_general(
-            rows_buffer[:, step * part : (step + 1) * part],
-            jnp.concatenate(tiles, axis=1),
-            (((1,), (1,)), ((), ())),
-            preferred_element_type=jnp.float32,
-        )
-        if step == 0:
-            total[...] = partial
-        else:
-            total[...] += partial
-
-
-def turned(shards, total, rows_buffer):
-    rows = total.shape[0]
-    depth = rows // shards
-    to = lax.broadcasted_iota(jnp.int32, (rows, rows), 0)
-    source = lax.broadcasted_iota(jnp.int32, (rows, rows), 1)
-    turn = (source == (to % depth) * shards + to // depth).astype(jnp.bfloat16)
-    empty = rows_buffer[:, :128].astype(jnp.float32)[:, 0:1] > EMPTY_FROM
-    kept = jnp.where(empty, EMPTY, total[...]).astype(jnp.bfloat16)
-    return jnp.dot(turn, kept, preferred_element_type=jnp.float32).astype(jnp.bfloat16)
-
-
-def first_kernel(shards, count, *refs):
-    out_ref, rows_buffer, weights, total, row_sems, weight_sems = refs[count + 1 :]
-    block_product(refs[:count], refs[count], rows_buffer, weights, total, row_sems, weight_sems)
-    out_ref[...] = turned(shards, total, rows_buffer)
-
-
-def second_kernel(shards, count, core_ref, first_ref, *refs):
-    out_ref, rows_buffer, weights, total, row_sems, weight_sems = refs[count + 1 :]
-    block_product(refs[:count], refs[count], rows_buffer, weights, total, row_sems, weight_sems)
+
+    block_product(rows_ref, weights, half, total, steps, ready)
+    out_ref[...] = turned(shards, total, rows_ref)
+
+
+def first_product(pieces, weights, half, shards):
+    y_count, shares, _, tile = weights.shape
+    depth = y_count * (shares // 2) * tile
+    count = len(pieces)
+    total_rows = pieces[0].shape[0] * count
+    steps = 4
+    in_vmem = pl.BlockSpec(memory_space=pltpu.VMEM)
+    return pl.pallas_call(
+        functools.partial(first_kernel, shards, half, count),
+        out_shape=(
+            jax.ShapeDtypeStruct((total_rows, 2 * half), jnp.bfloat16),
+            jax.ShapeDtypeStruct((total_rows, depth), jnp.bfloat16),
+        ),
+        in_specs=[pl.BlockSpec(memory_space=pl.ANY)] * (count + 1),
+        out_specs=(in_vmem, in_vmem),
+        scratch_shapes=[
+            pltpu.VMEM(weights.shape, jnp.bfloat16),
+            pltpu.VMEM((total_rows, 2 * half), jnp.float32),
+            pltpu.SemaphoreType.DMA((count, steps)),
+            pltpu.SemaphoreType.DMA((steps,)),
+        ],
+        compiler_params=pltpu.CompilerParams(vmem_limit_bytes=FIRST_MIB * MIB),
+        cost_estimate=pl.CostEstimate(
+            flops=4 * total_rows * depth * half,
+            bytes_accessed=2 * depth * (total_rows + 2 * half),
+            transcendentals=0,
+        ),
+    )(*pieces, weights)
+
+
+def second_kernel(shards, half, core_ref, first_ref, rows_ref, weights_ref, out_ref, total):
+    block_product(rows_ref, weights_ref, half, total, 2, lambda step: None)
     width = total.shape[1]
     mine = first_ref[...]
-    other = turned(shards, total, rows_buffer)
+    other = turned(shards, total, rows_ref)
 
     @pl.when(core_ref[0] == 0)
     def _():
@@ -133,38 +182,22 @@
         out_ref[:, width:] = mine
 
 
-def product(pieces, weights, shards, core=None, first=None):
-    y_count, shares, half, tile = weights.shape
-    width = 2 * half
-    depth = y_count * (shares // 2) * tile
-    count = len(pieces)
-    total_rows = pieces[0].shape[0] * count
-    steps = 4
-    joined = first is not None
+def second_product(core, first, rows, weights, half, shards):
+    total_rows, depth = rows.shape
     in_vmem = pl.BlockSpec(memory_space=pltpu.VMEM)
-    head = [pl.BlockSpec(memory_space=pltpu.SMEM), in_vmem] if joined else []
-    kernel = second_kernel if joined else first_kernel
     return pl.pallas_call(
-        functools.partial(kernel, shards, count),
-        out_shape=jax.ShapeDtypeStruct(
-            (total_rows, 2 * width if joined else width), jnp.bfloat16
-        ),
-        in_specs=head + [pl.BlockSpec(memory_space=pl.ANY)] * (count + 1),
+        functools.partial(second_kernel, shards, half),
+        out_shape=jax.ShapeDtypeStruct((total_rows, 4 * half), jnp.bfloat16),
+        in_specs=[pl.BlockSpec(memory_space=pltpu.SMEM)] + [in_vmem] * 3,
         out_specs=in_vmem,
-        scratch_shapes=[
-            pltpu.VMEM((total_rows, depth), jnp.bfloat16),
-            pltpu.VMEM(weights.shape, jnp.bfloat16),
-            pltpu.VMEM((total_rows, width), jnp.float32),
-            pltpu.SemaphoreType.DMA((count, steps)),
-            pltpu.SemaphoreType.DMA((steps,)),
-        ],
-        compiler_params=pltpu.CompilerParams(vmem_limit_bytes=56 * MIB),
+        scratch_shapes=[pltpu.VMEM((total_rows, 2 * half), jnp.float32)],
+        compiler_params=pltpu.CompilerParams(vmem_limit_bytes=SECOND_MIB * MIB),
         cost_estimate=pl.CostEstimate(
-            flops=2 * total_rows * depth * width,
-            bytes_accessed=2 * depth * (total_rows + width),
+            flops=4 * total_rows * depth * half,
+            bytes_accessed=2 * depth * (total_rows + 2 * half),
             transcendentals=0,
         ),
-    )(*((core, first) if joined else ()), *pieces, weights)
+    )(core, first, rows, weights)
 
 
 def finish_kernel(
@@ -291,10 +324,10 @@
     )
     parts = spread[:, half:].reshape(mp_count, extra * tile).astype(jnp.float32)
     gains = parts[:, :width] + parts[:, width : 2 * width] + parts[:, 2 * width : 3 * width]
-    tiles = spread[:, :half].reshape(mp_count * half, tile)
+    tiles = spread.reshape(mp_count * (half + extra), tile)
     y_groups = [[y * x_count + x for y in range(y_count)] for x in range(x_count)]
     mine = lax.all_gather(tiles, "dp", axis=0, axis_index_groups=y_groups, tiled=True)
-    return mine.reshape(y_count, mp_count, half, tile), gains.reshape(mp_count * width)
+    return mine.reshape(y_count, mp_count, half + extra, tile), gains.reshape(mp_count * width)
 
 
 def local(teacher_hidden, teacher_gain, projector, live, placement, student_hidden, student_gain):
@@ -330,8 +363,10 @@
     pieces = ring_gather(top, low, x_count, dp_count)
     mine, pieces = lax.optimization_barrier((mine, pieces))
     other = lax.ppermute(mine, "group", [(0, 1), (1, 0)])
-    first = product(pieces, mine, dp_count)
-    buffer = product(pieces, other, dp_count, core.astype(jnp.int32).reshape(1), first)
+    half = share_width // 2
+    first, rows = first_product(pieces, mine, half, dp_count)
+    place = core.astype(jnp.int32).reshape(1)
+    buffer = second_product(place, first, rows, other, half, dp_count)
     quarter = buffer.shape[1]
     deep = x_count * capacity
     received = lax.all_to_all(

time: 215 us -> 213 us (level)
  Pallas kernels: 19.3 us -> 14.3 us
  local copies, waits for them, and re-layouts: 6.75 us -> 10.4 us
    pallas_call x2, Pallas kernels: 15.3 us -> 10.3 us  [the longest x1 6.45 us: first_product(): pl.pallas_call(functools.partial(first_kernel, shards, half, count), out_...]
    unnamed x25 -> x19, local copies, waits for them, and re-layouts: 4.32 us -> 8.82 us
  transfers between devices with their start and end apart: 11 -> 11, of which waited for: 7 -> 7; matrix products, arithmetic and copies ran while one was open for 2% -> 2% of each run, Pallas kernels for 4% -> 3%
where the time goes in v5:
time: 213 us; the launch traced here: 212 us
  waiting for transfers between devices  67 us (31%)
  blocking collectives  56.9 us (27%)
  starting transfers between devices  43 us (20%)
  between operations  16.6 us (8%)
  Pallas kernels  14.3 us (7%)
  local copies, waits for them, and re-layouts  10.4 us (5%)
  other arithmetic  4.36 us (2%)
    all_to_all x1, blocking collectives, projector_columns(): lax.all_to_all(jnp.broadcast_to(message[None], (mp_count,) + message.shap...  29 us
    all_to_all x1, waiting for transfers between devices, local(): moved = lax.all_to_all(blocks, 'mp', 0, 0, tiled=True)  23.8 us
    all_to_all x1, waiting for transfers between devices, local(): lax.all_to_all(buffer.reshape(dp_count, deep, quarter), 'dp', 0, 0, tiled...  23.6 us
    all_to_all x1, blocking collectives, local(): lax.all_to_all(jnp.broadcast_to(over_mp[None, :], (peers, over_mp.shape[0...  18.9 us
    ppermute x1, waiting for transfers between devices, ring_gather(): far_top = lax.ppermute(left_top, 'dp', forward)  11.2 us
    all_to_all x1, starting transfers between devices, local(): lax.all_to_all(buffer.reshape(dp_count, deep, quarter), 'dp', 0, 0, tiled...  9.86 us
    all_to_all x1, blocking collectives, local(): lax.all_to_all(message, 'mp', 0, 0, tiled=True)  8.97 us
    unnamed x19, local copies, waits for them, and re-layouts  8.82 us
  transfers between devices with their start and end apart: 11, of which 7 were waited for; matrix products, arithmetic and copies ran while one was open for 2% of the time, Pallas kernels for 3%

profile of v5, /device:TPU:1, one launch (start us, length us, event | category | flops | bytes accessed | tf_op | source)
XLA Modules:
  0.0 212.5 jit_solution(8123358296483038366)
XLA Ops:
  8.1 5.4 %collective-permute-start = (bf16[224,128]{1,0:T(8,128)(2,1)S(1)}, bf16[224,128]{1,0:T(8,128)(2,1)S(1)}, u32[]{:S(2)}, u32[]{:S(2)}) collective-permute-start(bf16[224,128]{1,0:T(8,128)(2,1)S(1)} %dynamic-slice_bitcast_fusion), channel_id=1, source_target_pairs={{0,0},{1,256},{2,8},{3,264},{4,16},{5,272},{6,24},{7,280},{8,2},{9... | collective-permute-start | bytes 172040 | tf_op jit(solution)/shard_map/ppermute | solution.py:312
  15.4 29.0 %all_to_all.26 = bf16[8,240,128]{2,1,0:T(8,128)(2,1)} all-to-all(bf16[8,240,128]{2,1,0:T(8,128)(2,1)S(1)} %broadcast_in_dim.13), channel_id=1, replica_groups=mesh['group'=2,'dp'=32,'mp'=8] {'mp'}, dimensions={0} | all-to-all | bytes 983040 | tf_op jit(solution)/shard_map/all_to_all | solution.py:322
  44.5 3.6 %all-to-all-start.1 = ((bf16[8,128,512]{2,1,0:T(8,128)(2,1)}), bf16[8,128,512]{2,1,0:T(8,128)(2,1)S(1)}, u32[]{:S(2)}, u32[]{:S(2)}) async-start(bf16[8,128,512]{2,1,0:T(8,128)(2,1)} %bitcast.32), calls=%async_computation.1 | async-start | bytes 2097152 | tf_op jit(solution)/shard_map/all_to_all | solution.py:348
  50.3 23.8 %all-to-all-done.1.moved_ref = bf16[8,128,512]{2,1,0:T(8,128)(2,1)S(1)} async-done(((bf16[8,128,512]{2,1,0:T(8,128)(2,1)}), bf16[8,128,512]{2,1,0:T(8,128)(2,1)S(1)}, u32[]{:S(2)}, u32[]{:S(2)}) %all-to-all-start.1) | async-done | bytes 1048608 | tf_op jit(solution)/shard_map/all_to_all | solution.py:348
  74.7 2.9 %collective-permute-start.1 = (bf16[64,4096]{1,0:T(8,128)(2,1)S(1)}, bf16[64,4096]{1,0:T(8,128)(2,1)S(1)}, u32[]{:S(2)}, u32[]{:S(2)}) collective-permute-start(bf16[64,4096]{1,0:T(8,128)(2,1)S(1)} %get-tuple-element.20.refs_0_), channel_id=1, source_target_pairs={{0,8},{8,16},{16,24},{24,0},{32,40},{40,48},{48,56},{56,32},{64,72... | collective-permute-start | bytes 1572872 | tf_op jit(solution)/shard_map/ppermute | solution.py:289
  77.6 3.6 %collective-permute-start.4 = (bf16[64,4096]{1,0:T(8,128)(2,1)S(1)}, bf16[64,4096]{1,0:T(8,128)(2,1)S(1)}, u32[]{:S(2)}, u32[]{:S(2)}) collective-permute-start(bf16[64,4096]{1,0:T(8,128)(2,1)S(1)} %get-tuple-element.21.refs_1_), channel_id=1, source_target_pairs={{0,24},{8,0},{16,8},{24,16},{32,56},{40,32},{48,40},{56,48},{64,88... | collective-permute-start | bytes 1572872 | tf_op jit(solution)/shard_map/ppermute | solution.py:290
  81.2 1.9 collective-permute-start.6
  83.2 3.4 %collective-permute-start.2 = (bf16[64,4096]{1,0:T(8,128)(2,1)S(1)}, bf16[64,4096]{1,0:T(8,128)(2,1)S(1)}, u32[]{:S(2)}, u32[]{:S(2)}) collective-permute-start(bf16[64,4096]{1,0:T(8,128)(2,1)S(1)} %get-tuple-element.21.refs_1_), channel_id=1, source_target_pairs={{0,8},{8,16},{16,24},{24,0},{32,40},{40,48},{48,56},{56,32},{64,72... | collective-permute-start | bytes 1572872 | tf_op jit(solution)/shard_map/ppermute | solution.py:291
  86.5 1.2 collective-permute-done.1.refs_2_
  87.7 1.9 collective-permute-start.3
  89.6 4.6 %collective-permute-start.5 = (bf16[64,4096]{1,0:T(8,128)(2,1)S(1)}, bf16[64,4096]{1,0:T(8,128)(2,1)S(1)}, u32[]{:S(2)}, u32[]{:S(2)}) collective-permute-start(bf16[64,4096]{1,0:T(8,128)(2,1)S(1)} %collective-permute-done.4.refs_7_), channel_id=1, source_target_pairs={{0,24},{8,0},{16,8},{24,16},{32,56},{40,32},{48,40},{56,48},{64,88... | collective-permute-start | bytes 1572872 | tf_op jit(solution)/shard_map/ppermute | solution.py:294
  94.2 5.9 %collective-permute-done.6.refs_6_ = bf16[64,4096]{1,0:T(8,128)(2,1)S(1)} collective-permute-done((bf16[64,4096]{1,0:T(8,128)(2,1)S(1)}, bf16[64,4096]{1,0:T(8,128)(2,1)S(1)}, u32[]{:S(2)}, u32[]{:S(2)}) %collective-permute-start.6) | collective-permute-done | bytes 524320 | tf_op jit(solution)/shard_map/ppermute | solution.py:292
  100.3 11.2 %collective-permute-done.3.refs_4_ = bf16[64,4096]{1,0:T(8,128)(2,1)S(1)} collective-permute-done((bf16[64,4096]{1,0:T(8,128)(2,1)S(1)}, bf16[64,4096]{1,0:T(8,128)(2,1)S(1)}, u32[]{:S(2)}, u32[]{:S(2)}) %collective-permute-start.3) | collective-permute-done | bytes 524320 | tf_op jit(solution)/shard_map/ppermute | solution.py:293
  113.1 5.9 %collective-permute-start.7 = (bf16[8,8,240,128]{3,2,1,0:T(8,128)(2,1)}, bf16[8,8,240,128]{3,2,1,0:T(8,128)(2,1)S(1)}, u32[]{:S(2)}, u32[]{:S(2)}) collective-permute-start(bf16[8,8,240,128]{3,2,1,0:T(8,128)(2,1)} %bitcast.27), channel_id=1, source_target_pairs={{0,256},{256,0},{1,257},{257,1},{2,258},{258,2},{3,259},{259,3},{4... | collective-permute-start | bytes 11796488 | tf_op jit(solution)/shard_map/ppermute | solution.py:365
  119.0 2.1 copy-done.2
  123.2 6.4 %shard_map.95 = (bf16[512,448]{1,0:T(8,128)(2,1)S(1)}, bf16[512,4096]{1,0:T(8,128)(2,1)}) custom-call(bf16[64,4096]{1,0:T(8,128)(2,1)S(1)} %get-tuple-element.20.refs_0_, bf16[64,4096]{1,0:T(8,128)(2,1)S(1)} %get-tuple-element.21.refs_1_, bf16[64,4096]{1,0:T(8,128)(2,1)S(1)} %collective-permute-done.1.refs_2_, ...), custom_call_target="tpu_custom_call" | custom-call | flops 1879048192 | bytes 7864320 | tf_op jit(solution)/shard_map/pallas_call | solution.py:145
  129.7 2.2 %copy-done.1 = bf16[512,4096]{1,0:T(8,128)(2,1)S(1)} copy-done((bf16[512,4096]{1,0:T(8,128)(2,1)S(1)}, bf16[512,4096]{1,0:T(8,128)(2,1)}, u32[]{:S(2)}) %copy-start.1) | copy-done | bytes 4194328
  131.8 3.9 %shard_map.96 = bf16[512,896]{1,0:T(8,128)(2,1)} custom-call(s32[1]{0:T(128)} %bitcast.core_ref, bf16[512,448]{1,0:T(8,128)(2,1)S(1)} %get-tuple-element.29.first_ref, bf16[512,4096]{1,0:T(8,128)(2,1)S(1)} %copy-done.1, bf16[8,8,240,128]{3,2,1,0:T(8,128)(2,1)S(1)} %collective-permute-done.7.weights_ref), custom_call_target="tpu_custom_call" | custom-call | flops 1879048192 | bytes 7864320 | tf_op jit(solution)/shard_map/pallas_call | solution.py:188
  135.7 9.9 %all-to-all-start.2 = ((bf16[32,16,896]{2,1,0:T(8,128)(2,1)}), bf16[32,16,896]{2,1,0:T(8,128)(2,1)S(1)}, u32[]{:S(2)}, u32[]{:S(2)}) async-start(bf16[32,16,896]{2,1,0:T(8,128)(2,1)} %bitcast.12), calls=%async_computation.2 | async-start | bytes 1835008 | tf_op jit(solution)/shard_map/all_to_all | solution.py:372
  146.5 23.6 %all-to-all-done.2 = bf16[32,16,896]{2,1,0:T(8,128)(2,1)S(1)} async-done(((bf16[32,16,896]{2,1,0:T(8,128)(2,1)}), bf16[32,16,896]{2,1,0:T(8,128)(2,1)S(1)}, u32[]{:S(2)}, u32[]{:S(2)}) %all-to-all-start.2) | async-done | bytes 917536 | tf_op jit(solution)/shard_map/all_to_all | solution.py:372
  170.2 3.3 %shard_map.97 = (bf16[128,3584]{1,0:T(8,128)(2,1)}, f32[8,1,512]{2,1,0:T(1,128)S(1)}) custom-call(bf16[8,4,16,896]{3,2,1,0:T(8,128)(2,1)S(1)} %bitcast.29, bf16[128,3584]{1,0:T(8,128)(2,1)S(1)} %copy-done.3, f32[1,3584]{1,0:T(1,128)S(1)} %broadcast_in_dim_reshape.3.gain_ref), custom_call_target="tpu_custom_call" | custom-call | flops 117440512 | bytes 2752512 | tf_op jit(solution)/shard_map/pallas_call | solution.py:267
  173.5 9.0 %all_to_all.27 = f32[8,1,512]{2,1,0:T(1,128)S(1)} all-to-all(f32[8,1,512]{2,1,0:T(1,128)S(1)} %get-tuple-element.32), channel_id=1, replica_groups=mesh['group'=2,'dp'=32,'mp'=8] {'mp'}, dimensions={0} | all-to-all | bytes 32768 | tf_op jit(solution)/shard_map/all_to_all | solution.py:377
  182.6 18.9 %all_to_all.28 = f32[64,1,512]{2,1,0:T(1,128)S(1)} all-to-all(f32[64,1,512]{2,1,0:T(1,128)S(1)} %broadcast_in_dim.16), channel_id=1, replica_groups=mesh['group'=2,'dp'=32,'mp'=8] {'group','dp'}, dimensions={0} | all-to-all | bytes 262144 | tf_op jit(solution)/shard_map/all_to_all | solution.py:380
  202.2 1.1 slice_divide_fusion
  (43 shorter events, 11.3 us)
Async XLA Ops:
  7.2 0.9 copy-start
  7.2 66.9 %copy-start.8 = (f32[4096]{0:T(1024)S(1)}, f32[4096]{0:T(1024)}, u32[]{:S(2)}) copy-start(f32[4096]{0:T(1024)} %param.8) | copy-start | bytes 49156
  7.2 105.9 %all-gather.2.cloned.1.call-start = ((), (), s32[]{:S(2)}) async-start(), calls=%async_computation.5 | async-start | bytes 4423680 | tf_op jit(solution)/shard_map/all_gather | solution.py:329
  8.1 7.2 %collective-permute-start = (bf16[224,128]{1,0:T(8,128)(2,1)S(1)}, bf16[224,128]{1,0:T(8,128)(2,1)S(1)}, u32[]{:S(2)}, u32[]{:S(2)}) collective-permute-start(bf16[224,128]{1,0:T(8,128)(2,1)S(1)} %dynamic-slice_bitcast_fusion), channel_id=1, source_target_pairs={{0,0},{1,256},{2,8},{3,264},{4,16},{5,272},{6,24},{7,280},{8,2},{9... | collective-permute-start | bytes 172040 | tf_op jit(solution)/shard_map/ppermute | solution.py:312
  44.5 29.6 %all-to-all-start.1 = ((bf16[8,128,512]{2,1,0:T(8,128)(2,1)}), bf16[8,128,512]{2,1,0:T(8,128)(2,1)S(1)}, u32[]{:S(2)}, u32[]{:S(2)}) async-start(bf16[8,128,512]{2,1,0:T(8,128)(2,1)} %bitcast.32), calls=%async_computation.1 | async-start | bytes 2097152 | tf_op jit(solution)/shard_map/all_to_all | solution.py:348
  74.7 13.0 %collective-permute-start.1 = (bf16[64,4096]{1,0:T(8,128)(2,1)S(1)}, bf16[64,4096]{1,0:T(8,128)(2,1)S(1)}, u32[]{:S(2)}, u32[]{:S(2)}) collective-permute-start(bf16[64,4096]{1,0:T(8,128)(2,1)S(1)} %get-tuple-element.20.refs_0_), channel_id=1, source_target_pairs={{0,8},{8,16},{16,24},{24,0},{32,40},{40,48},{48,56},{56,32},{64,72... | collective-permute-start | bytes 1572872 | tf_op jit(solution)/shard_map/ppermute | solution.py:289
  77.6 12.0 %collective-permute-start.4 = (bf16[64,4096]{1,0:T(8,128)(2,1)S(1)}, bf16[64,4096]{1,0:T(8,128)(2,1)S(1)}, u32[]{:S(2)}, u32[]{:S(2)}) collective-permute-start(bf16[64,4096]{1,0:T(8,128)(2,1)S(1)} %get-tuple-element.21.refs_1_), channel_id=1, source_target_pairs={{0,24},{8,0},{16,8},{24,16},{32,56},{40,32},{48,40},{56,48},{64,88... | collective-permute-start | bytes 1572872 | tf_op jit(solution)/shard_map/ppermute | solution.py:290
  81.2 18.9 %collective-permute-start.6 = (bf16[64,4096]{1,0:T(8,128)(2,1)S(1)}, bf16[64,4096]{1,0:T(8,128)(2,1)S(1)}, u32[]{:S(2)}, u32[]{:S(2)}) collective-permute-start(bf16[64,4096]{1,0:T(8,128)(2,1)S(1)} %get-tuple-element.20.refs_0_), channel_id=1, source_target_pairs={{0,24},{8,0},{16,8},{24,16},{32,56},{40,32},{48,40},{56,48},{64,88... | collective-permute-start | bytes 1572872 | tf_op jit(solution)/shard_map/ppermute | solution.py:292
  83.2 17.1 %collective-permute-start.2 = (bf16[64,4096]{1,0:T(8,128)(2,1)S(1)}, bf16[64,4096]{1,0:T(8,128)(2,1)S(1)}, u32[]{:S(2)}, u32[]{:S(2)}) collective-permute-start(bf16[64,4096]{1,0:T(8,128)(2,1)S(1)} %get-tuple-element.21.refs_1_), channel_id=1, source_target_pairs={{0,8},{8,16},{16,24},{24,0},{32,40},{40,48},{48,56},{56,32},{64,72... | collective-permute-start | bytes 1572872 | tf_op jit(solution)/shard_map/ppermute | solution.py:291
  87.7 23.8 %collective-permute-start.3 = (bf16[64,4096]{1,0:T(8,128)(2,1)S(1)}, bf16[64,4096]{1,0:T(8,128)(2,1)S(1)}, u32[]{:S(2)}, u32[]{:S(2)}) collective-permute-start(bf16[64,4096]{1,0:T(8,128)(2,1)S(1)} %collective-permute-done.1.refs_2_), channel_id=1, source_target_pairs={{0,8},{8,16},{16,24},{24,0},{32,40},{40,48},{48,56},{56,32},{64,72... | collective-permute-start | bytes 1572872 | tf_op jit(solution)/shard_map/ppermute | solution.py:293
  89.6 22.7 %collective-permute-start.5 = (bf16[64,4096]{1,0:T(8,128)(2,1)S(1)}, bf16[64,4096]{1,0:T(8,128)(2,1)S(1)}, u32[]{:S(2)}, u32[]{:S(2)}) collective-permute-start(bf16[64,4096]{1,0:T(8,128)(2,1)S(1)} %collective-permute-done.4.refs_7_), channel_id=1, source_target_pairs={{0,24},{8,0},{16,8},{24,16},{32,56},{40,32},{48,40},{56,48},{64,88... | collective-permute-start | bytes 1572872 | tf_op jit(solution)/shard_map/ppermute | solution.py:294
  111.5 0.8 copy-start.4
  112.3 0.8 copy-start.6
  113.1 16.6 %collective-permute-start.7 = (bf16[8,8,240,128]{3,2,1,0:T(8,128)(2,1)}, bf16[8,8,240,128]{3,2,1,0:T(8,128)(2,1)S(1)}, u32[]{:S(2)}, u32[]{:S(2)}) collective-permute-start(bf16[8,8,240,128]{3,2,1,0:T(8,128)(2,1)} %bitcast.27), channel_id=1, source_target_pairs={{0,256},{256,0},{1,257},{257,1},{2,258},{258,2},{3,259},{259,3},{4... | collective-permute-start | bytes 11796488 | tf_op jit(solution)/shard_map/ppermute | solution.py:365
  119.0 2.1 copy-start.2
  121.1 1.0 copy-start.5
  122.2 1.0 copy-start.7
  129.7 2.2 %copy-start.1 = (bf16[512,4096]{1,0:T(8,128)(2,1)S(1)}, bf16[512,4096]{1,0:T(8,128)(2,1)}, u32[]{:S(2)}) copy-start(bf16[512,4096]{1,0:T(8,128)(2,1)} %get-tuple-element.30.rows_ref) | copy-start | bytes 12582916
  131.8 38.3 %copy-start.3 = (bf16[128,3584]{1,0:T(8,128)(2,1)S(1)}, bf16[128,3584]{1,0:T(8,128)(2,1)}, u32[]{:S(2)}) copy-start(bf16[128,3584]{1,0:T(8,128)(2,1)} %hidden_ref.1) | copy-start | bytes 2752516
  135.7 34.5 %all-to-all-start.2 = ((bf16[32,16,896]{2,1,0:T(8,128)(2,1)}), bf16[32,16,896]{2,1,0:T(8,128)(2,1)S(1)}, u32[]{:S(2)}, u32[]{:S(2)}) async-start(bf16[32,16,896]{2,1,0:T(8,128)(2,1)} %bitcast.12), calls=%async_computation.2 | async-start | bytes 1835008 | tf_op jit(solution)/shard_map/all_to_all | solution.py:372
Sparse Core Ops, SparseCore 0:
  44.6 52.1 all-gather.1

commit v6 on v5

--- a/solution.py
+++ b/solution.py
@@ -10,8 +10,6 @@
 EPSILON = 1e-06
 RING = 4
 MIB = 1024 * 1024
-FIRST_MIB = 44
-SECOND_MIB = 16
 EMPTY = 1e30
 EMPTY_FROM = 1e20
 
@@ -70,14 +68,15 @@
     )
 
 
-def block_product(rows, weights, half, total, steps, ready):
+def block_product(pieces, weights, half, total):
     y_count, shares = weights.shape[:2]
+    steps = 4
     spans = y_count // steps
-    part = rows.shape[1] // steps
+    part = pieces[0].shape[1] // steps
     for step in range(steps):
-        ready(step)
+        features = slice(step * part, (step + 1) * part)
         partial = block_dot(
-            rows[:, step * part : (step + 1) * part],
+            jnp.concatenate([piece[:, features] for piece in pieces], axis=0),
             weights,
             half,
             range(step * spans, (step + 1) * spans),
@@ -89,115 +88,66 @@
             total[...] += partial
 
 
-def turned(shards, total, all_rows):
+def turned(shards, total, pieces):
     rows = total.shape[0]
     depth = rows // shards
     to = lax.broadcasted_iota(jnp.int32, (rows, rows), 0)
     source = lax.broadcasted_iota(jnp.int32, (rows, rows), 1)
     turn = (source == (to % depth) * shards + to // depth).astype(jnp.bfloat16)
-    empty = all_rows[:, :128].astype(jnp.float32)[:, 0:1] > EMPTY_FROM
+    first_features = jnp.concatenate([piece[:, :128] for piece in pieces], axis=0)
+    empty = first_features.astype(jnp.float32)[:, 0:1] > EMPTY_FROM
     kept = jnp.where(empty, EMPTY, total[...]).astype(jnp.bfloat16)
     return jnp.dot(turn, kept, preferred_element_type=jnp.float32).astype(jnp.bfloat16)
 
 
 def first_kernel(shards, half, count, *refs):
-    sources, weight_source = refs[:count], refs[count]
-    out_ref, rows_ref, weights, total, row_sems, weight_sems = refs[count + 1 :]
-    steps = weight_sems.shape[0]
-    spans = weights.shape[0] // steps
-    part = rows_ref.shape[1] // steps
-    height = sources[0].shape[0]
-    copies = []
-    for step in range(steps):
-        features = pl.ds(step * part, part)
-        chunk = [
-            pltpu.make_async_copy(
-                source.at[:, features],
-                rows_ref.at[pl.ds(i * height, height), features],
-                row_sems.at[i, step],
-            )
-            for i, source in enumerate(sources)
-        ]
-        blocks = pl.ds(step * spans, spans)
-        chunk.append(
-            pltpu.make_async_copy(weight_source.at[blocks], weights.at[blocks], weight_sems.at[step])
-        )
-        copies.append(chunk)
-    for chunk in copies:
-        for copy in chunk:
-            copy.start()
-
-    def ready(step):
-        for copy in copies[step]:
-            copy.wait()
-
-    block_product(rows_ref, weights, half, total, steps, ready)
-    out_ref[...] = turned(shards, total, rows_ref)
-
-
-def first_product(pieces, weights, half, shards):
+    pieces, weights_ref, out_ref, total = refs[:count], *refs[count:]
+    block_product(pieces, weights_ref, half, total)
+    out_ref[...] = turned(shards, total, pieces)
+
+
+def second_kernel(shards, half, count, core_ref, first_ref, *refs):
+    pieces, weights_ref, out_ref, total = refs[:count], *refs[count:]
+    block_product(pieces, weights_ref, half, total)
+    width = total.shape[1]
+    mine = first_ref[...]
+    other = turned(shards, total, pieces)
+
+    @pl.when(core_ref[0] == 0)
+    def _():
+        out_ref[:, :width] = mine
+        out_ref[:, width:] = other
+
+    @pl.when(core_ref[0] != 0)
+    def _():
+        out_ref[:, :width] = other
+        out_ref[:, width:] = mine
+
+
+def product(pieces, weights, half, shards, core=None, first=None):
     y_count, shares, _, tile = weights.shape
     depth = y_count * (shares // 2) * tile
     count = len(pieces)
     total_rows = pieces[0].shape[0] * count
-    steps = 4
+    joined = first is not None
     in_vmem = pl.BlockSpec(memory_space=pltpu.VMEM)
+    head = [pl.BlockSpec(memory_space=pltpu.SMEM), in_vmem] if joined else []
+    kernel = second_kernel if joined else first_kernel
     return pl.pallas_call(
-        functools.partial(first_kernel, shards, half, count),
-        out_shape=(
-            jax.ShapeDtypeStruct((total_rows, 2 * half), jnp.bfloat16),
-            jax.ShapeDtypeStruct((total_rows, depth), jnp.bfloat16),
-        ),
-        in_specs=[pl.BlockSpec(memory_space=pl.ANY)] * (count + 1),
-        out_specs=(in_vmem, in_vmem),
-        scratch_shapes=[
-            pltpu.VMEM(weights.shape, jnp.bfloat16),
-            pltpu.VMEM((total_rows, 2 * half), jnp.float32),
-            pltpu.SemaphoreType.DMA((count, steps)),
-            pltpu.SemaphoreType.DMA((steps,)),
-        ],
-        compiler_params=pltpu.CompilerParams(vmem_limit_bytes=FIRST_MIB * MIB),
+        functools.partial(kernel, shards, half, count),
+        out_shape=jax.ShapeDtypeStruct(
+            (total_rows, (4 if joined else 2) * half), jnp.bfloat16
+        ),
+        in_specs=head + [in_vmem] * (count + 1),
+        out_specs=in_vmem,
+        scratch_shapes=[pltpu.VMEM((total_rows, 2 * half), jnp.float32)],
+        compiler_params=pltpu.CompilerParams(vmem_limit_bytes=32 * MIB),
         cost_estimate=pl.CostEstimate(
             flops=4 * total_rows * depth * half,
             bytes_accessed=2 * depth * (total_rows + 2 * half),
             transcendentals=0,
         ),
-    )(*pieces, weights)
-
-
-def second_kernel(shards, half, core_ref, first_ref, rows_ref, weights_ref, out_ref, total):
-    block_product(rows_ref, weights_ref, half, total, 2, lambda step: None)
-    width = total.shape[1]
-    mine = first_ref[...]
-    other = turned(shards, total, rows_ref)
-
-    @pl.when(core_ref[0] == 0)
-    def _():
-        out_ref[:, :width] = mine
-        out_ref[:, width:] = other
-
-    @pl.when(core_ref[0] != 0)
-    def _():
-        out_ref[:, :width] = other
-        out_ref[:, width:] = mine
-
-
-def second_product(core, first, rows, weights, half, shards):
-    total_rows, depth = rows.shape
-    in_vmem = pl.BlockSpec(memory_space=pltpu.VMEM)
-    return pl.pallas_call(
-        functools.partial(second_kernel, shards, half),
-        out_shape=jax.ShapeDtypeStruct((total_rows, 4 * half), jnp.bfloat16),
-        in_specs=[pl.BlockSpec(memory_space=pltpu.SMEM)] + [in_vmem] * 3,
-        out_specs=in_vmem,
-        scratch_shapes=[pltpu.VMEM((total_rows, 2 * half), jnp.float32)],
-        compiler_params=pltpu.CompilerParams(vmem_limit_bytes=SECOND_MIB * MIB),
-        cost_estimate=pl.CostEstimate(
-            flops=4 * total_rows * depth * half,
-            bytes_accessed=2 * depth * (total_rows + 2 * half),
-            transcendentals=0,
-        ),
-    )(core, first, rows, weights)
+    )(*((core, first) if joined else ()), *pieces, weights)
 
 
 def finish_kernel(
@@ -364,9 +314,9 @@
     mine, pieces = lax.optimization_barrier((mine, pieces))
     other = lax.ppermute(mine, "group", [(0, 1), (1, 0)])
     half = share_width // 2
-    first, rows = first_product(pieces, mine, half, dp_count)
+    first = product(pieces, mine, half, dp_count)
     place = core.astype(jnp.int32).reshape(1)
-    buffer = second_product(place, first, rows, other, half, dp_count)
+    buffer = product(pieces, other, half, dp_count, place, first)
     quarter = buffer.shape[1]
     deep = x_count * capacity
     received = lax.all_to_all(

time: 213 us -> 209 us (0.981)
  Pallas kernels: 14.3 us -> 10.6 us
    pallas_call x2, Pallas kernels: 10.3 us -> 6.63 us  [product(): pl.pallas_call(functools.partial(kernel, shards, half, count), out_shape=...]
    unnamed x19 -> x17, local copies, waits for them, and re-layouts: 8.82 us -> 7.81 us
  transfers between devices with their start and end apart: 11 -> 11, of which waited for: 7 -> 7; matrix products, arithmetic and copies ran while one was open for 2% -> 2% of each run, Pallas kernels for 3% -> 2%
where the time goes in v6:
time: 209 us; the launch traced here: 208 us
  waiting for transfers between devices  67 us (32%)
  blocking collectives  56.9 us (27%)
  starting transfers between devices  43 us (21%)
  between operations  16.7 us (8%)
  Pallas kernels  10.6 us (5%)
  local copies, waits for them, and re-layouts  9.49 us (5%)
  other arithmetic  4.49 us (2%)
    all_to_all x1, blocking collectives, projector_columns(): lax.all_to_all(jnp.broadcast_to(message[None], (mp_count,) + message.shap...  29 us
    all_to_all x1, waiting for transfers between devices, local(): moved = lax.all_to_all(blocks, 'mp', 0, 0, tiled=True)  23.8 us
    all_to_all x1, waiting for transfers between devices, local(): lax.all_to_all(buffer.reshape(dp_count, deep, quarter), 'dp', 0, 0, tiled...  23.6 us
    all_to_all x1, blocking collectives, local(): lax.all_to_all(jnp.broadcast_to(over_mp[None, :], (peers, over_mp.shape[0...  18.9 us
    ppermute x1, waiting for transfers between devices, ring_gather(): far_top = lax.ppermute(left_top, 'dp', forward)  11.2 us
    all_to_all x1, starting transfers between devices, local(): lax.all_to_all(buffer.reshape(dp_count, deep, quarter), 'dp', 0, 0, tiled...  9.86 us
    all_to_all x1, blocking collectives, local(): lax.all_to_all(message, 'mp', 0, 0, tiled=True)  8.97 us
    unnamed x17, local copies, waits for them, and re-layouts  7.81 us
  transfers between devices with their start and end apart: 11, of which 7 were waited for; matrix products, arithmetic and copies ran while one was open for 2% of the time, Pallas kernels for 2%

profile of v6, /device:TPU:1, one launch (start us, length us, event | category | flops | bytes accessed | tf_op | source)
XLA Modules:
  0.0 208.1 jit_solution(8949495360245063990)
XLA Ops:
  8.1 5.4 %collective-permute-start = (bf16[224,128]{1,0:T(8,128)(2,1)S(1)}, bf16[224,128]{1,0:T(8,128)(2,1)S(1)}, u32[]{:S(2)}, u32[]{:S(2)}) collective-permute-start(bf16[224,128]{1,0:T(8,128)(2,1)S(1)} %dynamic-slice_bitcast_fusion), channel_id=1, source_target_pairs={{0,0},{1,256},{2,8},{3,264},{4,16},{5,272},{6,24},{7,280},{8,2},{9... | collective-permute-start | bytes 172040 | tf_op jit(solution)/shard_map/ppermute | solution.py:262
  15.4 29.0 %all_to_all.26 = bf16[8,240,128]{2,1,0:T(8,128)(2,1)} all-to-all(bf16[8,240,128]{2,1,0:T(8,128)(2,1)S(1)} %broadcast_in_dim.13), channel_id=1, replica_groups=mesh['group'=2,'dp'=32,'mp'=8] {'mp'}, dimensions={0} | all-to-all | bytes 983040 | tf_op jit(solution)/shard_map/all_to_all | solution.py:272
  44.5 3.6 %all-to-all-start.1 = ((bf16[8,128,512]{2,1,0:T(8,128)(2,1)}), bf16[8,128,512]{2,1,0:T(8,128)(2,1)S(1)}, u32[]{:S(2)}, u32[]{:S(2)}) async-start(bf16[8,128,512]{2,1,0:T(8,128)(2,1)} %bitcast.32), calls=%async_computation.1 | async-start | bytes 2097152 | tf_op jit(solution)/shard_map/all_to_all | solution.py:298
  50.3 23.8 %all-to-all-done.1.moved_ref = bf16[8,128,512]{2,1,0:T(8,128)(2,1)S(1)} async-done(((bf16[8,128,512]{2,1,0:T(8,128)(2,1)}), bf16[8,128,512]{2,1,0:T(8,128)(2,1)S(1)}, u32[]{:S(2)}, u32[]{:S(2)}) %all-to-all-start.1) | async-done | bytes 1048608 | tf_op jit(solution)/shard_map/all_to_all | solution.py:298
  74.7 2.9 %collective-permute-start.1 = (bf16[64,4096]{1,0:T(8,128)(2,1)S(1)}, bf16[64,4096]{1,0:T(8,128)(2,1)S(1)}, u32[]{:S(2)}, u32[]{:S(2)}) collective-permute-start(bf16[64,4096]{1,0:T(8,128)(2,1)S(1)} %get-tuple-element.18.refs_0_), channel_id=1, source_target_pairs={{0,8},{8,16},{16,24},{24,0},{32,40},{40,48},{48,56},{56,32},{64,72... | collective-permute-start | bytes 1572872 | tf_op jit(solution)/shard_map/ppermute | solution.py:239
  77.6 3.6 %collective-permute-start.4 = (bf16[64,4096]{1,0:T(8,128)(2,1)S(1)}, bf16[64,4096]{1,0:T(8,128)(2,1)S(1)}, u32[]{:S(2)}, u32[]{:S(2)}) collective-permute-start(bf16[64,4096]{1,0:T(8,128)(2,1)S(1)} %get-tuple-element.19.refs_1_), channel_id=1, source_target_pairs={{0,24},{8,0},{16,8},{24,16},{32,56},{40,32},{48,40},{56,48},{64,88... | collective-permute-start | bytes 1572872 | tf_op jit(solution)/shard_map/ppermute | solution.py:240
  81.2 1.9 collective-permute-start.6
  83.2 3.4 %collective-permute-start.2 = (bf16[64,4096]{1,0:T(8,128)(2,1)S(1)}, bf16[64,4096]{1,0:T(8,128)(2,1)S(1)}, u32[]{:S(2)}, u32[]{:S(2)}) collective-permute-start(bf16[64,4096]{1,0:T(8,128)(2,1)S(1)} %get-tuple-element.19.refs_1_), channel_id=1, source_target_pairs={{0,8},{8,16},{16,24},{24,0},{32,40},{40,48},{48,56},{56,32},{64,72... | collective-permute-start | bytes 1572872 | tf_op jit(solution)/shard_map/ppermute | solution.py:241
  86.5 1.2 collective-permute-done.1.refs_2_
  87.7 1.9 collective-permute-start.3
  89.6 4.6 %collective-permute-start.5 = (bf16[64,4096]{1,0:T(8,128)(2,1)S(1)}, bf16[64,4096]{1,0:T(8,128)(2,1)S(1)}, u32[]{:S(2)}, u32[]{:S(2)}) collective-permute-start(bf16[64,4096]{1,0:T(8,128)(2,1)S(1)} %collective-permute-done.4.refs_7_), channel_id=1, source_target_pairs={{0,24},{8,0},{16,8},{24,16},{32,56},{40,32},{48,40},{56,48},{64,88... | collective-permute-start | bytes 1572872 | tf_op jit(solution)/shard_map/ppermute | solution.py:244
  94.2 5.9 %collective-permute-done.6.refs_6_ = bf16[64,4096]{1,0:T(8,128)(2,1)S(1)} collective-permute-done((bf16[64,4096]{1,0:T(8,128)(2,1)S(1)}, bf16[64,4096]{1,0:T(8,128)(2,1)S(1)}, u32[]{:S(2)}, u32[]{:S(2)}) %collective-permute-start.6) | collective-permute-done | bytes 524320 | tf_op jit(solution)/shard_map/ppermute | solution.py:242
  100.3 11.2 %collective-permute-done.3.refs_4_ = bf16[64,4096]{1,0:T(8,128)(2,1)S(1)} collective-permute-done((bf16[64,4096]{1,0:T(8,128)(2,1)S(1)}, bf16[64,4096]{1,0:T(8,128)(2,1)S(1)}, u32[]{:S(2)}, u32[]{:S(2)}) %collective-permute-start.3) | collective-permute-done | bytes 524320 | tf_op jit(solution)/shard_map/ppermute | solution.py:243
  113.1 5.9 %collective-permute-start.7 = (bf16[8,8,240,128]{3,2,1,0:T(8,128)(2,1)}, bf16[8,8,240,128]{3,2,1,0:T(8,128)(2,1)S(1)}, u32[]{:S(2)}, u32[]{:S(2)}) collective-permute-start(bf16[8,8,240,128]{3,2,1,0:T(8,128)(2,1)} %bitcast.27), channel_id=1, source_target_pairs={{0,256},{256,0},{1,257},{257,1},{2,258},{258,2},{3,259},{259,3},{4... | collective-permute-start | bytes 11796488 | tf_op jit(solution)/shard_map/ppermute | solution.py:315
  119.0 2.1 %copy-done.1 = bf16[15360,128]{1,0:T(8,128)(2,1)S(1)} copy-done((bf16[15360,128]{1,0:T(8,128)(2,1)S(1)}, bf16[15360,128]{1,0:T(8,128)(2,1)}, u32[]{:S(2)}) %copy-start.1) | copy-done | bytes 3932184
  123.2 2.8 %shard_map.95.first_ref = bf16[512,448]{1,0:T(8,128)(2,1)S(1)} custom-call(bf16[64,4096]{1,0:T(8,128)(2,1)S(1)} %get-tuple-element.18.refs_0_, bf16[64,4096]{1,0:T(8,128)(2,1)S(1)} %get-tuple-element.19.refs_1_, bf16[64,4096]{1,0:T(8,128)(2,1)S(1)} %collective-permute-done.1.refs_2_, bf16[64,4096]{1,0:T(8,128)(2,1)S(1)} %collective-permute-done.2.refs_3_, ...), custom_call_target="tpu_custom_call" | custom-call | flops 1879048192 | bytes 7864320 | tf_op jit(solution)/shard_map/pallas_call | solution.py:136
  126.0 3.9 %shard_map.96 = bf16[512,896]{1,0:T(8,128)(2,1)} custom-call(s32[1]{0:T(128)} %bitcast.core_ref, bf16[512,448]{1,0:T(8,128)(2,1)S(1)} %shard_map.95.first_ref, bf16[64,4096]{1,0:T(8,128)(2,1)S(1)} %get-tuple-element.18.refs_0_, bf16[64,4096]{1,0:T(8,128)(2,1)S(1)} %get-tuple-element.19.refs_1_, bf16[64,4096]{1,0:T(8,128)(2,1)S(1)} %collective-permute-done.1.refs_2_, ...), custom_call_target="tpu_custom_call" | custom-call | flops 1879048192 | bytes 7864320 | tf_op jit(solution)/shard_map/pallas_call | solution.py:136
  129.8 9.9 %all-to-all-start.2 = ((bf16[32,16,896]{2,1,0:T(8,128)(2,1)}), bf16[32,16,896]{2,1,0:T(8,128)(2,1)S(1)}, u32[]{:S(2)}, u32[]{:S(2)}) async-start(bf16[32,16,896]{2,1,0:T(8,128)(2,1)} %bitcast.12), calls=%async_computation.2 | async-start | bytes 1835008 | tf_op jit(solution)/shard_map/all_to_all | solution.py:322
  140.7 23.6 %all-to-all-done.2 = bf16[32,16,896]{2,1,0:T(8,128)(2,1)S(1)} async-done(((bf16[32,16,896]{2,1,0:T(8,128)(2,1)}), bf16[32,16,896]{2,1,0:T(8,128)(2,1)S(1)}, u32[]{:S(2)}, u32[]{:S(2)}) %all-to-all-start.2) | async-done | bytes 917536 | tf_op jit(solution)/shard_map/all_to_all | solution.py:322
  164.3 1.2 copy-done.6
  165.5 3.3 %shard_map.97 = (bf16[128,3584]{1,0:T(8,128)(2,1)}, f32[8,1,512]{2,1,0:T(1,128)S(1)}) custom-call(bf16[8,4,16,896]{3,2,1,0:T(8,128)(2,1)S(1)} %bitcast.29, bf16[128,3584]{1,0:T(8,128)(2,1)S(1)} %copy-done.6, f32[1,3584]{1,0:T(1,128)S(1)} %broadcast_in_dim_reshape.3.gain_ref), custom_call_target="tpu_custom_call" | custom-call | flops 117440512 | bytes 2752512 | tf_op jit(solution)/shard_map/pallas_call | solution.py:217
  168.8 9.0 %all_to_all.27 = f32[8,1,512]{2,1,0:T(1,128)S(1)} all-to-all(f32[8,1,512]{2,1,0:T(1,128)S(1)} %get-tuple-element.28), channel_id=1, replica_groups=mesh['group'=2,'dp'=32,'mp'=8] {'mp'}, dimensions={0} | all-to-all | bytes 32768 | tf_op jit(solution)/shard_map/all_to_all | solution.py:327
  177.9 18.9 %all_to_all.28 = f32[64,1,512]{2,1,0:T(1,128)S(1)} all-to-all(f32[64,1,512]{2,1,0:T(1,128)S(1)} %broadcast_in_dim.16), channel_id=1, replica_groups=mesh['group'=2,'dp'=32,'mp'=8] {'group','dp'}, dimensions={0} | all-to-all | bytes 262144 | tf_op jit(solution)/shard_map/all_to_all | solution.py:330
  197.5 1.3 slice_divide_fusion
  (41 shorter events, 11.4 us)
Async XLA Ops:
  7.2 0.9 copy-start
  7.2 66.9 %copy-start.7 = (f32[4096]{0:T(1024)S(1)}, f32[4096]{0:T(1024)}, u32[]{:S(2)}) copy-start(f32[4096]{0:T(1024)} %param.8) | copy-start | bytes 49156
  7.2 105.9 %all-gather.2.cloned.1.call-start = ((), (), s32[]{:S(2)}) async-start(), calls=%async_computation.5 | async-start | bytes 4423680 | tf_op jit(solution)/shard_map/all_gather | solution.py:279
  8.1 7.2 %collective-permute-start = (bf16[224,128]{1,0:T(8,128)(2,1)S(1)}, bf16[224,128]{1,0:T(8,128)(2,1)S(1)}, u32[]{:S(2)}, u32[]{:S(2)}) collective-permute-start(bf16[224,128]{1,0:T(8,128)(2,1)S(1)} %dynamic-slice_bitcast_fusion), channel_id=1, source_target_pairs={{0,0},{1,256},{2,8},{3,264},{4,16},{5,272},{6,24},{7,280},{8,2},{9... | collective-permute-start | bytes 172040 | tf_op jit(solution)/shard_map/ppermute | solution.py:262
  44.5 29.6 %all-to-all-start.1 = ((bf16[8,128,512]{2,1,0:T(8,128)(2,1)}), bf16[8,128,512]{2,1,0:T(8,128)(2,1)S(1)}, u32[]{:S(2)}, u32[]{:S(2)}) async-start(bf16[8,128,512]{2,1,0:T(8,128)(2,1)} %bitcast.32), calls=%async_computation.1 | async-start | bytes 2097152 | tf_op jit(solution)/shard_map/all_to_all | solution.py:298
  74.7 13.0 %collective-permute-start.1 = (bf16[64,4096]{1,0:T(8,128)(2,1)S(1)}, bf16[64,4096]{1,0:T(8,128)(2,1)S(1)}, u32[]{:S(2)}, u32[]{:S(2)}) collective-permute-start(bf16[64,4096]{1,0:T(8,128)(2,1)S(1)} %get-tuple-element.18.refs_0_), channel_id=1, source_target_pairs={{0,8},{8,16},{16,24},{24,0},{32,40},{40,48},{48,56},{56,32},{64,72... | collective-permute-start | bytes 1572872 | tf_op jit(solution)/shard_map/ppermute | solution.py:239
  77.6 12.0 %collective-permute-start.4 = (bf16[64,4096]{1,0:T(8,128)(2,1)S(1)}, bf16[64,4096]{1,0:T(8,128)(2,1)S(1)}, u32[]{:S(2)}, u32[]{:S(2)}) collective-permute-start(bf16[64,4096]{1,0:T(8,128)(2,1)S(1)} %get-tuple-element.19.refs_1_), channel_id=1, source_target_pairs={{0,24},{8,0},{16,8},{24,16},{32,56},{40,32},{48,40},{56,48},{64,88... | collective-permute-start | bytes 1572872 | tf_op jit(solution)/shard_map/ppermute | solution.py:240
  81.2 18.9 %collective-permute-start.6 = (bf16[64,4096]{1,0:T(8,128)(2,1)S(1)}, bf16[64,4096]{1,0:T(8,128)(2,1)S(1)}, u32[]{:S(2)}, u32[]{:S(2)}) collective-permute-start(bf16[64,4096]{1,0:T(8,128)(2,1)S(1)} %get-tuple-element.18.refs_0_), channel_id=1, source_target_pairs={{0,24},{8,0},{16,8},{24,16},{32,56},{40,32},{48,40},{56,48},{64,88... | collective-permute-start | bytes 1572872 | tf_op jit(solution)/shard_map/ppermute | solution.py:242
  83.2 17.1 %collective-permute-start.2 = (bf16[64,4096]{1,0:T(8,128)(2,1)S(1)}, bf16[64,4096]{1,0:T(8,128)(2,1)S(1)}, u32[]{:S(2)}, u32[]{:S(2)}) collective-permute-start(bf16[64,4096]{1,0:T(8,128)(2,1)S(1)} %get-tuple-element.19.refs_1_), channel_id=1, source_target_pairs={{0,8},{8,16},{16,24},{24,0},{32,40},{40,48},{48,56},{56,32},{64,72... | collective-permute-start | bytes 1572872 | tf_op jit(solution)/shard_map/ppermute | solution.py:241
  87.7 23.8 %collective-permute-start.3 = (bf16[64,4096]{1,0:T(8,128)(2,1)S(1)}, bf16[64,4096]{1,0:T(8,128)(2,1)S(1)}, u32[]{:S(2)}, u32[]{:S(2)}) collective-permute-start(bf16[64,4096]{1,0:T(8,128)(2,1)S(1)} %collective-permute-done.1.refs_2_), channel_id=1, source_target_pairs={{0,8},{8,16},{16,24},{24,0},{32,40},{40,48},{48,56},{56,32},{64,72... | collective-permute-start | bytes 1572872 | tf_op jit(solution)/shard_map/ppermute | solution.py:243
  89.6 22.7 %collective-permute-start.5 = (bf16[64,4096]{1,0:T(8,128)(2,1)S(1)}, bf16[64,4096]{1,0:T(8,128)(2,1)S(1)}, u32[]{:S(2)}, u32[]{:S(2)}) collective-permute-start(bf16[64,4096]{1,0:T(8,128)(2,1)S(1)} %collective-permute-done.4.refs_7_), channel_id=1, source_target_pairs={{0,24},{8,0},{16,8},{24,16},{32,56},{40,32},{48,40},{56,48},{64,88... | collective-permute-start | bytes 1572872 | tf_op jit(solution)/shard_map/ppermute | solution.py:244
  111.5 0.8 copy-start.2
  112.3 0.8 copy-start.4
  113.1 12.9 %collective-permute-start.7 = (bf16[8,8,240,128]{3,2,1,0:T(8,128)(2,1)}, bf16[8,8,240,128]{3,2,1,0:T(8,128)(2,1)S(1)}, u32[]{:S(2)}, u32[]{:S(2)}) collective-permute-start(bf16[8,8,240,128]{3,2,1,0:T(8,128)(2,1)} %bitcast.27), channel_id=1, source_target_pairs={{0,256},{256,0},{1,257},{257,1},{2,258},{258,2},{3,259},{259,3},{4... | collective-permute-start | bytes 11796488 | tf_op jit(solution)/shard_map/ppermute | solution.py:315
  119.0 2.1 %copy-start.1 = (bf16[15360,128]{1,0:T(8,128)(2,1)S(1)}, bf16[15360,128]{1,0:T(8,128)(2,1)}, u32[]{:S(2)}) copy-start(bf16[15360,128]{1,0:T(8,128)(2,1)} %all-gather.2.cloned.1.call-done) | copy-start | bytes 11796484
  121.1 1.0 copy-start.3
  122.2 1.0 copy-start.5
  129.8 34.5 %all-to-all-start.2 = ((bf16[32,16,896]{2,1,0:T(8,128)(2,1)}), bf16[32,16,896]{2,1,0:T(8,128)(2,1)S(1)}, u32[]{:S(2)}, u32[]{:S(2)}) async-start(bf16[32,16,896]{2,1,0:T(8,128)(2,1)} %bitcast.12), calls=%async_computation.2 | async-start | bytes 1835008 | tf_op jit(solution)/shard_map/all_to_all | solution.py:322
  164.3 1.2 copy-start.6
Sparse Core Ops, SparseCore 0:
  44.6 52.1 all-gather.1

commit v7 on v6

--- a/solution.py
+++ b/solution.py
@@ -233,6 +233,27 @@
     )(received, hidden, gains[None, :])
 
 
+def last_kernel(share, width, parts_ref, gain_ref, loss_ref):
+    total = jnp.sum(parts_ref[...], axis=0)
+    tally = total[:, share + 1 : share + 2]
+    gain_ref[...] = total[:, :share] / tally
+    loss_ref[...] = total[:, share : share + 1] / (2.0 * tally * width)
+
+
+def last(parts, share, width):
+    in_vmem = pl.BlockSpec(memory_space=pltpu.VMEM)
+    return pl.pallas_call(
+        functools.partial(last_kernel, share, float(width)),
+        out_shape=(
+            jax.ShapeDtypeStruct((1, share), jnp.float32),
+            jax.ShapeDtypeStruct((1, 1), jnp.float32),
+        ),
+        in_specs=[in_vmem],
+        out_specs=(in_vmem, in_vmem),
+        compiler_params=pltpu.CompilerParams(vmem_limit_bytes=4 * MIB),
+    )(parts)
+
+
 def ring_gather(top, low, x_count, dp_count):
     forward = [(d, d - d % x_count + (d + 1) % x_count) for d in range(dp_count)]
     backward = [(d, d - d % x_count + (d - 1) % x_count) for d in range(dp_count)]
@@ -326,17 +347,15 @@
 
     over_mp = jnp.sum(lax.all_to_all(message, "mp", 0, 0, tiled=True), axis=(0, 1))
     peers = group_count * dp_count
-    totals = jnp.sum(
-        lax.all_to_all(
-            jnp.broadcast_to(over_mp[None, :], (peers, over_mp.shape[0])), ("group", "dp"), 0, 0, tiled=True
-        ),
-        axis=0,
-    )
-    square_sum = totals[share_width]
-    tally_sum = totals[share_width + 1]
-    grad_gain = totals[:share_width] / tally_sum
-    mean_loss = square_sum / (2.0 * tally_sum * width)
-    return (gradient, grad_gain, mean_loss)
+    parts = lax.all_to_all(
+        jnp.broadcast_to(over_mp[None, None, :], (peers, 1, over_mp.shape[0])),
+        ("group", "dp"),
+        0,
+        0,
+        tiled=True,
+    )
+    grad_gain, mean_loss = last(parts, share_width, width)
+    return (gradient, grad_gain.reshape(share_width), mean_loss.reshape(()))
 
 
 def solution(mesh):

time: 209 us -> 205 us (0.981)
  between operations: 16.7 us -> 14.2 us
where the time goes in v7:
time: 205 us; the launch traced here: 204 us
  waiting for transfers between devices  67 us (33%)
  blocking collectives  56.9 us (28%)
  starting transfers between devices  43 us (21%)
  between operations  14.2 us (7%)
  Pallas kernels  11.4 us (6%)
  local copies, waits for them, and re-layouts  8.84 us (4%)
  other arithmetic  3.1 us (2%)
    all_to_all x1, blocking collectives, projector_columns(): lax.all_to_all(jnp.broadcast_to(message[None], (mp_count,) + message.shap...  29 us
    all_to_all x1, waiting for transfers between devices, local(): moved = lax.all_to_all(blocks, 'mp', 0, 0, tiled=True)  23.8 us
    all_to_all x1, waiting for transfers between devices, local(): lax.all_to_all(buffer.reshape(dp_count, deep, quarter), 'dp', 0, 0, tiled...  23.6 us
    all_to_all x1, blocking collectives, local(): lax.all_to_all(jnp.broadcast_to(over_mp[None, None, :], (peers, 1, over_m...  18.9 us
    ppermute x1, waiting for transfers between devices, ring_gather(): far_top = lax.ppermute(left_top, 'dp', forward)  11.2 us
    all_to_all x1, starting transfers between devices, local(): lax.all_to_all(buffer.reshape(dp_count, deep, quarter), 'dp', 0, 0, tiled...  9.86 us
    all_to_all x1, blocking collectives, local(): lax.all_to_all(message, 'mp', 0, 0, tiled=True)  8.97 us
    unnamed x17, local copies, waits for them, and re-layouts  7.83 us
  transfers between devices with their start and end apart: 11, of which 7 were waited for; matrix products, arithmetic and copies ran while one was open for 2% of the time, Pallas kernels for 2%

profile of v7, /device:TPU:1, one launch (start us, length us, event | category | flops | bytes accessed | tf_op | source)
XLA Modules:
  0.0 204.4 jit_solution(16870245921714952939)
XLA Ops:
  8.1 5.4 %collective-permute-start = (bf16[224,128]{1,0:T(8,128)(2,1)S(1)}, bf16[224,128]{1,0:T(8,128)(2,1)S(1)}, u32[]{:S(2)}, u32[]{:S(2)}) collective-permute-start(bf16[224,128]{1,0:T(8,128)(2,1)S(1)} %dynamic-slice_bitcast_fusion), channel_id=1, source_target_pairs={{0,0},{1,256},{2,8},{3,264},{4,16},{5,272},{6,24},{7,280},{8,2},{9... | collective-permute-start | bytes 172040 | tf_op jit(solution)/shard_map/ppermute | solution.py:283
  14.2 1.1 collective-permute-done
  15.4 29.0 %all_to_all.25 = bf16[8,240,128]{2,1,0:T(8,128)(2,1)} all-to-all(bf16[8,240,128]{2,1,0:T(8,128)(2,1)S(1)} %broadcast_in_dim.13), channel_id=1, replica_groups=mesh['group'=2,'dp'=32,'mp'=8] {'mp'}, dimensions={0} | all-to-all | bytes 983040 | tf_op jit(solution)/shard_map/all_to_all | solution.py:293
  44.5 3.6 %all-to-all-start.1 = ((bf16[8,128,512]{2,1,0:T(8,128)(2,1)}), bf16[8,128,512]{2,1,0:T(8,128)(2,1)S(1)}, u32[]{:S(2)}, u32[]{:S(2)}) async-start(bf16[8,128,512]{2,1,0:T(8,128)(2,1)} %bitcast.32), calls=%async_computation.1 | async-start | bytes 2097152 | tf_op jit(solution)/shard_map/all_to_all | solution.py:319
  50.3 23.8 %all-to-all-done.1.moved_ref = bf16[8,128,512]{2,1,0:T(8,128)(2,1)S(1)} async-done(((bf16[8,128,512]{2,1,0:T(8,128)(2,1)}), bf16[8,128,512]{2,1,0:T(8,128)(2,1)S(1)}, u32[]{:S(2)}, u32[]{:S(2)}) %all-to-all-start.1) | async-done | bytes 1048608 | tf_op jit(solution)/shard_map/all_to_all | solution.py:319
  74.7 2.9 %collective-permute-start.1 = (bf16[64,4096]{1,0:T(8,128)(2,1)S(1)}, bf16[64,4096]{1,0:T(8,128)(2,1)S(1)}, u32[]{:S(2)}, u32[]{:S(2)}) collective-permute-start(bf16[64,4096]{1,0:T(8,128)(2,1)S(1)} %get-tuple-element.20.refs_0_), channel_id=1, source_target_pairs={{0,8},{8,16},{16,24},{24,0},{32,40},{40,48},{48,56},{56,32},{64,72... | collective-permute-start | bytes 1572872 | tf_op jit(solution)/shard_map/ppermute | solution.py:260
  77.6 3.6 %collective-permute-start.4 = (bf16[64,4096]{1,0:T(8,128)(2,1)S(1)}, bf16[64,4096]{1,0:T(8,128)(2,1)S(1)}, u32[]{:S(2)}, u32[]{:S(2)}) collective-permute-start(bf16[64,4096]{1,0:T(8,128)(2,1)S(1)} %get-tuple-element.21.refs_1_), channel_id=1, source_target_pairs={{0,24},{8,0},{16,8},{24,16},{32,56},{40,32},{48,40},{56,48},{64,88... | collective-permute-start | bytes 1572872 | tf_op jit(solution)/shard_map/ppermute | solution.py:261
  81.2 1.9 collective-permute-start.6
  83.2 3.4 %collective-permute-start.2 = (bf16[64,4096]{1,0:T(8,128)(2,1)S(1)}, bf16[64,4096]{1,0:T(8,128)(2,1)S(1)}, u32[]{:S(2)}, u32[]{:S(2)}) collective-permute-start(bf16[64,4096]{1,0:T(8,128)(2,1)S(1)} %get-tuple-element.21.refs_1_), channel_id=1, source_target_pairs={{0,8},{8,16},{16,24},{24,0},{32,40},{40,48},{48,56},{56,32},{64,72... | collective-permute-start | bytes 1572872 | tf_op jit(solution)/shard_map/ppermute | solution.py:262
  86.5 1.2 collective-permute-done.1.refs_2_
  87.7 1.9 collective-permute-start.3
  89.6 4.6 %collective-permute-start.5 = (bf16[64,4096]{1,0:T(8,128)(2,1)S(1)}, bf16[64,4096]{1,0:T(8,128)(2,1)S(1)}, u32[]{:S(2)}, u32[]{:S(2)}) collective-permute-start(bf16[64,4096]{1,0:T(8,128)(2,1)S(1)} %collective-permute-done.4.refs_7_), channel_id=1, source_target_pairs={{0,24},{8,0},{16,8},{24,16},{32,56},{40,32},{48,40},{56,48},{64,88... | collective-permute-start | bytes 1572872 | tf_op jit(solution)/shard_map/ppermute | solution.py:265
  94.2 5.9 %collective-permute-done.6.refs_6_ = bf16[64,4096]{1,0:T(8,128)(2,1)S(1)} collective-permute-done((bf16[64,4096]{1,0:T(8,128)(2,1)S(1)}, bf16[64,4096]{1,0:T(8,128)(2,1)S(1)}, u32[]{:S(2)}, u32[]{:S(2)}) %collective-permute-start.6) | collective-permute-done | bytes 524320 | tf_op jit(solution)/shard_map/ppermute | solution.py:263
  100.3 11.2 %collective-permute-done.3.refs_4_ = bf16[64,4096]{1,0:T(8,128)(2,1)S(1)} collective-permute-done((bf16[64,4096]{1,0:T(8,128)(2,1)S(1)}, bf16[64,4096]{1,0:T(8,128)(2,1)S(1)}, u32[]{:S(2)}, u32[]{:S(2)}) %collective-permute-start.3) | collective-permute-done | bytes 524320 | tf_op jit(solution)/shard_map/ppermute | solution.py:264
  113.1 5.9 %collective-permute-start.7 = (bf16[8,8,240,128]{3,2,1,0:T(8,128)(2,1)}, bf16[8,8,240,128]{3,2,1,0:T(8,128)(2,1)S(1)}, u32[]{:S(2)}, u32[]{:S(2)}) collective-permute-start(bf16[8,8,240,128]{3,2,1,0:T(8,128)(2,1)} %bitcast.27), channel_id=1, source_target_pairs={{0,256},{256,0},{1,257},{257,1},{2,258},{258,2},{3,259},{259,3},{4... | collective-permute-start | bytes 11796488 | tf_op jit(solution)/shard_map/ppermute | solution.py:336
  119.0 2.1 %copy-done.1 = bf16[15360,128]{1,0:T(8,128)(2,1)S(1)} copy-done((bf16[15360,128]{1,0:T(8,128)(2,1)S(1)}, bf16[15360,128]{1,0:T(8,128)(2,1)}, u32[]{:S(2)}) %copy-start.1) | copy-done | bytes 3932184
  123.2 2.7 %shard_map.95.first_ref = bf16[512,448]{1,0:T(8,128)(2,1)S(1)} custom-call(bf16[64,4096]{1,0:T(8,128)(2,1)S(1)} %get-tuple-element.20.refs_0_, bf16[64,4096]{1,0:T(8,128)(2,1)S(1)} %get-tuple-element.21.refs_1_, bf16[64,4096]{1,0:T(8,128)(2,1)S(1)} %collective-permute-done.1.refs_2_, bf16[64,4096]{1,0:T(8,128)(2,1)S(1)} %collective-permute-done.2.refs_3_, ...), custom_call_target="tpu_custom_call" | custom-call | flops 1879048192 | bytes 7864320 | tf_op jit(solution)/shard_map/pallas_call | solution.py:136
  126.0 3.9 %shard_map.96 = bf16[512,896]{1,0:T(8,128)(2,1)} custom-call(s32[1]{0:T(128)} %bitcast.core_ref, bf16[512,448]{1,0:T(8,128)(2,1)S(1)} %shard_map.95.first_ref, bf16[64,4096]{1,0:T(8,128)(2,1)S(1)} %get-tuple-element.20.refs_0_, bf16[64,4096]{1,0:T(8,128)(2,1)S(1)} %get-tuple-element.21.refs_1_, bf16[64,4096]{1,0:T(8,128)(2,1)S(1)} %collective-permute-done.1.refs_2_, ...), custom_call_target="tpu_custom_call" | custom-call | flops 1879048192 | bytes 7864320 | tf_op jit(solution)/shard_map/pallas_call | solution.py:136
  129.9 9.9 %all-to-all-start.2 = ((bf16[32,16,896]{2,1,0:T(8,128)(2,1)}), bf16[32,16,896]{2,1,0:T(8,128)(2,1)S(1)}, u32[]{:S(2)}, u32[]{:S(2)}) async-start(bf16[32,16,896]{2,1,0:T(8,128)(2,1)} %bitcast.12), calls=%async_computation.2 | async-start | bytes 1835008 | tf_op jit(solution)/shard_map/all_to_all | solution.py:343
  140.7 23.6 %all-to-all-done.2 = bf16[32,16,896]{2,1,0:T(8,128)(2,1)S(1)} async-done(((bf16[32,16,896]{2,1,0:T(8,128)(2,1)}), bf16[32,16,896]{2,1,0:T(8,128)(2,1)S(1)}, u32[]{:S(2)}, u32[]{:S(2)}) %all-to-all-start.2) | async-done | bytes 917536 | tf_op jit(solution)/shard_map/all_to_all | solution.py:343
  164.3 1.2 copy-done.6
  165.5 3.3 %shard_map.97 = (bf16[128,3584]{1,0:T(8,128)(2,1)}, f32[8,1,512]{2,1,0:T(1,128)S(1)}) custom-call(bf16[8,4,16,896]{3,2,1,0:T(8,128)(2,1)S(1)} %bitcast.29, bf16[128,3584]{1,0:T(8,128)(2,1)S(1)} %copy-done.6, f32[1,3584]{1,0:T(1,128)S(1)} %broadcast_in_dim_reshape.3.gain_ref), custom_call_target="tpu_custom_call" | custom-call | flops 117440512 | bytes 2752512 | tf_op jit(solution)/shard_map/pallas_call | solution.py:217
  168.8 9.0 %all_to_all.26 = f32[8,1,512]{2,1,0:T(1,128)S(1)} all-to-all(f32[8,1,512]{2,1,0:T(1,128)S(1)} %get-tuple-element.30), channel_id=1, replica_groups=mesh['group'=2,'dp'=32,'mp'=8] {'mp'}, dimensions={0} | all-to-all | bytes 32768 | tf_op jit(solution)/shard_map/all_to_all | solution.py:348
  177.9 18.9 %all_to_all.27.parts_ref = f32[64,1,512]{2,1,0:T(1,128)S(1)} all-to-all(f32[64,1,512]{2,1,0:T(1,128)S(1)} %broadcast_in_dim.16), channel_id=1, replica_groups=mesh['group'=2,'dp'=32,'mp'=8] {'group','dp'}, dimensions={0} | all-to-all | bytes 262144 | tf_op jit(solution)/shard_map/all_to_all | solution.py:350
  (39 shorter events, 10.3 us)
Async XLA Ops:
  7.2 0.9 copy-start
  7.2 66.9 %copy-start.7 = (f32[4096]{0:T(1024)S(1)}, f32[4096]{0:T(1024)}, u32[]{:S(2)}) copy-start(f32[4096]{0:T(1024)} %param.8) | copy-start | bytes 49156
  7.2 105.9 %all-gather.2.cloned.1.call-start = ((), (), s32[]{:S(2)}) async-start(), calls=%async_computation.5 | async-start | bytes 4423680 | tf_op jit(solution)/shard_map/all_gather | solution.py:300
  8.1 7.2 %collective-permute-start = (bf16[224,128]{1,0:T(8,128)(2,1)S(1)}, bf16[224,128]{1,0:T(8,128)(2,1)S(1)}, u32[]{:S(2)}, u32[]{:S(2)}) collective-permute-start(bf16[224,128]{1,0:T(8,128)(2,1)S(1)} %dynamic-slice_bitcast_fusion), channel_id=1, source_target_pairs={{0,0},{1,256},{2,8},{3,264},{4,16},{5,272},{6,24},{7,280},{8,2},{9... | collective-permute-start | bytes 172040 | tf_op jit(solution)/shard_map/ppermute | solution.py:283
  44.5 29.6 %all-to-all-start.1 = ((bf16[8,128,512]{2,1,0:T(8,128)(2,1)}), bf16[8,128,512]{2,1,0:T(8,128)(2,1)S(1)}, u32[]{:S(2)}, u32[]{:S(2)}) async-start(bf16[8,128,512]{2,1,0:T(8,128)(2,1)} %bitcast.32), calls=%async_computation.1 | async-start | bytes 2097152 | tf_op jit(solution)/shard_map/all_to_all | solution.py:319
  74.7 13.0 %collective-permute-start.1 = (bf16[64,4096]{1,0:T(8,128)(2,1)S(1)}, bf16[64,4096]{1,0:T(8,128)(2,1)S(1)}, u32[]{:S(2)}, u32[]{:S(2)}) collective-permute-start(bf16[64,4096]{1,0:T(8,128)(2,1)S(1)} %get-tuple-element.20.refs_0_), channel_id=1, source_target_pairs={{0,8},{8,16},{16,24},{24,0},{32,40},{40,48},{48,56},{56,32},{64,72... | collective-permute-start | bytes 1572872 | tf_op jit(solution)/shard_map/ppermute | solution.py:260
  77.6 12.0 %collective-permute-start.4 = (bf16[64,4096]{1,0:T(8,128)(2,1)S(1)}, bf16[64,4096]{1,0:T(8,128)(2,1)S(1)}, u32[]{:S(2)}, u32[]{:S(2)}) collective-permute-start(bf16[64,4096]{1,0:T(8,128)(2,1)S(1)} %get-tuple-element.21.refs_1_), channel_id=1, source_target_pairs={{0,24},{8,0},{16,8},{24,16},{32,56},{40,32},{48,40},{56,48},{64,88... | collective-permute-start | bytes 1572872 | tf_op jit(solution)/shard_map/ppermute | solution.py:261
  81.2 18.9 %collective-permute-start.6 = (bf16[64,4096]{1,0:T(8,128)(2,1)S(1)}, bf16[64,4096]{1,0:T(8,128)(2,1)S(1)}, u32[]{:S(2)}, u32[]{:S(2)}) collective-permute-start(bf16[64,4096]{1,0:T(8,128)(2,1)S(1)} %get-tuple-element.20.refs_0_), channel_id=1, source_target_pairs={{0,24},{8,0},{16,8},{24,16},{32,56},{40,32},{48,40},{56,48},{64,88... | collective-permute-start | bytes 1572872 | tf_op jit(solution)/shard_map/ppermute | solution.py:263
  83.2 17.1 %collective-permute-start.2 = (bf16[64,4096]{1,0:T(8,128)(2,1)S(1)}, bf16[64,4096]{1,0:T(8,128)(2,1)S(1)}, u32[]{:S(2)}, u32[]{:S(2)}) collective-permute-start(bf16[64,4096]{1,0:T(8,128)(2,1)S(1)} %get-tuple-element.21.refs_1_), channel_id=1, source_target_pairs={{0,8},{8,16},{16,24},{24,0},{32,40},{40,48},{48,56},{56,32},{64,72... | collective-permute-start | bytes 1572872 | tf_op jit(solution)/shard_map/ppermute | solution.py:262
  87.7 23.8 %collective-permute-start.3 = (bf16[64,4096]{1,0:T(8,128)(2,1)S(1)}, bf16[64,4096]{1,0:T(8,128)(2,1)S(1)}, u32[]{:S(2)}, u32[]{:S(2)}) collective-permute-start(bf16[64,4096]{1,0:T(8,128)(2,1)S(1)} %collective-permute-done.1.refs_2_), channel_id=1, source_target_pairs={{0,8},{8,16},{16,24},{24,0},{32,40},{40,48},{48,56},{56,32},{64,72... | collective-permute-start | bytes 1572872 | tf_op jit(solution)/shard_map/ppermute | solution.py:264
  89.6 22.7 %collective-permute-start.5 = (bf16[64,4096]{1,0:T(8,128)(2,1)S(1)}, bf16[64,4096]{1,0:T(8,128)(2,1)S(1)}, u32[]{:S(2)}, u32[]{:S(2)}) collective-permute-start(bf16[64,4096]{1,0:T(8,128)(2,1)S(1)} %collective-permute-done.4.refs_7_), channel_id=1, source_target_pairs={{0,24},{8,0},{16,8},{24,16},{32,56},{40,32},{48,40},{56,48},{64,88... | collective-permute-start | bytes 1572872 | tf_op jit(solution)/shard_map/ppermute | solution.py:265
  111.5 0.8 copy-start.2
  112.3 0.8 copy-start.4
  113.1 12.9 %collective-permute-start.7 = (bf16[8,8,240,128]{3,2,1,0:T(8,128)(2,1)}, bf16[8,8,240,128]{3,2,1,0:T(8,128)(2,1)S(1)}, u32[]{:S(2)}, u32[]{:S(2)}) collective-permute-start(bf16[8,8,240,128]{3,2,1,0:T(8,128)(2,1)} %bitcast.27), channel_id=1, source_target_pairs={{0,256},{256,0},{1,257},{257,1},{2,258},{258,2},{3,259},{259,3},{4... | collective-permute-start | bytes 11796488 | tf_op jit(solution)/shard_map/ppermute | solution.py:336
  119.0 2.1 %copy-start.1 = (bf16[15360,128]{1,0:T(8,128)(2,1)S(1)}, bf16[15360,128]{1,0:T(8,128)(2,1)}, u32[]{:S(2)}) copy-start(bf16[15360,128]{1,0:T(8,128)(2,1)} %all-gather.2.cloned.1.call-done) | copy-start | bytes 11796484
  121.1 1.0 copy-start.3
  122.2 1.0 copy-start.5
  129.9 34.5 %all-to-all-start.2 = ((bf16[32,16,896]{2,1,0:T(8,128)(2,1)}), bf16[32,16,896]{2,1,0:T(8,128)(2,1)S(1)}, u32[]{:S(2)}, u32[]{:S(2)}) async-start(bf16[32,16,896]{2,1,0:T(8,128)(2,1)} %bitcast.12), calls=%async_computation.2 | async-start | bytes 1835008 | tf_op jit(solution)/shard_map/all_to_all | solution.py:343
  164.3 1.2 copy-start.6
Sparse Core Ops, SparseCore 0:
  44.6 52.1 all-gather.1

commit v8 on v7

--- a/solution.py
+++ b/solution.py
@@ -150,18 +150,46 @@
     )(*((core, first) if joined else ()), *pieces, weights)
 
 
-def finish_kernel(
-    mp_count, received_ref, hidden_ref, gain_ref, gradient_ref, message_ref, weighted_sum, gain_sum
-):
-    y_count, x_count, deep, quarter = received_ref.shape
+def student_kernel(hidden_ref, normal_ref, rms_ref):
     rows, width = hidden_ref.shape
-    capacity = deep // x_count
-    spans = [slice(x * quarter, (x + 1) * quarter) for x in range(x_count)]
+    quarter = width // 4
+    spans = [slice(x * quarter, (x + 1) * quarter) for x in range(4)]
     total = jnp.zeros((rows, 1), jnp.float32)
     for span in spans:
         values = hidden_ref[:, span].astype(jnp.float32)
         total += jnp.sum(values * values, axis=1, keepdims=True)
     inverse_rms = lax.rsqrt(total * (1.0 / width) + EPSILON)
+    for span in spans:
+        normal_ref[:, span] = hidden_ref[:, span].astype(jnp.float32) * inverse_rms
+    rms_ref[...] = jnp.broadcast_to(inverse_rms, rms_ref.shape)
+
+
+def student_rows(hidden):
+    rows, width = hidden.shape
+    in_vmem = pl.BlockSpec(memory_space=pltpu.VMEM)
+    return pl.pallas_call(
+        student_kernel,
+        out_shape=(
+            jax.ShapeDtypeStruct((rows, width), jnp.float32),
+            jax.ShapeDtypeStruct((rows, 128), jnp.float32),
+        ),
+        in_specs=[in_vmem],
+        out_specs=(in_vmem, in_vmem),
+        compiler_params=pltpu.CompilerParams(vmem_limit_bytes=16 * MIB),
+        cost_estimate=pl.CostEstimate(
+            flops=4 * rows * width, bytes_accessed=6 * rows * width, transcendentals=rows
+        ),
+    )(hidden)
+
+
+def finish_kernel(
+    mp_count, received_ref, normal_ref, rms_ref, gain_ref, gradient_ref, message_ref, weighted_sum, gain_sum
+):
+    y_count, x_count, deep, quarter = received_ref.shape
+    rows, width = normal_ref.shape
+    capacity = deep // x_count
+    spans = [slice(x * quarter, (x + 1) * quarter) for x in range(x_count)]
+    inverse_rms = rms_ref[:, 0:1]
     to = lax.broadcasted_iota(jnp.int32, (rows, rows), 0)
     source = lax.broadcasted_iota(jnp.int32, (rows, rows), 1)
 
@@ -188,7 +216,7 @@
             chooser, block, (((0,), (0,)), ((), ())), preferred_element_type=jnp.float32
         )
         gain = gain_ref[:, span]
-        normal = hidden_ref[:, span].astype(jnp.float32) * inverse_rms
+        normal = normal_ref[:, span]
         mismatch = (normal * gain - target) * filled
         weighted = mismatch * gain
         weighted_sum[:, span] = weighted
@@ -197,7 +225,7 @@
         gain_sum[:, span] = jnp.sum(mismatch * normal, axis=0, keepdims=True)
     row_mean = row_terms * (1.0 / width)
     for span in spans:
-        normal = hidden_ref[:, span].astype(jnp.float32) * inverse_rms
+        normal = normal_ref[:, span]
         gradient_ref[:, span] = (
             inverse_rms * (weighted_sum[:, span] - normal * row_mean)
         ).astype(jnp.bfloat16)
@@ -210,8 +238,8 @@
         message_ref[m, :, share:] = tail
 
 
-def finish(received, hidden, gains, mp_count):
-    rows, width = hidden.shape
+def finish(received, normal, inverse_rms, gains, mp_count):
+    rows, width = normal.shape
     share = width // mp_count
     in_vmem = pl.BlockSpec(memory_space=pltpu.VMEM)
     return pl.pallas_call(
@@ -220,7 +248,7 @@
             jax.ShapeDtypeStruct((rows, width), jnp.bfloat16),
             jax.ShapeDtypeStruct((mp_count, 1, share + 64), jnp.float32),
         ),
-        in_specs=[in_vmem] * 3,
+        in_specs=[in_vmem] * 4,
         out_specs=(in_vmem, in_vmem),
         scratch_shapes=[
             pltpu.VMEM((rows, width), jnp.float32),
@@ -230,7 +258,7 @@
         cost_estimate=pl.CostEstimate(
             flops=2 * rows * rows * width, bytes_accessed=6 * rows * width, transcendentals=rows
         ),
-    )(received, hidden, gains[None, :])
+    )(received, normal, inverse_rms, gains[None, :])
 
 
 def last_kernel(share, width, parts_ref, gain_ref, loss_ref):
@@ -343,7 +371,9 @@
     received = lax.all_to_all(
         buffer.reshape(dp_count, deep, quarter), "dp", 0, 0, tiled=True
     ).reshape(y_count, x_count, deep, quarter)
-    gradient, message = finish(received, student_hidden, gains, mp_count)
+    hidden, _ = lax.optimization_barrier((student_hidden, buffer))
+    normal, inverse_rms = student_rows(hidden)
+    gradient, message = finish(received, normal, inverse_rms, gains, mp_count)
 
     over_mp = jnp.sum(lax.all_to_all(message, "mp", 0, 0, tiled=True), axis=(0, 1))
     peers = group_count * dp_count

time: 205 us -> 203 us (level)
  no operation moved by 1% of the time
where the time goes in v8:
time: 203 us
  waiting for transfers between devices  65.4 us (32%)
  blocking collectives  56.9 us (28%)
  starting transfers between devices  43 us (21%)
  between operations  14.2 us (7%)
  Pallas kernels  11.1 us (5%)
  local copies, waits for them, and re-layouts  8.83 us (4%)
  other arithmetic  3.1 us (2%)
    all_to_all x1, blocking collectives, projector_columns(): lax.all_to_all(jnp.broadcast_to(message[None], (mp_count,) + message.shap...  29 us
    all_to_all x1, waiting for transfers between devices, local(): moved = lax.all_to_all(blocks, 'mp', 0, 0, tiled=True)  23.8 us
    all_to_all x1, waiting for transfers between devices, local(): lax.all_to_all(buffer.reshape(dp_count, deep, quarter), 'dp', 0, 0, tiled...  22.1 us
    all_to_all x1, blocking collectives, local(): lax.all_to_all(jnp.broadcast_to(over_mp[None, None, :], (peers, 1, over_m...  18.9 us
    ppermute x1, waiting for transfers between devices, ring_gather(): far_top = lax.ppermute(left_top, 'dp', forward)  11.2 us
    all_to_all x1, starting transfers between devices, local(): lax.all_to_all(buffer.reshape(dp_count, deep, quarter), 'dp', 0, 0, tiled...  9.86 us
    all_to_all x1, blocking collectives, local(): lax.all_to_all(message, 'mp', 0, 0, tiled=True)  8.97 us
    unnamed x17, local copies, waits for them, and re-layouts  7.82 us
  transfers between devices with their start and end apart: 11, of which 7 were waited for; matrix products, arithmetic and copies ran while one was open for 2% of the time, Pallas kernels for 2%

profile of v8, /device:TPU:1, one launch (start us, length us, event | category | flops | bytes accessed | tf_op | source)
XLA Modules:
  0.0 202.5 jit_solution(932041330074962674)
XLA Ops:
  8.1 5.4 %collective-permute-start = (bf16[224,128]{1,0:T(8,128)(2,1)S(1)}, bf16[224,128]{1,0:T(8,128)(2,1)S(1)}, u32[]{:S(2)}, u32[]{:S(2)}) collective-permute-start(bf16[224,128]{1,0:T(8,128)(2,1)S(1)} %dynamic-slice_bitcast_fusion), channel_id=1, source_target_pairs={{0,0},{1,256},{2,8},{3,264},{4,16},{5,272},{6,24},{7,280},{8,2},{9... | collective-permute-start | bytes 172040 | tf_op jit(solution)/shard_map/ppermute | solution.py:311
  14.2 1.1 collective-permute-done
  15.4 29.0 %all_to_all.25 = bf16[8,240,128]{2,1,0:T(8,128)(2,1)} all-to-all(bf16[8,240,128]{2,1,0:T(8,128)(2,1)S(1)} %broadcast_in_dim.13), channel_id=1, replica_groups=mesh['group'=2,'dp'=32,'mp'=8] {'mp'}, dimensions={0} | all-to-all | bytes 983040 | tf_op jit(solution)/shard_map/all_to_all | solution.py:321
  44.5 3.6 %all-to-all-start.1 = ((bf16[8,128,512]{2,1,0:T(8,128)(2,1)}), bf16[8,128,512]{2,1,0:T(8,128)(2,1)S(1)}, u32[]{:S(2)}, u32[]{:S(2)}) async-start(bf16[8,128,512]{2,1,0:T(8,128)(2,1)} %bitcast.32), calls=%async_computation.1 | async-start | bytes 2097152 | tf_op jit(solution)/shard_map/all_to_all | solution.py:347
  50.3 23.8 %all-to-all-done.1.moved_ref = bf16[8,128,512]{2,1,0:T(8,128)(2,1)S(1)} async-done(((bf16[8,128,512]{2,1,0:T(8,128)(2,1)}), bf16[8,128,512]{2,1,0:T(8,128)(2,1)S(1)}, u32[]{:S(2)}, u32[]{:S(2)}) %all-to-all-start.1) | async-done | bytes 1048608 | tf_op jit(solution)/shard_map/all_to_all | solution.py:347
  74.7 2.9 %collective-permute-start.1 = (bf16[64,4096]{1,0:T(8,128)(2,1)S(1)}, bf16[64,4096]{1,0:T(8,128)(2,1)S(1)}, u32[]{:S(2)}, u32[]{:S(2)}) collective-permute-start(bf16[64,4096]{1,0:T(8,128)(2,1)S(1)} %get-tuple-element.23.refs_0_), channel_id=1, source_target_pairs={{0,8},{8,16},{16,24},{24,0},{32,40},{40,48},{48,56},{56,32},{64,72... | collective-permute-start | bytes 1572872 | tf_op jit(solution)/shard_map/ppermute | solution.py:288
  77.6 3.6 %collective-permute-start.4 = (bf16[64,4096]{1,0:T(8,128)(2,1)S(1)}, bf16[64,4096]{1,0:T(8,128)(2,1)S(1)}, u32[]{:S(2)}, u32[]{:S(2)}) collective-permute-start(bf16[64,4096]{1,0:T(8,128)(2,1)S(1)} %get-tuple-element.24.refs_1_), channel_id=1, source_target_pairs={{0,24},{8,0},{16,8},{24,16},{32,56},{40,32},{48,40},{56,48},{64,88... | collective-permute-start | bytes 1572872 | tf_op jit(solution)/shard_map/ppermute | solution.py:289
  81.2 1.9 collective-permute-start.6
  83.2 3.4 %collective-permute-start.2 = (bf16[64,4096]{1,0:T(8,128)(2,1)S(1)}, bf16[64,4096]{1,0:T(8,128)(2,1)S(1)}, u32[]{:S(2)}, u32[]{:S(2)}) collective-permute-start(bf16[64,4096]{1,0:T(8,128)(2,1)S(1)} %get-tuple-element.24.refs_1_), channel_id=1, source_target_pairs={{0,8},{8,16},{16,24},{24,0},{32,40},{40,48},{48,56},{56,32},{64,72... | collective-permute-start | bytes 1572872 | tf_op jit(solution)/shard_map/ppermute | solution.py:290
  86.5 1.2 collective-permute-done.1.refs_2_
  87.7 1.9 collective-permute-start.3
  89.6 4.6 %collective-permute-start.5 = (bf16[64,4096]{1,0:T(8,128)(2,1)S(1)}, bf16[64,4096]{1,0:T(8,128)(2,1)S(1)}, u32[]{:S(2)}, u32[]{:S(2)}) collective-permute-start(bf16[64,4096]{1,0:T(8,128)(2,1)S(1)} %collective-permute-done.4.refs_7_), channel_id=1, source_target_pairs={{0,24},{8,0},{16,8},{24,16},{32,56},{40,32},{48,40},{56,48},{64,88... | collective-permute-start | bytes 1572872 | tf_op jit(solution)/shard_map/ppermute | solution.py:293
  94.2 5.9 %collective-permute-done.6.refs_6_ = bf16[64,4096]{1,0:T(8,128)(2,1)S(1)} collective-permute-done((bf16[64,4096]{1,0:T(8,128)(2,1)S(1)}, bf16[64,4096]{1,0:T(8,128)(2,1)S(1)}, u32[]{:S(2)}, u32[]{:S(2)}) %collective-permute-start.6) | collective-permute-done | bytes 524320 | tf_op jit(solution)/shard_map/ppermute | solution.py:291
  100.3 11.2 %collective-permute-done.3.refs_4_ = bf16[64,4096]{1,0:T(8,128)(2,1)S(1)} collective-permute-done((bf16[64,4096]{1,0:T(8,128)(2,1)S(1)}, bf16[64,4096]{1,0:T(8,128)(2,1)S(1)}, u32[]{:S(2)}, u32[]{:S(2)}) %collective-permute-start.3) | collective-permute-done | bytes 524320 | tf_op jit(solution)/shard_map/ppermute | solution.py:292
  113.1 5.9 %collective-permute-start.7 = (bf16[8,8,240,128]{3,2,1,0:T(8,128)(2,1)}, bf16[8,8,240,128]{3,2,1,0:T(8,128)(2,1)S(1)}, u32[]{:S(2)}, u32[]{:S(2)}) collective-permute-start(bf16[8,8,240,128]{3,2,1,0:T(8,128)(2,1)} %bitcast.27), channel_id=1, source_target_pairs={{0,256},{256,0},{1,257},{257,1},{2,258},{258,2},{3,259},{259,3},{4... | collective-permute-start | bytes 11796488 | tf_op jit(solution)/shard_map/ppermute | solution.py:364
  119.0 2.1 %copy-done.1 = bf16[15360,128]{1,0:T(8,128)(2,1)S(1)} copy-done((bf16[15360,128]{1,0:T(8,128)(2,1)S(1)}, bf16[15360,128]{1,0:T(8,128)(2,1)}, u32[]{:S(2)}) %copy-start.1) | copy-done | bytes 3932184
  123.2 2.7 %shard_map.95.first_ref = bf16[512,448]{1,0:T(8,128)(2,1)S(1)} custom-call(bf16[64,4096]{1,0:T(8,128)(2,1)S(1)} %get-tuple-element.23.refs_0_, bf16[64,4096]{1,0:T(8,128)(2,1)S(1)} %get-tuple-element.24.refs_1_, bf16[64,4096]{1,0:T(8,128)(2,1)S(1)} %collective-permute-done.1.refs_2_, bf16[64,4096]{1,0:T(8,128)(2,1)S(1)} %collective-permute-done.2.refs_3_, ...), custom_call_target="tpu_custom_call" | custom-call | flops 1879048192 | bytes 7864320 | tf_op jit(solution)/shard_map/pallas_call | solution.py:136
  126.0 3.9 %shard_map.96 = bf16[512,896]{1,0:T(8,128)(2,1)} custom-call(s32[1]{0:T(128)} %bitcast.core_ref, bf16[512,448]{1,0:T(8,128)(2,1)S(1)} %shard_map.95.first_ref, bf16[64,4096]{1,0:T(8,128)(2,1)S(1)} %get-tuple-element.23.refs_0_, bf16[64,4096]{1,0:T(8,128)(2,1)S(1)} %get-tuple-element.24.refs_1_, bf16[64,4096]{1,0:T(8,128)(2,1)S(1)} %collective-permute-done.1.refs_2_, ...), custom_call_target="tpu_custom_call" | custom-call | flops 1879048192 | bytes 7864320 | tf_op jit(solution)/shard_map/pallas_call | solution.py:136
  129.8 9.9 %all-to-all-start.2 = ((bf16[32,16,896]{2,1,0:T(8,128)(2,1)}), bf16[32,16,896]{2,1,0:T(8,128)(2,1)S(1)}, u32[]{:S(2)}, u32[]{:S(2)}) async-start(bf16[32,16,896]{2,1,0:T(8,128)(2,1)} %bitcast.12), calls=%async_computation.2 | async-start | bytes 1835008 | tf_op jit(solution)/shard_map/all_to_all | solution.py:371
  140.7 1.2 copy-done.6
  142.2 22.1 %all-to-all-done.2 = bf16[32,16,896]{2,1,0:T(8,128)(2,1)S(1)} async-done(((bf16[32,16,896]{2,1,0:T(8,128)(2,1)}), bf16[32,16,896]{2,1,0:T(8,128)(2,1)S(1)}, u32[]{:S(2)}, u32[]{:S(2)}) %all-to-all-start.2) | async-done | bytes 917536 | tf_op jit(solution)/shard_map/all_to_all | solution.py:371
  164.3 2.7 %shard_map.98 = (bf16[128,3584]{1,0:T(8,128)(2,1)}, f32[8,1,512]{2,1,0:T(1,128)S(1)}) custom-call(bf16[8,4,16,896]{3,2,1,0:T(8,128)(2,1)S(1)} %bitcast.29, f32[128,3584]{1,0:T(8,128)S(1)} %get-tuple-element.33.normal_ref, f32[128,128]{1,0:T(8,128)S(1)} %get-tuple-element.34.rms_ref, f32[1,3584]{1,0:T(1,128)S(1)} %broadcast_in_dim_reshape.3.gain_ref), custom_call_target="tpu_custom_call" | custom-call | flops 117440512 | bytes 2752512 | tf_op jit(solution)/shard_map/pallas_call | solution.py:245
  167.0 9.0 %all_to_all.26 = f32[8,1,512]{2,1,0:T(1,128)S(1)} all-to-all(f32[8,1,512]{2,1,0:T(1,128)S(1)} %get-tuple-element.36), channel_id=1, replica_groups=mesh['group'=2,'dp'=32,'mp'=8] {'mp'}, dimensions={0} | all-to-all | bytes 32768 | tf_op jit(solution)/shard_map/all_to_all | solution.py:378
  176.1 18.9 %all_to_all.27.parts_ref = f32[64,1,512]{2,1,0:T(1,128)S(1)} all-to-all(f32[64,1,512]{2,1,0:T(1,128)S(1)} %broadcast_in_dim.16), channel_id=1, replica_groups=mesh['group'=2,'dp'=32,'mp'=8] {'group','dp'}, dimensions={0} | all-to-all | bytes 262144 | tf_op jit(solution)/shard_map/all_to_all | solution.py:380
  (40 shorter events, 10.6 us)
Async XLA Ops:
  7.2 0.9 copy-start
  7.2 66.9 %copy-start.7 = (f32[4096]{0:T(1024)S(1)}, f32[4096]{0:T(1024)}, u32[]{:S(2)}) copy-start(f32[4096]{0:T(1024)} %param.8) | copy-start | bytes 49156
  7.2 105.9 %all-gather.2.cloned.1.call-start = ((), (), s32[]{:S(2)}) async-start(), calls=%async_computation.5 | async-start | bytes 4423680 | tf_op jit(solution)/shard_map/all_gather | solution.py:328
  8.1 7.2 %collective-permute-start = (bf16[224,128]{1,0:T(8,128)(2,1)S(1)}, bf16[224,128]{1,0:T(8,128)(2,1)S(1)}, u32[]{:S(2)}, u32[]{:S(2)}) collective-permute-start(bf16[224,128]{1,0:T(8,128)(2,1)S(1)} %dynamic-slice_bitcast_fusion), channel_id=1, source_target_pairs={{0,0},{1,256},{2,8},{3,264},{4,16},{5,272},{6,24},{7,280},{8,2},{9... | collective-permute-start | bytes 172040 | tf_op jit(solution)/shard_map/ppermute | solution.py:311
  44.5 29.6 %all-to-all-start.1 = ((bf16[8,128,512]{2,1,0:T(8,128)(2,1)}), bf16[8,128,512]{2,1,0:T(8,128)(2,1)S(1)}, u32[]{:S(2)}, u32[]{:S(2)}) async-start(bf16[8,128,512]{2,1,0:T(8,128)(2,1)} %bitcast.32), calls=%async_computation.1 | async-start | bytes 2097152 | tf_op jit(solution)/shard_map/all_to_all | solution.py:347
  74.7 13.0 %collective-permute-start.1 = (bf16[64,4096]{1,0:T(8,128)(2,1)S(1)}, bf16[64,4096]{1,0:T(8,128)(2,1)S(1)}, u32[]{:S(2)}, u32[]{:S(2)}) collective-permute-start(bf16[64,4096]{1,0:T(8,128)(2,1)S(1)} %get-tuple-element.23.refs_0_), channel_id=1, source_target_pairs={{0,8},{8,16},{16,24},{24,0},{32,40},{40,48},{48,56},{56,32},{64,72... | collective-permute-start | bytes 1572872 | tf_op jit(solution)/shard_map/ppermute | solution.py:288
  77.6 12.0 %collective-permute-start.4 = (bf16[64,4096]{1,0:T(8,128)(2,1)S(1)}, bf16[64,4096]{1,0:T(8,128)(2,1)S(1)}, u32[]{:S(2)}, u32[]{:S(2)}) collective-permute-start(bf16[64,4096]{1,0:T(8,128)(2,1)S(1)} %get-tuple-element.24.refs_1_), channel_id=1, source_target_pairs={{0,24},{8,0},{16,8},{24,16},{32,56},{40,32},{48,40},{56,48},{64,88... | collective-permute-start | bytes 1572872 | tf_op jit(solution)/shard_map/ppermute | solution.py:289
  81.2 18.9 %collective-permute-start.6 = (bf16[64,4096]{1,0:T(8,128)(2,1)S(1)}, bf16[64,4096]{1,0:T(8,128)(2,1)S(1)}, u32[]{:S(2)}, u32[]{:S(2)}) collective-permute-start(bf16[64,4096]{1,0:T(8,128)(2,1)S(1)} %get-tuple-element.23.refs_0_), channel_id=1, source_target_pairs={{0,24},{8,0},{16,8},{24,16},{32,56},{40,32},{48,40},{56,48},{64,88... | collective-permute-start | bytes 1572872 | tf_op jit(solution)/shard_map/ppermute | solution.py:291
  83.2 17.1 %collective-permute-start.2 = (bf16[64,4096]{1,0:T(8,128)(2,1)S(1)}, bf16[64,4096]{1,0:T(8,128)(2,1)S(1)}, u32[]{:S(2)}, u32[]{:S(2)}) collective-permute-start(bf16[64,4096]{1,0:T(8,128)(2,1)S(1)} %get-tuple-element.24.refs_1_), channel_id=1, source_target_pairs={{0,8},{8,16},{16,24},{24,0},{32,40},{40,48},{48,56},{56,32},{64,72... | collective-permute-start | bytes 1572872 | tf_op jit(solution)/shard_map/ppermute | solution.py:290
  87.7 23.8 %collective-permute-start.3 = (bf16[64,4096]{1,0:T(8,128)(2,1)S(1)}, bf16[64,4096]{1,0:T(8,128)(2,1)S(1)}, u32[]{:S(2)}, u32[]{:S(2)}) collective-permute-start(bf16[64,4096]{1,0:T(8,128)(2,1)S(1)} %collective-permute-done.1.refs_2_), channel_id=1, source_target_pairs={{0,8},{8,16},{16,24},{24,0},{32,40},{40,48},{48,56},{56,32},{64,72... | collective-permute-start | bytes 1572872 | tf_op jit(solution)/shard_map/ppermute | solution.py:292
  89.6 22.7 %collective-permute-start.5 = (bf16[64,4096]{1,0:T(8,128)(2,1)S(1)}, bf16[64,4096]{1,0:T(8,128)(2,1)S(1)}, u32[]{:S(2)}, u32[]{:S(2)}) collective-permute-start(bf16[64,4096]{1,0:T(8,128)(2,1)S(1)} %collective-permute-done.4.refs_7_), channel_id=1, source_target_pairs={{0,24},{8,0},{16,8},{24,16},{32,56},{40,32},{48,40},{56,48},{64,88... | collective-permute-start | bytes 1572872 | tf_op jit(solution)/shard_map/ppermute | solution.py:293
  111.5 0.8 copy-start.2
  112.3 0.8 copy-start.4
  113.1 12.9 %collective-permute-start.7 = (bf16[8,8,240,128]{3,2,1,0:T(8,128)(2,1)}, bf16[8,8,240,128]{3,2,1,0:T(8,128)(2,1)S(1)}, u32[]{:S(2)}, u32[]{:S(2)}) collective-permute-start(bf16[8,8,240,128]{3,2,1,0:T(8,128)(2,1)} %bitcast.27), channel_id=1, source_target_pairs={{0,256},{256,0},{1,257},{257,1},{2,258},{258,2},{3,259},{259,3},{4... | collective-permute-start | bytes 11796488 | tf_op jit(solution)/shard_map/ppermute | solution.py:364
  119.0 2.1 %copy-start.1 = (bf16[15360,128]{1,0:T(8,128)(2,1)S(1)}, bf16[15360,128]{1,0:T(8,128)(2,1)}, u32[]{:S(2)}) copy-start(bf16[15360,128]{1,0:T(8,128)(2,1)} %all-gather.2.cloned.1.call-done) | copy-start | bytes 11796484
  121.1 1.0 copy-start.3
  122.2 1.0 copy-start.5
  129.8 34.5 %all-to-all-start.2 = ((bf16[32,16,896]{2,1,0:T(8,128)(2,1)}), bf16[32,16,896]{2,1,0:T(8,128)(2,1)S(1)}, u32[]{:S(2)}, u32[]{:S(2)}) async-start(bf16[32,16,896]{2,1,0:T(8,128)(2,1)} %bitcast.12), calls=%async_computation.2 | async-start | bytes 1835008 | tf_op jit(solution)/shard_map/all_to_all | solution.py:371
  140.7 1.2 copy-start.6
Sparse Core Ops, SparseCore 0:
  44.6 52.1 all-gather.1

commit v9 on v8

--- a/solution.py
+++ b/solution.py
@@ -14,7 +14,7 @@
 EMPTY_FROM = 1e20
 
 
-def norm_kernel(moved_ref, slot_ref, gain_ref, top_ref, low_ref, packed):
+def norm_kernel(moved_ref, slot_ref, gain_ref, top_ref, low_ref, own_ref, packed):
     parts, rows, features = moved_ref.shape
     order = lax.broadcasted_iota(jnp.int32, (rows, rows), 0)
     packer = (order == slot_ref[...]).astype(jnp.bfloat16)
@@ -35,6 +35,7 @@
         normed = normed.astype(jnp.bfloat16)
         top_ref[:, columns] = normed[:half]
         low_ref[:, columns] = normed[half:]
+        own_ref[:, columns] = normed
 
 
 def norm_rows(moved, slot, teacher_gain):
@@ -42,7 +43,7 @@
     half = jax.ShapeDtypeStruct((rows // 2, parts * features), jnp.bfloat16)
     return pl.pallas_call(
         norm_kernel,
-        out_shape=(half, half),
+        out_shape=(half, half, jax.ShapeDtypeStruct((rows, parts * features), jnp.bfloat16)),
         scratch_shapes=[pltpu.VMEM((parts, rows, features), jnp.float32)],
         compiler_params=pltpu.CompilerParams(vmem_limit_bytes=16 * MIB),
         cost_estimate=pl.CostEstimate(
@@ -91,7 +92,7 @@
 def turned(shards, total, pieces):
     rows = total.shape[0]
     depth = rows // shards
-    to = lax.broadcasted_iota(jnp.int32, (rows, rows), 0)
+    to = lax.broadcasted_iota(jnp.int32, (rows, 1), 0)
     source = lax.broadcasted_iota(jnp.int32, (rows, rows), 1)
     turn = (source == (to % depth) * shards + to // depth).astype(jnp.bfloat16)
     first_features = jnp.concatenate([piece[:, :128] for piece in pieces], axis=0)
@@ -128,7 +129,7 @@
     y_count, shares, _, tile = weights.shape
     depth = y_count * (shares // 2) * tile
     count = len(pieces)
-    total_rows = pieces[0].shape[0] * count
+    total_rows = sum(piece.shape[0] for piece in pieces)
     joined = first is not None
     in_vmem = pl.BlockSpec(memory_space=pltpu.VMEM)
     head = [pl.BlockSpec(memory_space=pltpu.SMEM), in_vmem] if joined else []
@@ -291,7 +292,7 @@
     right_top = lax.ppermute(top, "dp", backward)
     far_top = lax.ppermute(left_top, "dp", forward)
     far_low = lax.ppermute(right_low, "dp", backward)
-    return [top, low, left_top, left_low, far_top, far_low, right_top, right_low]
+    return [left_top, left_low, far_top, far_low, right_top, right_low]
 
 
 def projector_columns(projector, student_gain, mp_count, x_count, y_count):
@@ -358,8 +359,8 @@
     rank = jnp.sum(same.astype(jnp.int32), axis=0)
     slot = jnp.where(own_live == 1, rank * dp_count + own_shards, -1)
 
-    top, low = norm_rows(moved, slot, teacher_gain)
-    pieces = ring_gather(top, low, x_count, dp_count)
+    top, low, own = norm_rows(moved, slot, teacher_gain)
+    pieces = [own] + ring_gather(top, low, x_count, dp_count)
     mine, pieces = lax.optimization_barrier((mine, pieces))
     other = lax.ppermute(mine, "group", [(0, 1), (1, 0)])
     half = share_width // 2

time: 203 us -> 203 us (level)
  no operation moved by 1% of the time
where the time goes in v9:
time: 203 us
  waiting for transfers between devices  65.4 us (32%)
  blocking collectives  56.9 us (28%)
  starting transfers between devices  43 us (21%)
  between operations  14.2 us (7%)
  Pallas kernels  11.1 us (5%)
  local copies, waits for them, and re-layouts  8.83 us (4%)
  other arithmetic  3.1 us (2%)
    all_to_all x1, blocking collectives, projector_columns(): lax.all_to_all(jnp.broadcast_to(message[None], (mp_count,) + message.shap...  29 us
    all_to_all x1, waiting for transfers between devices, local(): moved = lax.all_to_all(blocks, 'mp', 0, 0, tiled=True)  23.8 us
    all_to_all x1, waiting for transfers between devices, local(): lax.all_to_all(buffer.reshape(dp_count, deep, quarter), 'dp', 0, 0, tiled...  22.1 us
    all_to_all x1, blocking collectives, local(): lax.all_to_all(jnp.broadcast_to(over_mp[None, None, :], (peers, 1, over_m...  18.9 us
    ppermute x1, waiting for transfers between devices, ring_gather(): far_top = lax.ppermute(left_top, 'dp', forward)  11.2 us
    all_to_all x1, starting transfers between devices, local(): lax.all_to_all(buffer.reshape(dp_count, deep, quarter), 'dp', 0, 0, tiled...  9.86 us
    all_to_all x1, blocking collectives, local(): lax.all_to_all(message, 'mp', 0, 0, tiled=True)  8.97 us
    unnamed x17, local copies, waits for them, and re-layouts  7.82 us
  transfers between devices with their start and end apart: 11, of which 7 were waited for; matrix products, arithmetic and copies ran while one was open for 2% of the time, Pallas kernels for 2%

profile of v9, /device:TPU:1, one launch (start us, length us, event | category | flops | bytes accessed | tf_op | source)
XLA Modules:
  0.0 202.5 jit_solution(3776999797460961913)
XLA Ops:
  8.1 5.4 %collective-permute-start = (bf16[224,128]{1,0:T(8,128)(2,1)S(1)}, bf16[224,128]{1,0:T(8,128)(2,1)S(1)}, u32[]{:S(2)}, u32[]{:S(2)}) collective-permute-start(bf16[224,128]{1,0:T(8,128)(2,1)S(1)} %dynamic-slice_bitcast_fusion), channel_id=1, source_target_pairs={{0,0},{1,256},{2,8},{3,264},{4,16},{5,272},{6,24},{7,280},{8,2},{9... | collective-permute-start | bytes 172040 | tf_op jit(solution)/shard_map/ppermute | solution.py:312
  14.2 1.1 collective-permute-done
  15.4 29.0 %all_to_all.25 = bf16[8,240,128]{2,1,0:T(8,128)(2,1)} all-to-all(bf16[8,240,128]{2,1,0:T(8,128)(2,1)S(1)} %broadcast_in_dim.13), channel_id=1, replica_groups=mesh['group'=2,'dp'=32,'mp'=8] {'mp'}, dimensions={0} | all-to-all | bytes 983040 | tf_op jit(solution)/shard_map/all_to_all | solution.py:322
  44.5 3.6 %all-to-all-start.1 = ((bf16[8,128,512]{2,1,0:T(8,128)(2,1)}), bf16[8,128,512]{2,1,0:T(8,128)(2,1)S(1)}, u32[]{:S(2)}, u32[]{:S(2)}) async-start(bf16[8,128,512]{2,1,0:T(8,128)(2,1)} %bitcast.32), calls=%async_computation.1 | async-start | bytes 2097152 | tf_op jit(solution)/shard_map/all_to_all | solution.py:348
  50.3 23.8 %all-to-all-done.1.moved_ref = bf16[8,128,512]{2,1,0:T(8,128)(2,1)S(1)} async-done(((bf16[8,128,512]{2,1,0:T(8,128)(2,1)}), bf16[8,128,512]{2,1,0:T(8,128)(2,1)S(1)}, u32[]{:S(2)}, u32[]{:S(2)}) %all-to-all-start.1) | async-done | bytes 1048608 | tf_op jit(solution)/shard_map/all_to_all | solution.py:348
  74.7 2.9 %collective-permute-start.1 = (bf16[64,4096]{1,0:T(8,128)(2,1)S(1)}, bf16[64,4096]{1,0:T(8,128)(2,1)S(1)}, u32[]{:S(2)}, u32[]{:S(2)}) collective-permute-start(bf16[64,4096]{1,0:T(8,128)(2,1)S(1)} %get-tuple-element.22), channel_id=1, source_target_pairs={{0,8},{8,16},{16,24},{24,0},{32,40},{40,48},{48,56},{56,32},{64,72... | collective-permute-start | bytes 1572872 | tf_op jit(solution)/shard_map/ppermute | solution.py:289
  77.6 3.6 %collective-permute-start.4 = (bf16[64,4096]{1,0:T(8,128)(2,1)S(1)}, bf16[64,4096]{1,0:T(8,128)(2,1)S(1)}, u32[]{:S(2)}, u32[]{:S(2)}) collective-permute-start(bf16[64,4096]{1,0:T(8,128)(2,1)S(1)} %get-tuple-element.23), channel_id=1, source_target_pairs={{0,24},{8,0},{16,8},{24,16},{32,56},{40,32},{48,40},{56,48},{64,88... | collective-permute-start | bytes 1572872 | tf_op jit(solution)/shard_map/ppermute | solution.py:290
  81.2 1.9 collective-permute-start.6
  83.2 3.4 %collective-permute-start.2 = (bf16[64,4096]{1,0:T(8,128)(2,1)S(1)}, bf16[64,4096]{1,0:T(8,128)(2,1)S(1)}, u32[]{:S(2)}, u32[]{:S(2)}) collective-permute-start(bf16[64,4096]{1,0:T(8,128)(2,1)S(1)} %get-tuple-element.23), channel_id=1, source_target_pairs={{0,8},{8,16},{16,24},{24,0},{32,40},{40,48},{48,56},{56,32},{64,72... | collective-permute-start | bytes 1572872 | tf_op jit(solution)/shard_map/ppermute | solution.py:291
  86.5 1.2 collective-permute-done.1.refs_1_
  87.7 1.9 collective-permute-start.3
  89.7 4.6 %collective-permute-start.5 = (bf16[64,4096]{1,0:T(8,128)(2,1)S(1)}, bf16[64,4096]{1,0:T(8,128)(2,1)S(1)}, u32[]{:S(2)}, u32[]{:S(2)}) collective-permute-start(bf16[64,4096]{1,0:T(8,128)(2,1)S(1)} %collective-permute-done.4.refs_6_), channel_id=1, source_target_pairs={{0,24},{8,0},{16,8},{24,16},{32,56},{40,32},{48,40},{56,48},{64,88... | collective-permute-start | bytes 1572872 | tf_op jit(solution)/shard_map/ppermute | solution.py:294
  94.2 5.9 %collective-permute-done.6.refs_5_ = bf16[64,4096]{1,0:T(8,128)(2,1)S(1)} collective-permute-done((bf16[64,4096]{1,0:T(8,128)(2,1)S(1)}, bf16[64,4096]{1,0:T(8,128)(2,1)S(1)}, u32[]{:S(2)}, u32[]{:S(2)}) %collective-permute-start.6) | collective-permute-done | bytes 524320 | tf_op jit(solution)/shard_map/ppermute | solution.py:292
  100.3 11.2 %collective-permute-done.3.refs_3_ = bf16[64,4096]{1,0:T(8,128)(2,1)S(1)} collective-permute-done((bf16[64,4096]{1,0:T(8,128)(2,1)S(1)}, bf16[64,4096]{1,0:T(8,128)(2,1)S(1)}, u32[]{:S(2)}, u32[]{:S(2)}) %collective-permute-start.3) | collective-permute-done | bytes 524320 | tf_op jit(solution)/shard_map/ppermute | solution.py:293
  113.1 5.9 %collective-permute-start.7 = (bf16[8,8,240,128]{3,2,1,0:T(8,128)(2,1)}, bf16[8,8,240,128]{3,2,1,0:T(8,128)(2,1)S(1)}, u32[]{:S(2)}, u32[]{:S(2)}) collective-permute-start(bf16[8,8,240,128]{3,2,1,0:T(8,128)(2,1)} %bitcast.27), channel_id=1, source_target_pairs={{0,256},{256,0},{1,257},{257,1},{2,258},{258,2},{3,259},{259,3},{4... | collective-permute-start | bytes 11796488 | tf_op jit(solution)/shard_map/ppermute | solution.py:365
  119.0 2.1 %copy-done.1 = bf16[15360,128]{1,0:T(8,128)(2,1)S(1)} copy-done((bf16[15360,128]{1,0:T(8,128)(2,1)S(1)}, bf16[15360,128]{1,0:T(8,128)(2,1)}, u32[]{:S(2)}) %copy-start.1) | copy-done | bytes 3932184
  123.2 2.7 %shard_map.95.first_ref = bf16[512,448]{1,0:T(8,128)(2,1)S(1)} custom-call(bf16[128,4096]{1,0:T(8,128)(2,1)S(1)} %get-tuple-element.24.refs_0_, bf16[64,4096]{1,0:T(8,128)(2,1)S(1)} %collective-permute-done.1.refs_1_, bf16[64,4096]{1,0:T(8,128)(2,1)S(1)} %collective-permute-done.2.refs_2_, bf16[64,4096]{1,0:T(8,128)(2,1)S(1)} %copy-done.3, ...), custom_call_target="tpu_custom_call" | custom-call | flops 1879048192 | bytes 7864320 | tf_op jit(solution)/shard_map/pallas_call | solution.py:137
  126.0 3.9 %shard_map.96 = bf16[512,896]{1,0:T(8,128)(2,1)} custom-call(s32[1]{0:T(128)} %bitcast.core_ref, bf16[512,448]{1,0:T(8,128)(2,1)S(1)} %shard_map.95.first_ref, bf16[128,4096]{1,0:T(8,128)(2,1)S(1)} %get-tuple-element.24.refs_0_, bf16[64,4096]{1,0:T(8,128)(2,1)S(1)} %collective-permute-done.1.refs_1_, bf16[64,4096]{1,0:T(8,128)(2,1)S(1)} %collective-permute-done.2.refs_2_, ...), custom_call_target="tpu_custom_call" | custom-call | flops 1879048192 | bytes 7864320 | tf_op jit(solution)/shard_map/pallas_call | solution.py:137
  129.9 9.9 %all-to-all-start.2 = ((bf16[32,16,896]{2,1,0:T(8,128)(2,1)}), bf16[32,16,896]{2,1,0:T(8,128)(2,1)S(1)}, u32[]{:S(2)}, u32[]{:S(2)}) async-start(bf16[32,16,896]{2,1,0:T(8,128)(2,1)} %bitcast.12), calls=%async_computation.2 | async-start | bytes 1835008 | tf_op jit(solution)/shard_map/all_to_all | solution.py:372
  140.7 1.2 copy-done.6
  142.2 22.1 %all-to-all-done.2 = bf16[32,16,896]{2,1,0:T(8,128)(2,1)S(1)} async-done(((bf16[32,16,896]{2,1,0:T(8,128)(2,1)}), bf16[32,16,896]{2,1,0:T(8,128)(2,1)S(1)}, u32[]{:S(2)}, u32[]{:S(2)}) %all-to-all-start.2) | async-done | bytes 917536 | tf_op jit(solution)/shard_map/all_to_all | solution.py:372
  164.3 2.7 %shard_map.98 = (bf16[128,3584]{1,0:T(8,128)(2,1)}, f32[8,1,512]{2,1,0:T(1,128)S(1)}) custom-call(bf16[8,4,16,896]{3,2,1,0:T(8,128)(2,1)S(1)} %bitcast.29, f32[128,3584]{1,0:T(8,128)S(1)} %get-tuple-element.33.normal_ref, f32[128,128]{1,0:T(8,128)S(1)} %get-tuple-element.34.rms_ref, f32[1,3584]{1,0:T(1,128)S(1)} %broadcast_in_dim_reshape.3.gain_ref), custom_call_target="tpu_custom_call" | custom-call | flops 117440512 | bytes 2752512 | tf_op jit(solution)/shard_map/pallas_call | solution.py:246
  167.0 9.0 %all_to_all.26 = f32[8,1,512]{2,1,0:T(1,128)S(1)} all-to-all(f32[8,1,512]{2,1,0:T(1,128)S(1)} %get-tuple-element.36), channel_id=1, replica_groups=mesh['group'=2,'dp'=32,'mp'=8] {'mp'}, dimensions={0} | all-to-all | bytes 32768 | tf_op jit(solution)/shard_map/all_to_all | solution.py:379
  176.1 18.9 %all_to_all.27.parts_ref = f32[64,1,512]{2,1,0:T(1,128)S(1)} all-to-all(f32[64,1,512]{2,1,0:T(1,128)S(1)} %broadcast_in_dim.16), channel_id=1, replica_groups=mesh['group'=2,'dp'=32,'mp'=8] {'group','dp'}, dimensions={0} | all-to-all | bytes 262144 | tf_op jit(solution)/shard_map/all_to_all | solution.py:381
  (40 shorter events, 10.7 us)
Async XLA Ops:
  7.2 0.9 copy-start
  7.2 66.9 %copy-start.7 = (f32[4096]{0:T(1024)S(1)}, f32[4096]{0:T(1024)}, u32[]{:S(2)}) copy-start(f32[4096]{0:T(1024)} %param.8) | copy-start | bytes 49156
  7.2 105.9 %all-gather.2.cloned.1.call-start = ((), (), s32[]{:S(2)}) async-start(), calls=%async_computation.5 | async-start | bytes 4423680 | tf_op jit(solution)/shard_map/all_gather | solution.py:329
  8.1 7.2 %collective-permute-start = (bf16[224,128]{1,0:T(8,128)(2,1)S(1)}, bf16[224,128]{1,0:T(8,128)(2,1)S(1)}, u32[]{:S(2)}, u32[]{:S(2)}) collective-permute-start(bf16[224,128]{1,0:T(8,128)(2,1)S(1)} %dynamic-slice_bitcast_fusion), channel_id=1, source_target_pairs={{0,0},{1,256},{2,8},{3,264},{4,16},{5,272},{6,24},{7,280},{8,2},{9... | collective-permute-start | bytes 172040 | tf_op jit(solution)/shard_map/ppermute | solution.py:312
  44.5 29.6 %all-to-all-start.1 = ((bf16[8,128,512]{2,1,0:T(8,128)(2,1)}), bf16[8,128,512]{2,1,0:T(8,128)(2,1)S(1)}, u32[]{:S(2)}, u32[]{:S(2)}) async-start(bf16[8,128,512]{2,1,0:T(8,128)(2,1)} %bitcast.32), calls=%async_computation.1 | async-start | bytes 2097152 | tf_op jit(solution)/shard_map/all_to_all | solution.py:348
  74.7 13.0 %collective-permute-start.1 = (bf16[64,4096]{1,0:T(8,128)(2,1)S(1)}, bf16[64,4096]{1,0:T(8,128)(2,1)S(1)}, u32[]{:S(2)}, u32[]{:S(2)}) collective-permute-start(bf16[64,4096]{1,0:T(8,128)(2,1)S(1)} %get-tuple-element.22), channel_id=1, source_target_pairs={{0,8},{8,16},{16,24},{24,0},{32,40},{40,48},{48,56},{56,32},{64,72... | collective-permute-start | bytes 1572872 | tf_op jit(solution)/shard_map/ppermute | solution.py:289
  77.6 12.0 %collective-permute-start.4 = (bf16[64,4096]{1,0:T(8,128)(2,1)S(1)}, bf16[64,4096]{1,0:T(8,128)(2,1)S(1)}, u32[]{:S(2)}, u32[]{:S(2)}) collective-permute-start(bf16[64,4096]{1,0:T(8,128)(2,1)S(1)} %get-tuple-element.23), channel_id=1, source_target_pairs={{0,24},{8,0},{16,8},{24,16},{32,56},{40,32},{48,40},{56,48},{64,88... | collective-permute-start | bytes 1572872 | tf_op jit(solution)/shard_map/ppermute | solution.py:290
  81.2 18.9 %collective-permute-start.6 = (bf16[64,4096]{1,0:T(8,128)(2,1)S(1)}, bf16[64,4096]{1,0:T(8,128)(2,1)S(1)}, u32[]{:S(2)}, u32[]{:S(2)}) collective-permute-start(bf16[64,4096]{1,0:T(8,128)(2,1)S(1)} %get-tuple-element.22), channel_id=1, source_target_pairs={{0,24},{8,0},{16,8},{24,16},{32,56},{40,32},{48,40},{56,48},{64,88... | collective-permute-start | bytes 1572872 | tf_op jit(solution)/shard_map/ppermute | solution.py:292
  83.2 17.1 %collective-permute-start.2 = (bf16[64,4096]{1,0:T(8,128)(2,1)S(1)}, bf16[64,4096]{1,0:T(8,128)(2,1)S(1)}, u32[]{:S(2)}, u32[]{:S(2)}) collective-permute-start(bf16[64,4096]{1,0:T(8,128)(2,1)S(1)} %get-tuple-element.23), channel_id=1, source_target_pairs={{0,8},{8,16},{16,24},{24,0},{32,40},{40,48},{48,56},{56,32},{64,72... | collective-permute-start | bytes 1572872 | tf_op jit(solution)/shard_map/ppermute | solution.py:291
  87.7 23.8 %collective-permute-start.3 = (bf16[64,4096]{1,0:T(8,128)(2,1)S(1)}, bf16[64,4096]{1,0:T(8,128)(2,1)S(1)}, u32[]{:S(2)}, u32[]{:S(2)}) collective-permute-start(bf16[64,4096]{1,0:T(8,128)(2,1)S(1)} %collective-permute-done.1.refs_1_), channel_id=1, source_target_pairs={{0,8},{8,16},{16,24},{24,0},{32,40},{40,48},{48,56},{56,32},{64,72... | collective-permute-start | bytes 1572872 | tf_op jit(solution)/shard_map/ppermute | solution.py:293
  89.7 22.7 %collective-permute-start.5 = (bf16[64,4096]{1,0:T(8,128)(2,1)S(1)}, bf16[64,4096]{1,0:T(8,128)(2,1)S(1)}, u32[]{:S(2)}, u32[]{:S(2)}) collective-permute-start(bf16[64,4096]{1,0:T(8,128)(2,1)S(1)} %collective-permute-done.4.refs_6_), channel_id=1, source_target_pairs={{0,24},{8,0},{16,8},{24,16},{32,56},{40,32},{48,40},{56,48},{64,88... | collective-permute-start | bytes 1572872 | tf_op jit(solution)/shard_map/ppermute | solution.py:294
  111.5 0.8 copy-start.2
  112.3 0.8 copy-start.4
  113.1 12.9 %collective-permute-start.7 = (bf16[8,8,240,128]{3,2,1,0:T(8,128)(2,1)}, bf16[8,8,240,128]{3,2,1,0:T(8,128)(2,1)S(1)}, u32[]{:S(2)}, u32[]{:S(2)}) collective-permute-start(bf16[8,8,240,128]{3,2,1,0:T(8,128)(2,1)} %bitcast.27), channel_id=1, source_target_pairs={{0,256},{256,0},{1,257},{257,1},{2,258},{258,2},{3,259},{259,3},{4... | collective-permute-start | bytes 11796488 | tf_op jit(solution)/shard_map/ppermute | solution.py:365
  119.0 2.1 %copy-start.1 = (bf16[15360,128]{1,0:T(8,128)(2,1)S(1)}, bf16[15360,128]{1,0:T(8,128)(2,1)}, u32[]{:S(2)}) copy-start(bf16[15360,128]{1,0:T(8,128)(2,1)} %all-gather.2.cloned.1.call-done) | copy-start | bytes 11796484
  121.1 1.0 copy-start.3
  122.2 1.0 copy-start.5
  129.9 34.5 %all-to-all-start.2 = ((bf16[32,16,896]{2,1,0:T(8,128)(2,1)}), bf16[32,16,896]{2,1,0:T(8,128)(2,1)S(1)}, u32[]{:S(2)}, u32[]{:S(2)}) async-start(bf16[32,16,896]{2,1,0:T(8,128)(2,1)} %bitcast.12), calls=%async_computation.2 | async-start | bytes 1835008 | tf_op jit(solution)/shard_map/all_to_all | solution.py:372
  140.7 1.2 copy-start.6
Sparse Core Ops, SparseCore 0:
  44.6 52.1 all-gather.1

commit v10 on v8

--- a/solution.py
+++ b/solution.py
@@ -182,14 +182,10 @@
     )(hidden)
 
 
-def finish_kernel(
-    mp_count, received_ref, normal_ref, rms_ref, gain_ref, gradient_ref, message_ref, weighted_sum, gain_sum
-):
+def student_parts(received_ref, normal_ref, gain_ref):
     y_count, x_count, deep, quarter = received_ref.shape
-    rows, width = normal_ref.shape
+    rows = normal_ref.shape[0]
     capacity = deep // x_count
-    spans = [slice(x * quarter, (x + 1) * quarter) for x in range(x_count)]
-    inverse_rms = rms_ref[:, 0:1]
     to = lax.broadcasted_iota(jnp.int32, (rows, rows), 0)
     source = lax.broadcasted_iota(jnp.int32, (rows, rows), 1)
 
@@ -197,10 +193,10 @@
         y, j, rank = row // deep, (row // capacity) % x_count, row % capacity
         return (y * x_count + (x - j + x_count) % x_count) * capacity + rank
 
-    row_terms = jnp.zeros((rows, 1), jnp.float32)
-    squares = jnp.zeros((rows, 1), jnp.float32)
+    parts = []
     tally = None
-    for x, span in enumerate(spans):
+    for x in range(x_count):
+        span = slice(x * quarter, (x + 1) * quarter)
         block = received_ref[:, x].reshape(y_count * deep, quarter)
         live = jnp.where(block[:, 0:1].astype(jnp.float32) < EMPTY_FROM, 1.0, 0.0)
         live = jnp.broadcast_to(live, (rows, rows))
@@ -217,18 +213,17 @@
         )
         gain = gain_ref[:, span]
         normal = normal_ref[:, span]
-        mismatch = (normal * gain - target) * filled
-        weighted = mismatch * gain
-        weighted_sum[:, span] = weighted
-        row_terms += jnp.sum(weighted * normal, axis=1, keepdims=True)
+        parts.append((span, normal, gain, (normal * gain - target) * filled))
+    return parts, tally
+
+
+def message_kernel(mp_count, received_ref, normal_ref, gain_ref, message_ref, gain_sum):
+    rows, width = normal_ref.shape
+    parts, tally = student_parts(received_ref, normal_ref, gain_ref)
+    squares = jnp.zeros((rows, 1), jnp.float32)
+    for span, normal, _, mismatch in parts:
         squares += jnp.sum(mismatch * mismatch, axis=1, keepdims=True)
         gain_sum[:, span] = jnp.sum(mismatch * normal, axis=0, keepdims=True)
-    row_mean = row_terms * (1.0 / width)
-    for span in spans:
-        normal = normal_ref[:, span]
-        gradient_ref[:, span] = (
-            inverse_rms * (weighted_sum[:, span] - normal * row_mean)
-        ).astype(jnp.bfloat16)
     share = width // mp_count
     square_sum = jnp.sum(squares, axis=0, keepdims=True)
     lane = lax.broadcasted_iota(jnp.int32, (1, message_ref.shape[2] - share), 1)
@@ -238,25 +233,52 @@
         message_ref[m, :, share:] = tail
 
 
-def finish(received, normal, inverse_rms, gains, mp_count):
+def gradient_kernel(received_ref, normal_ref, rms_ref, gain_ref, gradient_ref, weighted_sum):
+    rows, width = normal_ref.shape
+    parts, _ = student_parts(received_ref, normal_ref, gain_ref)
+    row_terms = jnp.zeros((rows, 1), jnp.float32)
+    for span, normal, gain, mismatch in parts:
+        weighted = mismatch * gain
+        weighted_sum[:, span] = weighted
+        row_terms += jnp.sum(weighted * normal, axis=1, keepdims=True)
+    row_mean = row_terms * (1.0 / width)
+    for span, _, _, _ in parts:
+        gradient_ref[:, span] = (
+            rms_ref[:, 0:1] * (weighted_sum[:, span] - normal_ref[:, span] * row_mean)
+        ).astype(jnp.bfloat16)
+
+
+def finish(received, normal, gains, mp_count):
     rows, width = normal.shape
     share = width // mp_count
     in_vmem = pl.BlockSpec(memory_space=pltpu.VMEM)
+    cost = pl.CostEstimate(
+        flops=2 * rows * rows * width, bytes_accessed=6 * rows * width, transcendentals=0
+    )
+    message = pl.pallas_call(
+        functools.partial(message_kernel, mp_count),
+        out_shape=jax.ShapeDtypeStruct((mp_count, 1, share + 64), jnp.float32),
+        in_specs=[in_vmem] * 3,
+        out_specs=in_vmem,
+        scratch_shapes=[pltpu.VMEM((1, width), jnp.float32)],
+        compiler_params=pltpu.CompilerParams(vmem_limit_bytes=16 * MIB),
+        cost_estimate=cost,
+    )(received, normal, gains[None, :])
+    return message
+
+
+def student_gradient(received, normal, inverse_rms, gains):
+    rows, width = normal.shape
+    in_vmem = pl.BlockSpec(memory_space=pltpu.VMEM)
     return pl.pallas_call(
-        functools.partial(finish_kernel, mp_count),
-        out_shape=(
-            jax.ShapeDtypeStruct((rows, width), jnp.bfloat16),
-            jax.ShapeDtypeStruct((mp_count, 1, share + 64), jnp.float32),
-        ),
+        gradient_kernel,
+        out_shape=jax.ShapeDtypeStruct((rows, width), jnp.bfloat16),
         in_specs=[in_vmem] * 4,
-        out_specs=(in_vmem, in_vmem),
-        scratch_shapes=[
-            pltpu.VMEM((rows, width), jnp.float32),
-            pltpu.VMEM((1, width), jnp.float32),
-        ],
+        out_specs=in_vmem,
+        scratch_shapes=[pltpu.VMEM((rows, width), jnp.float32)],
         compiler_params=pltpu.CompilerParams(vmem_limit_bytes=16 * MIB),
         cost_estimate=pl.CostEstimate(
-            flops=2 * rows * rows * width, bytes_accessed=6 * rows * width, transcendentals=rows
+            flops=2 * rows * rows * width, bytes_accessed=6 * rows * width, transcendentals=0
         ),
     )(received, normal, inverse_rms, gains[None, :])
 
@@ -373,9 +395,11 @@
     ).reshape(y_count, x_count, deep, quarter)
     hidden, _ = lax.optimization_barrier((student_hidden, buffer))
     normal, inverse_rms = student_rows(hidden)
-    gradient, message = finish(received, normal, inverse_rms, gains, mp_count)
+    message = finish(received, normal, gains, mp_count)
 
     over_mp = jnp.sum(lax.all_to_all(message, "mp", 0, 0, tiled=True), axis=(0, 1))
+    received, _ = lax.optimization_barrier((received, over_mp))
+    gradient = student_gradient(received, normal, inverse_rms, gains)
     peers = group_count * dp_count
     parts = lax.all_to_all(
         jnp.broadcast_to(over_mp[None, None, :], (peers, 1, over_mp.shape[0])),

time: 203 us -> 203 us (level)
  blocking collectives: 56.9 us -> 38 us
  starting transfers between devices: 43 us -> 51.6 us
  waiting for transfers between devices: 65.4 us -> 73.4 us
    all_to_all x1 -> x0, blocking collectives: 18.9 us -> none  [local(): lax.all_to_all(jnp.broadcast_to(over_mp[None, None, :], (peers, 1, over_m...]
    all_to_all x0 -> x1, starting transfers between devices: none -> 8.59 us  [local(): lax.all_to_all(jnp.broadcast_to(over_mp[None, None, :], (peers, 1, over_m...]
    all_to_all x0 -> x1, waiting for transfers between devices: none -> 8.01 us  [local(): lax.all_to_all(jnp.broadcast_to(over_mp[None, None, :], (peers, 1, over_m...]
  transfers between devices with their start and end apart: 11 -> 12, of which waited for: 7 -> 8; matrix products, arithmetic and copies ran while one was open for 2% -> 2% of each run, Pallas kernels for 2% -> 3%
where the time goes in v10:
time: 203 us; the launch traced here: 202 us
  waiting for transfers between devices  73.4 us (36%)
  starting transfers between devices  51.6 us (25%)
  blocking collectives  38 us (19%)
  between operations  14.2 us (7%)
  Pallas kernels  12.3 us (6%)
  local copies, waits for them, and re-layouts  9.48 us (5%)
  other arithmetic  3.1 us (2%)
    all_to_all x1, blocking collectives, projector_columns(): lax.all_to_all(jnp.broadcast_to(message[None], (mp_count,) + message.shap...  29 us
    all_to_all x1, waiting for transfers between devices, local(): moved = lax.all_to_all(blocks, 'mp', 0, 0, tiled=True)  23.8 us
    all_to_all x1, waiting for transfers between devices, local(): lax.all_to_all(buffer.reshape(dp_count, deep, quarter), 'dp', 0, 0, tiled...  22.1 us
    ppermute x1, waiting for transfers between devices, ring_gather(): far_top = lax.ppermute(left_top, 'dp', forward)  11.2 us
    all_to_all x1, starting transfers between devices, local(): lax.all_to_all(buffer.reshape(dp_count, deep, quarter), 'dp', 0, 0, tiled...  9.86 us
    all_to_all x1, blocking collectives, local(): lax.all_to_all(message, 'mp', 0, 0, tiled=True)  8.98 us
    all_to_all x1, starting transfers between devices, local(): lax.all_to_all(jnp.broadcast_to(over_mp[None, None, :], (peers, 1, over_m...  8.59 us
    all_to_all x1, waiting for transfers between devices, local(): lax.all_to_all(jnp.broadcast_to(over_mp[None, None, :], (peers, 1, over_m...  8.01 us
  transfers between devices with their start and end apart: 12, of which 8 were waited for; matrix products, arithmetic and copies ran while one was open for 2% of the time, Pallas kernels for 3%

profile of v10, /device:TPU:1, one launch (start us, length us, event | category | flops | bytes accessed | tf_op | source)
XLA Modules:
  0.0 202.2 jit_solution(10723119730494836841)
XLA Ops:
  8.1 5.4 %collective-permute-start = (bf16[224,128]{1,0:T(8,128)(2,1)S(1)}, bf16[224,128]{1,0:T(8,128)(2,1)S(1)}, u32[]{:S(2)}, u32[]{:S(2)}) collective-permute-start(bf16[224,128]{1,0:T(8,128)(2,1)S(1)} %dynamic-slice_bitcast_fusion), channel_id=1, source_target_pairs={{0,0},{1,256},{2,8},{3,264},{4,16},{5,272},{6,24},{7,280},{8,2},{9... | collective-permute-start | bytes 172040 | tf_op jit(solution)/shard_map/ppermute | solution.py:333
  15.4 29.0 %all_to_all.25 = bf16[8,240,128]{2,1,0:T(8,128)(2,1)} all-to-all(bf16[8,240,128]{2,1,0:T(8,128)(2,1)S(1)} %broadcast_in_dim.13), channel_id=1, replica_groups=mesh['group'=2,'dp'=32,'mp'=8] {'mp'}, dimensions={0} | all-to-all | bytes 983040 | tf_op jit(solution)/shard_map/all_to_all | solution.py:343
  44.5 3.6 %all-to-all-start.1 = ((bf16[8,128,512]{2,1,0:T(8,128)(2,1)}), bf16[8,128,512]{2,1,0:T(8,128)(2,1)S(1)}, u32[]{:S(2)}, u32[]{:S(2)}) async-start(bf16[8,128,512]{2,1,0:T(8,128)(2,1)} %bitcast.33), calls=%async_computation.1 | async-start | bytes 2097152 | tf_op jit(solution)/shard_map/all_to_all | solution.py:369
  50.3 23.8 %all-to-all-done.1.moved_ref = bf16[8,128,512]{2,1,0:T(8,128)(2,1)S(1)} async-done(((bf16[8,128,512]{2,1,0:T(8,128)(2,1)}), bf16[8,128,512]{2,1,0:T(8,128)(2,1)S(1)}, u32[]{:S(2)}, u32[]{:S(2)}) %all-to-all-start.1) | async-done | bytes 1048608 | tf_op jit(solution)/shard_map/all_to_all | solution.py:369
  74.7 2.9 %collective-permute-start.1 = (bf16[64,4096]{1,0:T(8,128)(2,1)S(1)}, bf16[64,4096]{1,0:T(8,128)(2,1)S(1)}, u32[]{:S(2)}, u32[]{:S(2)}) collective-permute-start(bf16[64,4096]{1,0:T(8,128)(2,1)S(1)} %get-tuple-element.22.refs_0_), channel_id=1, source_target_pairs={{0,8},{8,16},{16,24},{24,0},{32,40},{40,48},{48,56},{56,32},{64,72... | collective-permute-start | bytes 1572872 | tf_op jit(solution)/shard_map/ppermute | solution.py:310
  77.6 3.6 %collective-permute-start.4 = (bf16[64,4096]{1,0:T(8,128)(2,1)S(1)}, bf16[64,4096]{1,0:T(8,128)(2,1)S(1)}, u32[]{:S(2)}, u32[]{:S(2)}) collective-permute-start(bf16[64,4096]{1,0:T(8,128)(2,1)S(1)} %get-tuple-element.23.refs_1_), channel_id=1, source_target_pairs={{0,24},{8,0},{16,8},{24,16},{32,56},{40,32},{48,40},{56,48},{64,88... | collective-permute-start | bytes 1572872 | tf_op jit(solution)/shard_map/ppermute | solution.py:311
  81.2 1.9 collective-permute-start.6
  83.2 3.4 %collective-permute-start.2 = (bf16[64,4096]{1,0:T(8,128)(2,1)S(1)}, bf16[64,4096]{1,0:T(8,128)(2,1)S(1)}, u32[]{:S(2)}, u32[]{:S(2)}) collective-permute-start(bf16[64,4096]{1,0:T(8,128)(2,1)S(1)} %get-tuple-element.23.refs_1_), channel_id=1, source_target_pairs={{0,8},{8,16},{16,24},{24,0},{32,40},{40,48},{48,56},{56,32},{64,72... | collective-permute-start | bytes 1572872 | tf_op jit(solution)/shard_map/ppermute | solution.py:312
  86.5 1.2 collective-permute-done.1.refs_2_
  87.7 1.9 collective-permute-start.3
  89.6 4.6 %collective-permute-start.5 = (bf16[64,4096]{1,0:T(8,128)(2,1)S(1)}, bf16[64,4096]{1,0:T(8,128)(2,1)S(1)}, u32[]{:S(2)}, u32[]{:S(2)}) collective-permute-start(bf16[64,4096]{1,0:T(8,128)(2,1)S(1)} %collective-permute-done.4.refs_7_), channel_id=1, source_target_pairs={{0,24},{8,0},{16,8},{24,16},{32,56},{40,32},{48,40},{56,48},{64,88... | collective-permute-start | bytes 1572872 | tf_op jit(solution)/shard_map/ppermute | solution.py:315
  94.2 5.9 %collective-permute-done.6.refs_6_ = bf16[64,4096]{1,0:T(8,128)(2,1)S(1)} collective-permute-done((bf16[64,4096]{1,0:T(8,128)(2,1)S(1)}, bf16[64,4096]{1,0:T(8,128)(2,1)S(1)}, u32[]{:S(2)}, u32[]{:S(2)}) %collective-permute-start.6) | collective-permute-done | bytes 524320 | tf_op jit(solution)/shard_map/ppermute | solution.py:313
  100.3 11.2 %collective-permute-done.3.refs_4_ = bf16[64,4096]{1,0:T(8,128)(2,1)S(1)} collective-permute-done((bf16[64,4096]{1,0:T(8,128)(2,1)S(1)}, bf16[64,4096]{1,0:T(8,128)(2,1)S(1)}, u32[]{:S(2)}, u32[]{:S(2)}) %collective-permute-start.3) | collective-permute-done | bytes 524320 | tf_op jit(solution)/shard_map/ppermute | solution.py:314
  113.1 5.9 %collective-permute-start.7 = (bf16[8,8,240,128]{3,2,1,0:T(8,128)(2,1)}, bf16[8,8,240,128]{3,2,1,0:T(8,128)(2,1)S(1)}, u32[]{:S(2)}, u32[]{:S(2)}) collective-permute-start(bf16[8,8,240,128]{3,2,1,0:T(8,128)(2,1)} %bitcast.29), channel_id=1, source_target_pairs={{0,256},{256,0},{1,257},{257,1},{2,258},{258,2},{3,259},{259,3},{4... | collective-permute-start | bytes 11796488 | tf_op jit(solution)/shard_map/ppermute | solution.py:386
  119.0 2.1 %copy-done.1 = bf16[15360,128]{1,0:T(8,128)(2,1)S(1)} copy-done((bf16[15360,128]{1,0:T(8,128)(2,1)S(1)}, bf16[15360,128]{1,0:T(8,128)(2,1)}, u32[]{:S(2)}) %copy-start.1) | copy-done | bytes 3932184
  123.2 2.7 %shard_map.95.first_ref = bf16[512,448]{1,0:T(8,128)(2,1)S(1)} custom-call(bf16[64,4096]{1,0:T(8,128)(2,1)S(1)} %get-tuple-element.22.refs_0_, bf16[64,4096]{1,0:T(8,128)(2,1)S(1)} %get-tuple-element.23.refs_1_, bf16[64,4096]{1,0:T(8,128)(2,1)S(1)} %collective-permute-done.1.refs_2_, bf16[64,4096]{1,0:T(8,128)(2,1)S(1)} %collective-permute-done.2.refs_3_, ...), custom_call_target="tpu_custom_call" | custom-call | flops 1879048192 | bytes 7864320 | tf_op jit(solution)/shard_map/pallas_call | solution.py:136
  126.0 3.9 %shard_map.96 = bf16[512,896]{1,0:T(8,128)(2,1)} custom-call(s32[1]{0:T(128)} %bitcast.core_ref, bf16[512,448]{1,0:T(8,128)(2,1)S(1)} %shard_map.95.first_ref, bf16[64,4096]{1,0:T(8,128)(2,1)S(1)} %get-tuple-element.22.refs_0_, bf16[64,4096]{1,0:T(8,128)(2,1)S(1)} %get-tuple-element.23.refs_1_, bf16[64,4096]{1,0:T(8,128)(2,1)S(1)} %collective-permute-done.1.refs_2_, ...), custom_call_target="tpu_custom_call" | custom-call | flops 1879048192 | bytes 7864320 | tf_op jit(solution)/shard_map/pallas_call | solution.py:136
  129.8 9.9 %all-to-all-start.2 = ((bf16[32,16,896]{2,1,0:T(8,128)(2,1)}), bf16[32,16,896]{2,1,0:T(8,128)(2,1)S(1)}, u32[]{:S(2)}, u32[]{:S(2)}) async-start(bf16[32,16,896]{2,1,0:T(8,128)(2,1)} %bitcast.12), calls=%async_computation.2 | async-start | bytes 1835008 | tf_op jit(solution)/shard_map/all_to_all | solution.py:393
  142.2 22.1 %all-to-all-done.2 = bf16[32,16,896]{2,1,0:T(8,128)(2,1)S(1)} async-done(((bf16[32,16,896]{2,1,0:T(8,128)(2,1)}), bf16[32,16,896]{2,1,0:T(8,128)(2,1)S(1)}, u32[]{:S(2)}, u32[]{:S(2)}) %all-to-all-start.2) | async-done | bytes 917536 | tf_op jit(solution)/shard_map/all_to_all | solution.py:393
  164.3 1.5 shard_map.98
  165.8 9.0 %all_to_all.26 = f32[8,1,512]{2,1,0:T(1,128)S(1)} all-to-all(f32[8,1,512]{2,1,0:T(1,128)S(1)} %shard_map.98), channel_id=1, replica_groups=mesh['group'=2,'dp'=32,'mp'=8] {'mp'}, dimensions={0} | all-to-all | bytes 32768 | tf_op jit(solution)/shard_map/all_to_all | solution.py:400
  175.5 8.6 %all-to-all-start.4 = ((f32[64,1,512]{2,1,0:T(1,128)}), f32[64,1,512]{2,1,0:T(1,128)S(1)}, u32[]{:S(2)}, u32[]{:S(2)}) async-start(f32[64,1,512]{2,1,0:T(1,128)} %broadcast_in_dim.16), calls=%async_computation.4 | async-start | bytes 262144 | tf_op jit(solution)/shard_map/all_to_all | solution.py:404
  184.1 2.5 %shard_map.99 = bf16[128,3584]{1,0:T(8,128)(2,1)} custom-call(bf16[8,4,16,896]{3,2,1,0:T(8,128)(2,1)S(1)} %bitcast.28, f32[128,3584]{1,0:T(8,128)S(1)} %get-tuple-element.32.normal_ref, f32[128,128]{1,0:T(8,128)S(1)} %get-tuple-element.34.rms_ref, f32[1,3584]{1,0:T(1,128)S(1)} %broadcast_in_dim_reshape.4.gain_ref), custom_call_target="tpu_custom_call" | custom-call | flops 117440512 | bytes 2752512 | tf_op jit(solution)/shard_map/pallas_call | solution.py:273
  186.6 8.0 %all-to-all-done.4.parts_ref = f32[64,1,512]{2,1,0:T(1,128)S(1)} async-done(((f32[64,1,512]{2,1,0:T(1,128)}), f32[64,1,512]{2,1,0:T(1,128)S(1)}, u32[]{:S(2)}, u32[]{:S(2)}) %all-to-all-start.4) | async-done | bytes 131104 | tf_op jit(solution)/shard_map/all_to_all | solution.py:404
  (42 shorter events, 13.5 us)
Async XLA Ops:
  7.2 0.9 copy-start
  7.2 66.9 %copy-start.7 = (f32[4096]{0:T(1024)S(1)}, f32[4096]{0:T(1024)}, u32[]{:S(2)}) copy-start(f32[4096]{0:T(1024)} %param.8) | copy-start | bytes 49156
  7.2 105.9 %all-gather.2.cloned.1.call-start = ((), (), s32[]{:S(2)}) async-start(), calls=%async_computation.5 | async-start | bytes 4423680 | tf_op jit(solution)/shard_map/all_gather | solution.py:350
  8.1 7.2 %collective-permute-start = (bf16[224,128]{1,0:T(8,128)(2,1)S(1)}, bf16[224,128]{1,0:T(8,128)(2,1)S(1)}, u32[]{:S(2)}, u32[]{:S(2)}) collective-permute-start(bf16[224,128]{1,0:T(8,128)(2,1)S(1)} %dynamic-slice_bitcast_fusion), channel_id=1, source_target_pairs={{0,0},{1,256},{2,8},{3,264},{4,16},{5,272},{6,24},{7,280},{8,2},{9... | collective-permute-start | bytes 172040 | tf_op jit(solution)/shard_map/ppermute | solution.py:333
  44.5 29.6 %all-to-all-start.1 = ((bf16[8,128,512]{2,1,0:T(8,128)(2,1)}), bf16[8,128,512]{2,1,0:T(8,128)(2,1)S(1)}, u32[]{:S(2)}, u32[]{:S(2)}) async-start(bf16[8,128,512]{2,1,0:T(8,128)(2,1)} %bitcast.33), calls=%async_computation.1 | async-start | bytes 2097152 | tf_op jit(solution)/shard_map/all_to_all | solution.py:369
  74.7 13.0 %collective-permute-start.1 = (bf16[64,4096]{1,0:T(8,128)(2,1)S(1)}, bf16[64,4096]{1,0:T(8,128)(2,1)S(1)}, u32[]{:S(2)}, u32[]{:S(2)}) collective-permute-start(bf16[64,4096]{1,0:T(8,128)(2,1)S(1)} %get-tuple-element.22.refs_0_), channel_id=1, source_target_pairs={{0,8},{8,16},{16,24},{24,0},{32,40},{40,48},{48,56},{56,32},{64,72... | collective-permute-start | bytes 1572872 | tf_op jit(solution)/shard_map/ppermute | solution.py:310
  77.6 12.0 %collective-permute-start.4 = (bf16[64,4096]{1,0:T(8,128)(2,1)S(1)}, bf16[64,4096]{1,0:T(8,128)(2,1)S(1)}, u32[]{:S(2)}, u32[]{:S(2)}) collective-permute-start(bf16[64,4096]{1,0:T(8,128)(2,1)S(1)} %get-tuple-element.23.refs_1_), channel_id=1, source_target_pairs={{0,24},{8,0},{16,8},{24,16},{32,56},{40,32},{48,40},{56,48},{64,88... | collective-permute-start | bytes 1572872 | tf_op jit(solution)/shard_map/ppermute | solution.py:311
  81.2 18.9 %collective-permute-start.6 = (bf16[64,4096]{1,0:T(8,128)(2,1)S(1)}, bf16[64,4096]{1,0:T(8,128)(2,1)S(1)}, u32[]{:S(2)}, u32[]{:S(2)}) collective-permute-start(bf16[64,4096]{1,0:T(8,128)(2,1)S(1)} %get-tuple-element.22.refs_0_), channel_id=1, source_target_pairs={{0,24},{8,0},{16,8},{24,16},{32,56},{40,32},{48,40},{56,48},{64,88... | collective-permute-start | bytes 1572872 | tf_op jit(solution)/shard_map/ppermute | solution.py:313
  83.2 17.1 %collective-permute-start.2 = (bf16[64,4096]{1,0:T(8,128)(2,1)S(1)}, bf16[64,4096]{1,0:T(8,128)(2,1)S(1)}, u32[]{:S(2)}, u32[]{:S(2)}) collective-permute-start(bf16[64,4096]{1,0:T(8,128)(2,1)S(1)} %get-tuple-element.23.refs_1_), channel_id=1, source_target_pairs={{0,8},{8,16},{16,24},{24,0},{32,40},{40,48},{48,56},{56,32},{64,72... | collective-permute-start | bytes 1572872 | tf_op jit(solution)/shard_map/ppermute | solution.py:312
  87.7 23.8 %collective-permute-start.3 = (bf16[64,4096]{1,0:T(8,128)(2,1)S(1)}, bf16[64,4096]{1,0:T(8,128)(2,1)S(1)}, u32[]{:S(2)}, u32[]{:S(2)}) collective-permute-start(bf16[64,4096]{1,0:T(8,128)(2,1)S(1)} %collective-permute-done.1.refs_2_), channel_id=1, source_target_pairs={{0,8},{8,16},{16,24},{24,0},{32,40},{40,48},{48,56},{56,32},{64,72... | collective-permute-start | bytes 1572872 | tf_op jit(solution)/shard_map/ppermute | solution.py:314
  89.6 22.7 %collective-permute-start.5 = (bf16[64,4096]{1,0:T(8,128)(2,1)S(1)}, bf16[64,4096]{1,0:T(8,128)(2,1)S(1)}, u32[]{:S(2)}, u32[]{:S(2)}) collective-permute-start(bf16[64,4096]{1,0:T(8,128)(2,1)S(1)} %collective-permute-done.4.refs_7_), channel_id=1, source_target_pairs={{0,24},{8,0},{16,8},{24,16},{32,56},{40,32},{48,40},{56,48},{64,88... | collective-permute-start | bytes 1572872 | tf_op jit(solution)/shard_map/ppermute | solution.py:315
  111.5 0.8 copy-start.2
  112.3 0.8 copy-start.4
  113.1 12.9 %collective-permute-start.7 = (bf16[8,8,240,128]{3,2,1,0:T(8,128)(2,1)}, bf16[8,8,240,128]{3,2,1,0:T(8,128)(2,1)S(1)}, u32[]{:S(2)}, u32[]{:S(2)}) collective-permute-start(bf16[8,8,240,128]{3,2,1,0:T(8,128)(2,1)} %bitcast.29), channel_id=1, source_target_pairs={{0,256},{256,0},{1,257},{257,1},{2,258},{258,2},{3,259},{259,3},{4... | collective-permute-start | bytes 11796488 | tf_op jit(solution)/shard_map/ppermute | solution.py:386
  119.0 2.1 %copy-start.1 = (bf16[15360,128]{1,0:T(8,128)(2,1)S(1)}, bf16[15360,128]{1,0:T(8,128)(2,1)}, u32[]{:S(2)}) copy-start(bf16[15360,128]{1,0:T(8,128)(2,1)} %all-gather.2.cloned.1.call-done) | copy-start | bytes 11796484
  121.1 1.0 copy-start.3
  122.2 1.0 copy-start.5
  129.8 34.5 %all-to-all-start.2 = ((bf16[32,16,896]{2,1,0:T(8,128)(2,1)}), bf16[32,16,896]{2,1,0:T(8,128)(2,1)S(1)}, u32[]{:S(2)}, u32[]{:S(2)}) async-start(bf16[32,16,896]{2,1,0:T(8,128)(2,1)} %bitcast.12), calls=%async_computation.2 | async-start | bytes 1835008 | tf_op jit(solution)/shard_map/all_to_all | solution.py:393
  140.7 1.2 copy-start.6
  175.5 19.1 %all-to-all-start.4 = ((f32[64,1,512]{2,1,0:T(1,128)}), f32[64,1,512]{2,1,0:T(1,128)S(1)}, u32[]{:S(2)}, u32[]{:S(2)}) async-start(f32[64,1,512]{2,1,0:T(1,128)} %broadcast_in_dim.16), calls=%async_computation.4 | async-start | bytes 262144 | tf_op jit(solution)/shard_map/all_to_all | solution.py:404
Sparse Core Ops, SparseCore 0:
  44.6 52.1 all-gather.1
